TPU v7x, 512 devices: a whole 4x8x8 slice. The times are simulated.
512 devices in a mesh: cond: 32 (over y_lo, z), grid: 16 (over x, y_hi, core).
Axes of the slice: x: 4, y: 8 (y_hi: 2, y_lo: 4; y = y_hi * 4 + y_lo), z: 8, core: 2. Of those that a mesh axis runs over, the one named last changes fastest.
Arguments:
- adjoint_source: float32 [64, 5, 32, 64, 128], P('cond', None, 'grid'), may hold values from -6 to 6
- adjoint_start: float32 [64, 5, 32, 64, 128], P('cond', None, 'grid'), may hold values from -4 to 4
- spectral_radius: float32 [32, 64, 128], P('grid'), may hold values from 0.5 to 2
- coupling: float32 [64, 5, 5], P('cond'), may hold values from -0.6 to 1.4, as said below
- left_vectors: float32 [64, 5, 5], P('cond'), may hold values from -0.6 to 1.4, as said below
- right_vectors: float32 [64, 5, 5], P('cond'), may hold values from -0.6 to 1.4, as said below
- implicit_scales: float32 [64, 5, 3], P('cond'), may hold values from 1 to 200
- sensitivity_map: float32 [64, 3, 5], P('cond'), may hold values from -4 to 4
- condition_weights: int32 [64], P('cond'), may hold values from 1 to 8
Outputs:
- adjoint: float32 [64, 5, 32, 64, 128], P('cond', None, 'grid')
- mesh_sensitivity: float32 [3, 32, 64, 128], P(None, 'grid')
Inputs may be any that keep to these rules, and one draw needn't show every extreme that they name: `coupling`: mixing coefficients among the 5 flow variables. `left_vectors`: mixing coefficients among the 5 flow variables. `right_vectors`: mixing coefficients among the 5 flow variables.
All inputs are finite; a program needn't handle non-finite values.
Results may differ from a plain program's by a relative error of at most 0.0001.
Values sent between devices are 32-bit elements; how exact they have to be, the bound alone decides.
No kernel may reach another device: no remote copies, remote signals or barrier semaphores. Data moves between devices by JAX's collectives and lax.ppermute only.
A program may use at most 64 MiB of HBM per device.

v0:
```python
import math

import jax
import jax.numpy as jnp
from jax import lax
from jax.sharding import PartitionSpec as P

ITERS = 2


HIGH = lax.Precision.HIGHEST


def extended_2(array, sides, width):
    for axis, dim in sides:
        peers, length = (lax.axis_size(axis), array.shape[dim])
        up = [(i, (i + 1) % peers) for i in range(peers - 1)]
        down = [(j, i) for i, j in up]
        last = lax.slice_in_dim(array, length - width, length, axis=dim)
        leading = lax.slice_in_dim(array, 0, width, axis=dim)
        before = lax.ppermute(last, axis, up)
        after = lax.ppermute(leading, axis, down)
        array = jnp.concatenate([before, array, after], axis=dim)
    return array


def sine_tables(length):
    counter = jnp.arange(length, dtype=jnp.int32) + 1
    product = (counter[:, None] * counter[None, :]).astype(jnp.float32)
    sine_table = math.sqrt(2.0 / (length + 1)) * jnp.sin(product * (math.pi / (length + 1)))
    spectrum = 2.0 - 2.0 * jnp.cos(counter.astype(jnp.float32) * (math.pi / (length + 1)))
    return (sine_table, spectrum)


def solve_lines(charac, rates, line_dim):
    length = charac.shape[line_dim]
    sine_table, spectrum = sine_tables(length)
    denom = 1.0 + rates[:, :, None] * (spectrum + spectrum * spectrum)[None, None, :]
    charac = (
        jnp.einsum("jk,cfkyz->cfjyz", sine_table, charac, precision=HIGH)
        / denom[:, :, :, None, None]
    )
    return jnp.einsum("jk,cfkyz->cfjyz", sine_table, charac, precision=HIGH)


def solve_local(charac, rates_y, rates_z):
    table_y, spec_y = sine_tables(charac.shape[3])
    table_z, spec_z = sine_tables(charac.shape[4])
    denom = 1.0 + rates_z[:, :, None] * (spec_z + spec_z * spec_z)[None, None, :]
    charac = (
        jnp.einsum("jk,cfxyk->cfxyj", table_z, charac, precision=HIGH) / denom[:, :, None, None, :]
    )
    charac = jnp.einsum("jk,cfxyk->cfxyj", table_z, charac, precision=HIGH)
    denom = 1.0 + rates_y[:, :, None] * (spec_y + spec_y * spec_y)[None, None, :]
    charac = (
        jnp.einsum("jk,cfxkz->cfxjz", table_y, charac, precision=HIGH) / denom[:, :, None, :, None]
    )
    return jnp.einsum("jk,cfxkz->cfxjz", table_y, charac, precision=HIGH)


def pad_sides(extended):
    return jnp.pad(extended, ((0, 0), (0, 0), (0, 0), (1, 1), (1, 1)))


def body(
    adjoint_source,
    adjoint_start,
    spectral_radius,
    coupling,
    left_vectors,
    right_vectors,
    implicit_scales,
    sensitivity_map,
    condition_weights,
):
    split_dim = 3
    line_dim = 2
    adjoint = adjoint_start
    for repeat in range(ITERS):
        extended = extended_2(adjoint, (("grid", 2),), 1)
        padded = pad_sides(extended)
        beside = padded[:, :, 2:, 1:-1, 1:-1] + padded[:, :, :-2, 1:-1, 1:-1]
        beside = beside + padded[:, :, 1:-1, 2:, 1:-1] + padded[:, :, 1:-1, :-2, 1:-1]
        beside = beside + padded[:, :, 1:-1, 1:-1, 2:] + padded[:, :, 1:-1, 1:-1, :-2]
        lapped = 6.0 * adjoint - beside
        residual = (
            adjoint_source
            - spectral_radius[None, None] * adjoint
            - jnp.einsum("cfg,cgxyz->cfxyz", coupling, lapped, precision=HIGH)
        )
        charac = jnp.einsum("cfg,cgxyz->cfxyz", left_vectors, residual, precision=HIGH)
        charac = solve_local(charac, implicit_scales[:, :, 1], implicit_scales[:, :, 2])
        lines = lax.all_to_all(
            charac, "grid", split_axis=split_dim, concat_axis=line_dim, tiled=True
        )
        lines = solve_lines(lines, implicit_scales[:, :, 0], line_dim)
        charac = lax.all_to_all(
            lines, "grid", split_axis=line_dim, concat_axis=split_dim, tiled=True
        )
        adjoint = adjoint + jnp.einsum("cfg,cgxyz->cfxyz", right_vectors, charac, precision=HIGH)
    extended = extended_2(adjoint, (("grid", 2),), 1)
    padded = pad_sides(extended)
    diff_x = padded[:, :, 2:, 1:-1, 1:-1] - padded[:, :, :-2, 1:-1, 1:-1]
    diff_y = padded[:, :, 1:-1, 2:, 1:-1] - padded[:, :, 1:-1, :-2, 1:-1]
    diff_z = padded[:, :, 1:-1, 1:-1, 2:] - padded[:, :, 1:-1, 1:-1, :-2]
    stacked = jnp.stack([adjoint * diff_x, adjoint * diff_y, adjoint * diff_z], axis=1)
    terms = jnp.einsum("ckf,ckfxyz->ckxyz", sensitivity_map, stacked, precision=HIGH)
    weights = condition_weights.astype(jnp.float32)
    partial_total = jnp.einsum("c,ckxyz->kxyz", weights, terms, precision=HIGH)
    total = lax.psum(partial_total, "cond")
    cond_count = lax.axis_size("cond") * condition_weights.shape[0]
    return (adjoint, total / cond_count)


def solution(mesh):
    in_specs = (
        P("cond", None, "grid", None, None),
        P("cond", None, "grid", None, None),
        P("grid", None, None),
        P("cond", None, None),
        P("cond", None, None),
        P("cond", None, None),
        P("cond", None, None),
        P("cond", None, None),
        P("cond"),
    )
    out_specs = (P("cond", None, "grid", None, None), P(None, "grid", None, None))
    return jax.shard_map(body, mesh=mesh, in_specs=in_specs, out_specs=out_specs, check_vma=False)
```

profile of v0, /device:TPU:4, one launch (start us, length us, event | category | flops | bytes accessed | tf_op | source)
XLA Modules:
  0.0 529.1 jit_solution(15406752801482384263)
XLA Ops:
  8.8 7.3 %collective-permute-start = (f32[2,5,1,64,128]{4,1,3,2,0:T(8,128)S(1)}, f32[2,5,1,64,128]{4,1,3,2,0:T(8,128)S(1)}, u32[]{:S(2)}, u32[]{:S(2)}) collective-permute-start(f32[2,5,1,64,128]{4,1,3,2,0:T(8,128)S(1)} %get-tuple-element.16), channel_id=1, source_target_pairs={{1,0},{2,1},{3,2},{4,3},{5,4},{6,5},{7,6},{8,7},{9,8},{10,9},{11,1... | collective-permute-start | bytes 983048 | tf_op jit(solution)/shard_map/ppermute | solution.py:22
  16.1 1.9 collective-permute-start.1
  19.0 11.3 %collective-permute-done = f32[2,5,1,64,128]{4,1,3,2,0:T(8,128)S(1)} collective-permute-done((f32[2,5,1,64,128]{4,1,3,2,0:T(8,128)S(1)}, f32[2,5,1,64,128]{4,1,3,2,0:T(8,128)S(1)}, u32[]{:S(2)}, u32[]{:S(2)}) %collective-permute-start) | collective-permute-done | bytes 327712 | tf_op jit(solution)/shard_map/ppermute | solution.py:22
  30.3 4.9 collective-permute-done.1
  35.2 1.8 select_maximum_fusion.4
  37.0 2.1 fusion.8
  45.3 9.7 %all-to-all-start = ((f32[2,5,2,64,128]{4,2,1,0,3:T(2,128)}), f32[2,5,2,64,128]{4,2,1,0,3:T(2,128)S(1)}, u32[]{:S(2)}, u32[]{:S(2)}) async-start(f32[2,5,2,64,128]{4,2,1,0,3:T(2,128)} %copy.54), calls=%async_computation | async-start | bytes 1310720 | tf_op jit(solution)/shard_map/all_to_all | solution.py:93
  55.2 13.5 %all-to-all-done = f32[2,5,2,64,128]{4,2,1,0,3:T(2,128)S(1)} async-done(((f32[2,5,2,64,128]{4,2,1,0,3:T(2,128)}), f32[2,5,2,64,128]{4,2,1,0,3:T(2,128)S(1)}, u32[]{:S(2)}, u32[]{:S(2)}) %all-to-all-start) | async-done | bytes 655392 | tf_op jit(solution)/shard_map/all_to_all | solution.py:93
  71.1 23.8 %all_to_all.72 = f32[2,5,32,4,128]{4,3,1,0,2:T(4,128)S(1)} all-to-all(f32[2,5,32,4,128]{4,3,1,0,2:T(4,128)S(1)} %copy.56), channel_id=1, replica_groups=mesh['cond'=32,'grid'=16] {'grid'}, dimensions={2} | all-to-all | bytes 1310720 | tf_op jit(solution)/shard_map/all_to_all | solution.py:97
  96.5 3.2 collective-permute-start.2
  99.7 1.9 collective-permute-start.3
  101.7 4.7 collective-permute-done.2
  106.4 11.5 %collective-permute-done.3 = f32[2,5,1,64,128]{4,1,3,2,0:T(8,128)S(1)} collective-permute-done((f32[2,5,1,64,128]{4,1,3,2,0:T(8,128)S(1)}, f32[2,5,1,64,128]{4,1,3,2,0:T(8,128)S(1)}, u32[]{:S(2)}, u32[]{:S(2)}) %collective-permute-start.3) | collective-permute-done | bytes 327712 | tf_op jit(solution)/shard_map/ppermute | solution.py:21
  119.7 2.1 fusion.6
  127.1 33.9 %all_to_all.73 = f32[2,5,2,64,128]{4,2,1,0,3:T(2,128)S(1)} all-to-all(f32[2,5,2,64,128]{4,2,1,0,3:T(2,128)S(1)} %copy.64), channel_id=1, replica_groups=mesh['cond'=32,'grid'=16] {'grid'}, dimensions={3} | all-to-all | bytes 1310720 | tf_op jit(solution)/shard_map/all_to_all | solution.py:93
  163.5 18.8 %all_to_all.74 = f32[2,5,32,4,128]{4,3,1,0,2:T(4,128)S(1)} all-to-all(f32[2,5,32,4,128]{4,3,1,0,2:T(4,128)S(1)} %copy.66), channel_id=1, replica_groups=mesh['cond'=32,'grid'=16] {'grid'}, dimensions={2} | all-to-all | bytes 1310720 | tf_op jit(solution)/shard_map/all_to_all | solution.py:97
  183.6 3.2 collective-permute-start.4
  186.9 1.9 collective-permute-start.5
  188.8 5.2 collective-permute-done.4
  194.0 11.0 %collective-permute-done.5 = f32[2,5,1,64,128]{4,1,3,2,0:T(8,128)S(1)} collective-permute-done((f32[2,5,1,64,128]{4,1,3,2,0:T(8,128)S(1)}, f32[2,5,1,64,128]{4,1,3,2,0:T(8,128)S(1)}, u32[]{:S(2)}, u32[]{:S(2)}) %collective-permute-start.5) | collective-permute-done | bytes 327712 | tf_op jit(solution)/shard_map/ppermute | solution.py:21
  205.0 1.8 select_maximum_fusion
  207.7 2.9 fusion.3
  210.6 2.3 fusion.38
  213.9 306.7 %all-reduce.5.cloned.1.call-done = f32[3,2,64,128]{3,2,1,0:T(8,128)} async-done(((f32[3,2,64,128]{3,2,1,0:T(8,128)}), f32[3,2,64,128]{3,2,1,0:T(8,128)}) %all-reduce.5.cloned.1.call-update) | async-done | bytes 196624 | tf_op jit(solution)/shard_map/psum | solution.py:110
  (60 shorter events, 27.1 us)
Async XLA Ops:
  7.2 29.8 %copy-start = (f32[2,5,5]{2,0,1:T(2,128)S(1)}, f32[2,5,5]{2,0,1:T(2,128)}, u32[]{:S(2)}) copy-start(f32[2,5,5]{2,0,1:T(2,128)} %param.12) | copy-start | bytes 604
  8.7 28.3 %copy-start.4 = (f32[2,5,2,64,128]{4,3,2,1,0:T(8,128)S(1)}, f32[2,5,2,64,128]{4,3,2,1,0:T(8,128)}, u32[]{:S(2)}) copy-start(f32[2,5,2,64,128]{4,3,2,1,0:T(8,128)} %param.9) | copy-start | bytes 1966084
  8.7 28.3 %copy-start.5 = (f32[2,64,128]{2,1,0:T(8,128)S(1)}, f32[2,64,128]{2,1,0:T(8,128)}, u32[]{:S(2)}) copy-start(f32[2,64,128]{2,1,0:T(8,128)} %param.11) | copy-start | bytes 196612
  8.8 21.5 %collective-permute-start = (f32[2,5,1,64,128]{4,1,3,2,0:T(8,128)S(1)}, f32[2,5,1,64,128]{4,1,3,2,0:T(8,128)S(1)}, u32[]{:S(2)}, u32[]{:S(2)}) collective-permute-start(f32[2,5,1,64,128]{4,1,3,2,0:T(8,128)S(1)} %get-tuple-element.16), channel_id=1, source_target_pairs={{1,0},{2,1},{3,2},{4,3},{5,4},{6,5},{7,6},{8,7},{9,8},{10,9},{11,1... | collective-permute-start | bytes 983048 | tf_op jit(solution)/shard_map/ppermute | solution.py:22
  16.1 19.1 %collective-permute-start.1 = (f32[2,5,1,64,128]{4,1,3,2,0:T(8,128)S(1)}, f32[2,5,1,64,128]{4,1,3,2,0:T(8,128)S(1)}, u32[]{:S(2)}, u32[]{:S(2)}) collective-permute-start(f32[2,5,1,64,128]{4,1,3,2,0:T(8,128)S(1)} %get-tuple-element.15), channel_id=1, source_target_pairs={{0,1},{1,2},{2,3},{3,4},{4,5},{5,6},{6,7},{7,8},{8,9},{9,10},{10,1... | collective-permute-start | bytes 983048 | tf_op jit(solution)/shard_map/ppermute | solution.py:21
  19.0 20.2 %copy-start.2 = (f32[2,5,5]{2,0,1:T(2,128)S(1)}, f32[2,5,5]{2,0,1:T(2,128)}, u32[]{:S(2)}) copy-start(f32[2,5,5]{2,0,1:T(2,128)} %param.13) | copy-start | bytes 604
  45.3 23.4 %all-to-all-start = ((f32[2,5,2,64,128]{4,2,1,0,3:T(2,128)}), f32[2,5,2,64,128]{4,2,1,0,3:T(2,128)S(1)}, u32[]{:S(2)}, u32[]{:S(2)}) async-start(f32[2,5,2,64,128]{4,2,1,0,3:T(2,128)} %copy.54), calls=%async_computation | async-start | bytes 1310720 | tf_op jit(solution)/shard_map/all_to_all | solution.py:93
  55.0 465.6 %all-reduce.5.cloned.1.call-start = ((), (), s32[]{:S(2)}) async-start(), calls=%async_computation.4 | async-start | bytes 393216 | tf_op jit(solution)/shard_map/psum | solution.py:110
  68.7 26.4 %copy-start.1 = (f32[2,5,2,64,128]{4,3,2,1,0:T(8,128)S(1)}, f32[2,5,2,64,128]{4,3,2,1,0:T(8,128)}, u32[]{:S(2)}) copy-start(f32[2,5,2,64,128]{4,3,2,1,0:T(8,128)} %param.10) | copy-start | bytes 1966084
  68.7 26.4 %copy-start.3 = (f32[2,5,5]{2,0,1:T(2,128)S(1)}, f32[2,5,5]{2,0,1:T(2,128)}, u32[]{:S(2)}) copy-start(f32[2,5,5]{2,0,1:T(2,128)} %param.14) | copy-start | bytes 604
  96.5 9.9 %collective-permute-start.2 = (f32[2,5,1,64,128]{4,1,3,2,0:T(8,128)S(1)}, f32[2,5,1,64,128]{4,1,3,2,0:T(8,128)S(1)}, u32[]{:S(2)}, u32[]{:S(2)}) collective-permute-start(f32[2,5,1,64,128]{4,1,3,2,0:T(8,128)S(1)} %get-tuple-element.14), channel_id=1, source_target_pairs={{1,0},{2,1},{3,2},{4,3},{5,4},{6,5},{7,6},{8,7},{9,8},{10,9},{11,1... | collective-permute-start | bytes 983048 | tf_op jit(solution)/shard_map/ppermute | solution.py:22
  99.7 18.1 %collective-permute-start.3 = (f32[2,5,1,64,128]{4,1,3,2,0:T(8,128)S(1)}, f32[2,5,1,64,128]{4,1,3,2,0:T(8,128)S(1)}, u32[]{:S(2)}, u32[]{:S(2)}) collective-permute-start(f32[2,5,1,64,128]{4,1,3,2,0:T(8,128)S(1)} %get-tuple-element.13), channel_id=1, source_target_pairs={{0,1},{1,2},{2,3},{3,4},{4,5},{5,6},{6,7},{7,8},{8,9},{9,10},{10,1... | collective-permute-start | bytes 983048 | tf_op jit(solution)/shard_map/ppermute | solution.py:21
  183.6 10.4 %collective-permute-start.4 = (f32[2,5,1,64,128]{4,1,3,2,0:T(8,128)S(1)}, f32[2,5,1,64,128]{4,1,3,2,0:T(8,128)S(1)}, u32[]{:S(2)}, u32[]{:S(2)}) collective-permute-start(f32[2,5,1,64,128]{4,1,3,2,0:T(8,128)S(1)} %get-tuple-element.12), channel_id=1, source_target_pairs={{1,0},{2,1},{3,2},{4,3},{5,4},{6,5},{7,6},{8,7},{9,8},{10,9},{11,1... | collective-permute-start | bytes 983048 | tf_op jit(solution)/shard_map/ppermute | solution.py:22
  186.9 18.1 %collective-permute-start.5 = (f32[2,5,1,64,128]{4,1,3,2,0:T(8,128)S(1)}, f32[2,5,1,64,128]{4,1,3,2,0:T(8,128)S(1)}, u32[]{:S(2)}, u32[]{:S(2)}) collective-permute-start(f32[2,5,1,64,128]{4,1,3,2,0:T(8,128)S(1)} %get-tuple-element.11), channel_id=1, source_target_pairs={{0,1},{1,2},{2,3},{3,4},{4,5},{5,6},{6,7},{7,8},{8,9},{9,10},{10,1... | collective-permute-start | bytes 983048 | tf_op jit(solution)/shard_map/ppermute | solution.py:21
  206.8 0.9 copy-start.6
  207.7 2.9 copy-start.7
Sparse Core Ops, SparseCore 0:
  213.1 307.5 all-reduce.4
where the time goes:
time: 530 us; the launch traced here: 529 us
  waiting for transfers between devices  369 us (70%)
  blocking collectives  76.5 us (14%)
  starting transfers between devices  29.2 us (6%)
  matrix products  24.7 us (5%)
  between operations  14.5 us (3%)
  other arithmetic  8.24 us (2%)
  local copies, waits for them, and re-layouts  7.15 us (1%)
    psum x1, waiting for transfers between devices, body(): total = lax.psum(partial_total, 'cond')  307 us
    all_to_all x2, blocking collectives, body(): lax.all_to_all(lines, 'grid', split_axis=line_dim, concat_axis=split_dim,...  42.6 us
    all_to_all x1, blocking collectives, body(): lax.all_to_all(charac, 'grid', split_axis=split_dim, concat_axis=line_dim...  33.9 us
    ppermute x3, waiting for transfers between devices, extended_2(): before = lax.ppermute(last, axis, up)  27.3 us
    ppermute x3, waiting for transfers between devices, extended_2(): after = lax.ppermute(leading, axis, down)  21.3 us
    ppermute x3, starting transfers between devices, extended_2(): after = lax.ppermute(leading, axis, down)  13.7 us
    all_to_all x1, waiting for transfers between devices, body(): lax.all_to_all(charac, 'grid', split_axis=split_dim, concat_axis=line_dim...  13.5 us
  transfers between devices with their start and end apart: 8, of which 8 were waited for; matrix products, arithmetic and copies ran while one was open for 0% of the time, Pallas kernels for 0%

commit v1 on v0

v1 whole, which is shorter than its diff:
```python
import functools
import math

import jax
import jax.numpy as jnp
import numpy as np
from jax import lax
from jax.experimental import pallas as pl
from jax.experimental.pallas import tpu as pltpu
from jax.sharding import PartitionSpec as P

HIGH = lax.Precision.HIGHEST
F32 = jnp.float32
FIELDS = 5
VMEM = pl.BlockSpec(memory_space=pltpu.VMEM)
SMEM = pl.BlockSpec(memory_space=pltpu.SMEM)
LIMIT = 40 * 1024 * 1024


def dot(a, b):
    return jnp.dot(a, b, precision=HIGH, preferred_element_type=F32)


def sine_tables(length):
    counter = np.arange(1, length + 1, dtype=np.float64)
    sine = math.sqrt(2.0 / (length + 1)) * np.sin(
        counter[:, None] * counter[None, :] * (math.pi / (length + 1))
    )
    spectrum = 2.0 - 2.0 * np.cos(counter * (math.pi / (length + 1)))
    return sine.astype(np.float32), (spectrum + spectrum * spectrum).astype(np.float32)


def call(kernel, outs, in_specs, flops, name, scratch=()):
    return pl.pallas_call(
        kernel,
        out_shape=outs,
        in_specs=in_specs,
        out_specs=jax.tree.map(lambda _: VMEM, outs),
        scratch_shapes=list(scratch),
        compiler_params=pltpu.CompilerParams(vmem_limit_bytes=LIMIT),
        cost_estimate=pl.CostEstimate(flops=flops, bytes_accessed=4_000_000, transcendentals=0),
        name=name,
    )


def shape(*dims):
    return jax.ShapeDtypeStruct(dims, F32)


def shifted(v, axis, step):
    size = v.shape[axis]
    rolled = pltpu.roll(v, (-step) % size, axis)
    at = lax.broadcasted_iota(jnp.int32, v.shape, axis)
    return jnp.where(at == (size - 1 if step > 0 else 0), 0.0, rolled)


def tables_kernel(rates, side, sine_z, spec_z, sine_y, spec_y, left_x, right_x, spec_x,
                  solve_z, solve_y, solve_x, solve_zb):
    for c in range(2):
        for f in range(FIELDS):
            denom = 1.0 + rates[c, f, 2] * spec_z[...]
            solve_z[c, f] = dot(sine_z[...] / denom, sine_z[...])
            denom = 1.0 + rates[c, f, 1] * spec_y[...]
            solve_y[c, f] = dot(sine_y[...] / denom, sine_y[...])
    mine = side[0]
    n = left_x.shape[0]
    row = lax.broadcasted_iota(jnp.int32, (n, n), 0)
    col = lax.broadcasted_iota(jnp.int32, (n, n), 1)
    same = (row & 7) == (col & 7)
    for f in range(FIELDS):
        denom = 1.0 + rates[mine, f, 0] * spec_x[...]
        solve_x[f] = jnp.where(same, dot(left_x[...] / denom, right_x[...]), 0.0)
        solve_zb[f] = solve_z[mine, f]


def first_kernel(coupling, left, adjoint, low, high, source, radius, solve_z, solve_y, out, lapped):
    blocks = adjoint.shape[3] // 8
    for c in range(2):
        for x in range(2):
            for f in range(FIELDS):
                v = adjoint[c, f, x]
                beside = (low[c, f] if x == 0 else adjoint[c, f, 0]) + (
                    adjoint[c, f, 1] if x == 0 else high[c, f]
                )
                beside = beside + shifted(v, 0, 1) + shifted(v, 0, -1)
                beside = beside + shifted(v, 1, 1) + shifted(v, 1, -1)
                lapped[f] = 6.0 * v - beside
            sr = radius[x]
            residual = []
            for f in range(FIELDS):
                r = source[c, f, x] - sr * adjoint[c, f, x]
                for g in range(FIELDS):
                    r = r - coupling[c, f, g] * lapped[g]
                residual.append(r)
            for f in range(FIELDS):
                r = left[c, f, 0] * residual[0]
                for g in range(1, FIELDS):
                    r = r + left[c, f, g] * residual[g]
                r = dot(solve_y[c, f], dot(r, solve_z[c, f]))
                for b in range(blocks):
                    out[(b // 2) * 4 + c * 2 + b % 2, f, x] = r[8 * b : 8 * b + 8]
            for b in range(blocks):
                out[(b // 2) * 4 + c * 2 + b % 2, FIELDS, x] = sr[8 * b : 8 * b + 8]


def across_kernel(lines, solve_x, solved, to_prev, to_next):
    n = solve_x.shape[1]
    for f in range(FIELDS):
        u = dot(solve_x[f], lines[:, f].reshape(n, 128)).reshape(n // 8, 8, 128)
        solved[f] = u
        quad = u.reshape(n // 32, 4, 8, 128)
        for j in range(4):
            to_prev[f, :, 2 * j : 2 * j + 2, :] = quad[:, j, 0:2, :]
            to_next[f, :, 2 * j : 2 * j + 2, :] = quad[:, j, 6:8, :]


def second_kernel(rates, inner, both, both_lap, solved, from_prev, from_next, lines, solve_x, solve_z,
                  out, lapped, kept):
    nx = solved.shape[1]
    full = (nx, 8, 128)
    row = lax.broadcasted_iota(jnp.int32, full, 1)
    has_prev, has_next = inner[0], inner[1]
    for f in range(FIELDS):
        u = solved[f]
        spread = lambda ref, at: jnp.stack(
            [pltpu.roll(ref[f], (at - 2 * j) % 8, 1) for j in range(4)], axis=1
        ).reshape(full)
        before, after = spread(from_prev, 6), spread(from_next, 0)
        up, down = pltpu.roll(u, 7, 1), pltpu.roll(u, 1, 1)
        nexts = jnp.where(row == 7, pltpu.roll(after, 7, 1), up)
        prevs = jnp.where(row == 0, pltpu.roll(before, 1, 1), down)
        ku = 2.0 * u - nexts - prevs
        k_before = (2.0 * before - pltpu.roll(before, 1, 1) - up) * has_prev
        k_after = (2.0 * after - pltpu.roll(after, 7, 1) - down) * has_next
        k_nexts = jnp.where(row == 7, pltpu.roll(k_after, 7, 1), pltpu.roll(ku, 7, 1))
        k_prevs = jnp.where(row == 0, pltpu.roll(k_before, 1, 1), pltpu.roll(ku, 1, 1))
        kku = 2.0 * ku - k_nexts - k_prevs
        kept[f] = 2.0 * (u + rates[f, 1] * (ku + kku))
        zero = jnp.zeros((1, 8, 128), F32)
        beside = jnp.concatenate([zero, u[:-1]], axis=0) + jnp.concatenate([u[1:], zero], axis=0)
        flat = u.reshape(nx * 8, 128)
        beside = beside + (shifted(flat, 1, 1) + shifted(flat, 1, -1)).reshape(full)
        lapped[f] = 4.0 * u + ku - beside
    sr = lines[:, FIELDS].reshape(full)
    for f in range(FIELDS):
        near = both[f, 0] * solved[0]
        far = both_lap[f, 0] * lapped[0]
        for g in range(1, FIELDS):
            near = near + both[f, g] * solved[g]
            far = far + both_lap[f, g] * lapped[g]
        v = (sr * near + far).reshape(nx * 8, 128)
        v = dot(solve_x[f], dot(v, solve_z[f]))
        out[:, f] = (kept[f] - v.reshape(full)).reshape(nx // 2, 2, 8, 128)


def update_kernel(right, adjoint, solved, solve_y, out, first, last, step):
    blocks = adjoint.shape[3] // 8
    for c in range(2):
        for x in range(2):
            for f in range(FIELDS):
                q = jnp.concatenate(
                    [solved[(b // 2) * 4 + c * 2 + b % 2, f, x] for b in range(blocks)], axis=0
                )
                step[f] = dot(solve_y[c, f], q)
            for f in range(FIELDS):
                a = adjoint[c, f, x]
                for g in range(FIELDS):
                    a = a + right[c, f, g] * step[g]
                out[c, f, x] = a
                if x == 0:
                    first[c, f] = a
                else:
                    last[c, f] = a


def terms_kernel(smap, weights, adjoint, low, high, out):
    for x in range(2):
        total = [None, None, None]
        for c in range(2):
            w = weights[c].astype(F32)
            for f in range(FIELDS):
                v = adjoint[c, f, x]
                diffs = (
                    (adjoint[c, f, 1] - low[c, f]) if x == 0 else (high[c, f] - adjoint[c, f, 0]),
                    shifted(v, 0, 1) - shifted(v, 0, -1),
                    shifted(v, 1, 1) - shifted(v, 1, -1),
                )
                for k in range(3):
                    t = (w * smap[c, k, f]) * (v * diffs[k])
                    total[k] = t if total[k] is None else total[k] + t
        for k in range(3):
            out[k, x] = total[k]


def sum_kernel(scale, pieces, out):
    total = pieces[0]
    for i in range(1, pieces.shape[0]):
        total = total + pieces[i]
    total = total * scale
    for i in range(out.shape[0]):
        out[i] = total


def exchange(first, last, axis, up, down):
    return lax.ppermute(last, axis, up), lax.ppermute(first, axis, down)


def body(
    adjoint_source,
    adjoint_start,
    spectral_radius,
    coupling,
    left_vectors,
    right_vectors,
    implicit_scales,
    sensitivity_map,
    condition_weights,
):
    peers = lax.axis_size("grid")
    conds = lax.axis_size("cond")
    _, fields, planes, ny, nz = adjoint_start.shape
    nx = peers * planes
    rows_b = nx * 8

    me = lax.axis_index("grid")
    side = (me // 2) % 2
    place = (me // 4) * 2 + me % 2

    sine_z, spec_z = sine_tables(nz)
    sine_y, spec_y = sine_tables(ny)
    sine_x, spec_x = sine_tables(nx)
    left_x = np.repeat(sine_x, 8, axis=0)

    up = [(i, i + 1) for i in range(peers - 1)]
    down = [(j, i) for i, j in up]
    low, high = exchange(adjoint_start[:, :, 0], adjoint_start[:, :, planes - 1], "grid", up, down)

    solve_z, solve_y, solve_x, solve_zb = call(
        tables_kernel,
        (shape(2, fields, nz, nz), shape(2, fields, ny, ny), shape(fields, rows_b, rows_b), shape(fields, nz, nz)),
        [SMEM, SMEM] + [VMEM] * 7,
        100_000_000,
        "solve_tables",
    )(
        implicit_scales,
        side.reshape(1).astype(jnp.int32),
        jnp.asarray(sine_z),
        jnp.asarray(spec_z[None, :]),
        jnp.asarray(sine_y),
        jnp.asarray(spec_y[None, :]),
        jnp.asarray(left_x),
        jnp.asarray(left_x.T.copy()),
        jnp.asarray(spec_x[None, :]),
    )

    lines = call(
        first_kernel,
        shape(peers, fields + 1, planes, 8, nz),
        [SMEM, SMEM] + [VMEM] * 7,
        200_000_000,
        "first_residual",
        [pltpu.VMEM((fields, ny, nz), F32)],
    )(coupling, left_vectors, adjoint_start, low, high, adjoint_source, spectral_radius, solve_z, solve_y)

    lines = lax.all_to_all(lines, "grid", 0, 0, tiled=True)

    solved, to_prev, to_next = call(
        across_kernel,
        (shape(fields, nx, 8, nz), shape(fields, nx // 4, 8, nz), shape(fields, nx // 4, 8, nz)),
        [VMEM, VMEM],
        100_000_000,
        "solve_across",
    )(lines, solve_x)

    spot = lambda s, b: (b // 2) * 4 + s * 2 + b % 2
    blocks = peers // 2
    up_b = [(spot(s, b), spot(s, b + 1)) for s in range(2) for b in range(blocks - 1)]
    down_b = [(j, i) for i, j in up_b]
    from_prev, from_next = exchange(to_prev, to_next, "grid", up_b, down_b)

    pick = lambda v: lax.dynamic_index_in_dim(v, side, 0, keepdims=False)
    left_b, coup_b, right_b = pick(left_vectors), pick(coupling), pick(right_vectors)
    both = jnp.sum(left_b[:, :, None] * right_b[None, :, :], axis=1)
    inner_mix = jnp.sum(coup_b[:, :, None] * right_b[None, :, :], axis=1)
    both_lap = jnp.sum(left_b[:, :, None] * inner_mix[None, :, :], axis=1)
    inner = jnp.stack([place > 0, place < blocks - 1]).astype(F32)

    step = call(
        second_kernel,
        shape(peers, fields, planes, 8, nz),
        [SMEM] * 4 + [VMEM] * 6,
        300_000_000,
        "second_residual",
        [pltpu.VMEM((fields, nx, 8, nz), F32), pltpu.VMEM((fields, nx, 8, nz), F32)],
    )(pick(implicit_scales), inner, both, both_lap, solved, from_prev, from_next, lines, solve_x, solve_zb)

    step = lax.all_to_all(step, "grid", 0, 0, tiled=True)

    adjoint, first, last = call(
        update_kernel,
        (shape(2, fields, planes, ny, nz), shape(2, fields, ny, nz), shape(2, fields, ny, nz)),
        [SMEM] + [VMEM] * 3,
        60_000_000,
        "update",
        [pltpu.VMEM((fields, ny, nz), F32)],
    )(right_vectors, adjoint_start, step, solve_y)

    low, high = exchange(first, last, "grid", up, down)

    terms = call(
        terms_kernel,
        shape(3, planes, ny, nz),
        [SMEM, SMEM] + [VMEM] * 3,
        10_000_000,
        "terms",
    )(sensitivity_map, condition_weights, adjoint, low, high)

    tiles = 3 * planes * ny // 8
    each = -(-tiles // conds)
    pieces = terms.reshape(tiles * 8, nz)
    pieces = jnp.pad(pieces, ((0, (conds * each - tiles) * 8), (0, 0))).reshape(conds, each * 8, nz)
    pieces = lax.all_to_all(pieces, "cond", 0, 0, tiled=True)
    scale = 1.0 / (conds * condition_weights.shape[0])
    pieces = call(
        functools.partial(sum_kernel, scale),
        shape(conds, each * 8, nz),
        [VMEM],
        1_000_000,
        "sum_conditions",
    )(pieces)
    pieces = lax.all_to_all(pieces, "cond", 0, 0, tiled=True)
    total = pieces.reshape(conds * each * 8, nz)[: tiles * 8].reshape(3, planes, ny, nz)
    return (adjoint, total)


def solution(mesh):
    in_specs = (
        P("cond", None, "grid", None, None),
        P("cond", None, "grid", None, None),
        P("grid", None, None),
        P("cond", None, None),
        P("cond", None, None),
        P("cond", None, None),
        P("cond", None, None),
        P("cond", None, None),
        P("cond"),
    )
    out_specs = (P("cond", None, "grid", None, None), P(None, "grid", None, None))
    return jax.shard_map(body, mesh=mesh, in_specs=in_specs, out_specs=out_specs, check_vma=False)
```

time: 530 us -> 168 us (0.32)
  the two profiles are of different devices: /device:TPU:4 before, /device:TPU:2 now
where the time goes in v1:
time: 168 us
  blocking collectives  72.5 us (43%)
  starting transfers between devices  36.2 us (22%)
  waiting for transfers between devices  29.5 us (18%)
  Pallas kernels  19.5 us (12%)
  local copies, waits for them, and re-layouts  8.59 us (5%)
    all_to_all x2, blocking collectives, body(): pieces = lax.all_to_all(pieces, 'cond', 0, 0, tiled=True)  52.5 us
    ppermute x6, starting transfers between devices, exchange(): return (lax.ppermute(last, axis, up), lax.ppermute(first, axis, down))  26.5 us
    all_to_all x1, blocking collectives, body(): step = lax.all_to_all(step, 'grid', 0, 0, tiled=True)  20.1 us
    all_to_all x1, waiting for transfers between devices, body(): lines = lax.all_to_all(lines, 'grid', 0, 0, tiled=True)  15.3 us
    ppermute x6, waiting for transfers between devices, exchange(): return (lax.ppermute(last, axis, up), lax.ppermute(first, axis, down))  14.2 us
    all_to_all x1, starting transfers between devices, body(): lines = lax.all_to_all(lines, 'grid', 0, 0, tiled=True)  9.63 us
    pallas_call x1, Pallas kernels, body(): call(first_kernel, shape(peers, fields + 1, planes, 8, nz), [SMEM, SMEM]...  7.65 us
    unnamed x43, local copies, waits for them, and re-layouts  5.68 us
  transfers between devices with their start and end apart: 7, of which 6 were waited for; matrix products, arithmetic and copies ran while one was open for 0% of the time, Pallas kernels for 2%

profile of v1, /device:TPU:2, one launch (start us, length us, event | category | flops | bytes accessed | tf_op | source)
XLA Modules:
  0.0 167.6 jit_solution(15237560008957134356)
XLA Ops:
  0.7 2.1 %slice_bitcast_fusion = (f32[2,5,64,128]{3,2,1,0:T(8,128)}, f32[2,5,64,128]{3,2,1,0:T(8,128)}) fusion(f32[2,5,2,64,128]{4,3,2,1,0:T(8,128)} %adjoint.3), kind=kLoop, calls=%fused_computation | loop fusion | bytes 1310720 | tf_op jit(solution)/shard_map/squeeze | solution.py:236
  2.8 1.9 %collective-permute-start = (f32[2,5,64,128]{3,2,1,0:T(8,128)}, f32[2,5,64,128]{3,2,1,0:T(8,128)}, u32[]{:S(2)}, u32[]{:S(2)}) collective-permute-start(f32[2,5,64,128]{3,2,1,0:T(8,128)} %get-tuple-element.25), channel_id=1, source_target_pairs={{0,1},{1,2},{2,3},{3,4},{4,5},{5,6},{6,7},{7,8},{8,9},{9,10},{10,1... | collective-permute-start | bytes 983048 | tf_op jit(solution)/shard_map/ppermute | solution.py:205
  4.7 8.4 %collective-permute-start.1 = (f32[2,5,64,128]{3,2,1,0:T(8,128)}, f32[2,5,64,128]{3,2,1,0:T(8,128)}, u32[]{:S(2)}, u32[]{:S(2)}) collective-permute-start(f32[2,5,64,128]{3,2,1,0:T(8,128)} %get-tuple-element.24), channel_id=1, source_target_pairs={{1,0},{2,1},{3,2},{4,3},{5,4},{6,5},{7,6},{8,7},{9,8},{10,9},{11,1... | collective-permute-start | bytes 983048 | tf_op jit(solution)/shard_map/ppermute | solution.py:205
  15.9 2.7 %solve_tables.1 = (f32[2,5,128,128]{3,2,1,0:T(8,128)S(1)}, f32[2,5,64,64]{3,2,1,0:T(8,128)S(1)}, f32[5,256,256]{2,1,0:T(8,128)S(1)}, f32[5,128,128]{2,1,0:T(8,128)S(1)}) custom-call(f32[2,5,3]{2,1,0:T(8,128)S(1)} %copy.45.rates, s32[1]{0:T(128)} %bitcast.8.side, f32[128,128]{1,0:T(8,128)S(1)} %copy-done.8, f32[1,128]{1,0:T(1,128)S(1)} %copy-done.11, ...), custom_call_target="tpu_custom_call" | custom-call | flops 100000000 | bytes 4000000 | tf_op jit(solution)/shard_map/solve_tables/pallas_call | solution.py:238
  18.6 6.8 %collective-permute-done.1.high = f32[2,5,64,128]{3,2,1,0:T(8,128)} collective-permute-done((f32[2,5,64,128]{3,2,1,0:T(8,128)}, f32[2,5,64,128]{3,2,1,0:T(8,128)}, u32[]{:S(2)}, u32[]{:S(2)}) %collective-permute-start.1) | collective-permute-done | bytes 327712 | tf_op jit(solution)/shard_map/ppermute | solution.py:205
  25.4 7.7 %first_residual.1 = f32[16,6,2,8,128]{4,3,2,1,0:T(8,128)} custom-call(f32[2,5,5]{2,1,0:T(8,128)S(1)} %copy.42.coupling, f32[2,5,5]{2,1,0:T(8,128)S(1)} %copy.40.left, f32[2,5,2,64,128]{4,3,2,1,0:T(8,128)S(1)} %copy-done, f32[2,5,64,128]{3,2,1,0:T(8,128)} %collective-permute-done.low, f32[2,5,64,128]{3,2,1,0:T(8,128)} %collective-permute-done.1.high, ...), custom_call_target="tpu_custom_call" | custom-call | flops 200000000 | bytes 4000000 | tf_op jit(solution)/shard_map/first_residual/pallas_call | solution.py:256
  33.1 9.6 %all-to-all-start = ((f32[16,6,2,8,128]{4,3,2,1,0:T(8,128)}), f32[16,6,2,8,128]{4,3,2,1,0:T(8,128)S(1)}, u32[]{:S(2)}, u32[]{:S(2)}) async-start(f32[16,6,2,8,128]{4,3,2,1,0:T(8,128)} %first_residual.1), calls=%async_computation | async-start | bytes 1572864 | tf_op jit(solution)/shard_map/all_to_all | solution.py:265
  42.9 15.3 %all-to-all-done.lines = f32[16,6,2,8,128]{4,3,2,1,0:T(8,128)S(1)} async-done(((f32[16,6,2,8,128]{4,3,2,1,0:T(8,128)}), f32[16,6,2,8,128]{4,3,2,1,0:T(8,128)S(1)}, u32[]{:S(2)}, u32[]{:S(2)}) %all-to-all-start) | async-done | bytes 786464 | tf_op jit(solution)/shard_map/all_to_all | solution.py:265
  58.2 1.9 %solve_across.1 = (f32[5,32,8,128]{3,2,1,0:T(8,128)S(1)}, f32[5,8,8,128]{3,2,1,0:T(8,128)}, f32[5,8,8,128]{3,2,1,0:T(8,128)}) custom-call(f32[16,6,2,8,128]{4,3,2,1,0:T(8,128)S(1)} %all-to-all-done.lines, f32[5,256,256]{2,1,0:T(8,128)S(1)} %get-tuple-element.14.solve_x), custom_call_target="tpu_custom_call" | custom-call | flops 100000000 | bytes 4000000 | tf_op jit(solution)/shard_map/solve_across/pallas_call | solution.py:267
  60.9 1.9 %collective-permute-start.2 = (f32[5,8,8,128]{3,2,1,0:T(8,128)}, f32[5,8,8,128]{3,2,1,0:T(8,128)}, u32[]{:S(2)}, u32[]{:S(2)}) collective-permute-start(f32[5,8,8,128]{3,2,1,0:T(8,128)} %get-tuple-element.16), channel_id=1, source_target_pairs={{0,1},{1,4},{4,5},{5,8},{8,9},{9,12},{12,13},{2,3},{3,6},{6,7},{7,... | collective-permute-start | bytes 491528 | tf_op jit(solution)/shard_map/ppermute | solution.py:205
  62.9 3.9 %collective-permute-start.3 = (f32[5,8,8,128]{3,2,1,0:T(8,128)}, f32[5,8,8,128]{3,2,1,0:T(8,128)}, u32[]{:S(2)}, u32[]{:S(2)}) collective-permute-start(f32[5,8,8,128]{3,2,1,0:T(8,128)} %get-tuple-element.17), channel_id=1, source_target_pairs={{1,0},{4,1},{5,4},{8,5},{9,8},{12,9},{13,12},{3,2},{6,3},{7,6},{10... | collective-permute-start | bytes 491528 | tf_op jit(solution)/shard_map/ppermute | solution.py:205
  67.1 1.1 collective-permute-done.2.from_prev
  68.2 1.8 %collective-permute-done.3.from_next = f32[5,8,8,128]{3,2,1,0:T(8,128)} collective-permute-done((f32[5,8,8,128]{3,2,1,0:T(8,128)}, f32[5,8,8,128]{3,2,1,0:T(8,128)}, u32[]{:S(2)}, u32[]{:S(2)}) %collective-permute-start.3) | collective-permute-done | bytes 163872 | tf_op jit(solution)/shard_map/ppermute | solution.py:205
  69.9 1.1 copy-done.2
  71.0 3.9 %second_residual.1 = f32[16,5,2,8,128]{4,3,2,1,0:T(8,128)S(1)} custom-call(f32[5,3]{1,0:T(8,128)S(1)} %bitcast.22, f32[2]{0:T(128)S(1)} %add_convert_fusion.inner, f32[5,5]{1,0:T(8,128)S(1)} %get-tuple-element.23.both, f32[5,5]{1,0:T(8,128)S(1)} %get-tuple-element.22.both_lap, f32[5,32,8,128]{3,2,1,0:T(8,128)S(1)} %copy-done.2, ...), custom_call_target="tpu_custom_call" | custom-call | flops 300000000 | bytes 4000000 | tf_op jit(solution)/shard_map/second_residual/pallas_call | solution.py:288
  74.9 20.1 %all_to_all.20.solved = f32[16,5,2,8,128]{4,3,2,1,0:T(8,128)S(1)} all-to-all(f32[16,5,2,8,128]{4,3,2,1,0:T(8,128)S(1)} %second_residual.1), channel_id=1, replica_groups=mesh['cond'=32,'grid'=16] {'grid'}, dimensions={0} | all-to-all | bytes 1310720 | tf_op jit(solution)/shard_map/all_to_all | solution.py:297
  95.0 2.3 %update.1 = (f32[2,5,2,64,128]{4,3,2,1,0:T(8,128)}, f32[2,5,64,128]{3,2,1,0:T(8,128)S(1)}, f32[2,5,64,128]{3,2,1,0:T(8,128)S(1)}) custom-call(f32[2,5,5]{2,1,0:T(8,128)S(1)} %copy.49.right, f32[2,5,2,64,128]{4,3,2,1,0:T(8,128)S(1)} %copy-done, f32[16,5,2,8,128]{4,3,2,1,0:T(8,128)S(1)} %all_to_all.20.solved, f32[2,5,64,64]{3,2,1,0:T(8,128)S(1)} %get-tuple-element.13.solve_y), custom_call_target="tpu_custom_call" | custom-call | flops 60000000 | bytes 4000000 | tf_op jit(solution)/shard_map/update/pallas_call | solution.py:299
  97.3 2.2 %collective-permute-start.4 = (f32[2,5,64,128]{3,2,1,0:T(8,128)S(1)}, f32[2,5,64,128]{3,2,1,0:T(8,128)S(1)}, u32[]{:S(2)}, u32[]{:S(2)}) collective-permute-start(f32[2,5,64,128]{3,2,1,0:T(8,128)S(1)} %get-tuple-element.20), channel_id=1, source_target_pairs={{0,1},{1,2},{2,3},{3,4},{4,5},{5,6},{6,7},{7,8},{8,9},{9,10},{10,1... | collective-permute-start | bytes 983048 | tf_op jit(solution)/shard_map/ppermute | solution.py:205
  99.5 8.2 %collective-permute-start.5 = (f32[2,5,64,128]{3,2,1,0:T(8,128)S(1)}, f32[2,5,64,128]{3,2,1,0:T(8,128)S(1)}, u32[]{:S(2)}, u32[]{:S(2)}) collective-permute-start(f32[2,5,64,128]{3,2,1,0:T(8,128)S(1)} %get-tuple-element.21), channel_id=1, source_target_pairs={{1,0},{2,1},{3,2},{4,3},{5,4},{6,5},{7,6},{8,7},{9,8},{10,9},{11,1... | collective-permute-start | bytes 983048 | tf_op jit(solution)/shard_map/ppermute | solution.py:205
  107.7 2.8 %collective-permute-done.4.low = f32[2,5,64,128]{3,2,1,0:T(8,128)S(1)} collective-permute-done((f32[2,5,64,128]{3,2,1,0:T(8,128)S(1)}, f32[2,5,64,128]{3,2,1,0:T(8,128)S(1)}, u32[]{:S(2)}, u32[]{:S(2)}) %collective-permute-start.4) | collective-permute-done | bytes 327712 | tf_op jit(solution)/shard_map/ppermute | solution.py:205
  110.5 1.8 %collective-permute-done.5.high = f32[2,5,64,128]{3,2,1,0:T(8,128)S(1)} collective-permute-done((f32[2,5,64,128]{3,2,1,0:T(8,128)S(1)}, f32[2,5,64,128]{3,2,1,0:T(8,128)S(1)}, u32[]{:S(2)}, u32[]{:S(2)}) %collective-permute-start.5) | collective-permute-done | bytes 327712 | tf_op jit(solution)/shard_map/ppermute | solution.py:205
  112.2 1.1 copy-done.3
  114.4 35.9 %all_to_all.21.pieces = f32[32,16,128]{2,1,0:T(8,128)S(1)} all-to-all(f32[32,16,128]{2,1,0:T(8,128)S(1)} %bitcast.23), channel_id=1, replica_groups=mesh['cond'=32,'grid'=16] {'cond'}, dimensions={0} | all-to-all | bytes 524288 | tf_op jit(solution)/shard_map/all_to_all | solution.py:322
  150.3 16.6 %all_to_all.22 = f32[32,16,128]{2,1,0:T(8,128)S(1)} all-to-all(f32[32,16,128]{2,1,0:T(8,128)S(1)} %sum_conditions.1), channel_id=1, replica_groups=mesh['cond'=32,'grid'=16] {'cond'}, dimensions={0} | all-to-all | bytes 524288 | tf_op jit(solution)/shard_map/all_to_all | solution.py:331
  (53 shorter events, 5.7 us)
Async XLA Ops:
  0.6 12.7 %copy-start.11 = (f32[1,128]{1,0:T(1,128)S(1)}, f32[1,128]{1,0:T(1,128)}, u32[]{:S(2)}) copy-start(f32[1,128]{1,0:T(1,128)} %constant.75.clone.spec_z) | copy-start | bytes 1540
  0.6 12.7 %copy-start.9 = (f32[64,64]{1,0:T(8,128)S(1)}, f32[64,64]{1,0:T(8,128)}, u32[]{:S(2)}) copy-start(f32[64,64]{1,0:T(8,128)} %constant.76.clone.sine_y) | copy-start | bytes 49156
  0.7 12.7 %copy-start.12 = (f32[1,64]{1,0:T(1,128)S(1)}, f32[1,64]{1,0:T(1,128)}, u32[]{:S(2)}) copy-start(f32[1,64]{1,0:T(1,128)} %constant.77.clone.spec_y) | copy-start | bytes 772
  0.7 12.7 %copy-start.13 = (f32[1,32]{1,0:T(1,128)S(1)}, f32[1,32]{1,0:T(1,128)}, u32[]{:S(2)}) copy-start(f32[1,32]{1,0:T(1,128)} %constant.80.clone.spec_x) | copy-start | bytes 388
  0.7 24.7 %copy-start = (f32[2,5,2,64,128]{4,3,2,1,0:T(8,128)S(1)}, f32[2,5,2,64,128]{4,3,2,1,0:T(8,128)}, u32[]{:S(2)}) copy-start(f32[2,5,2,64,128]{4,3,2,1,0:T(8,128)} %adjoint.3) | copy-start | bytes 1966084
  0.7 12.5 %copy-start.14 = (f32[2,5,3]{1,0,2:T(2,128)S(1)}, f32[2,5,3]{1,0,2:T(2,128)}, u32[]{:S(2)}) copy-start(f32[2,5,3]{1,0,2:T(2,128)} %param.22) | copy-start | bytes 364
  0.7 12.6 %copy-start.15 = (f32[2,5,5]{2,0,1:T(2,128)S(1)}, f32[2,5,5]{2,0,1:T(2,128)}, u32[]{:S(2)}) copy-start(f32[2,5,5]{2,0,1:T(2,128)} %param.20) | copy-start | bytes 604
  0.7 12.6 %copy-start.16 = (f32[2,5,5]{2,0,1:T(2,128)S(1)}, f32[2,5,5]{2,0,1:T(2,128)}, u32[]{:S(2)}) copy-start(f32[2,5,5]{2,0,1:T(2,128)} %param.19) | copy-start | bytes 604
  0.7 24.7 %copy-start.4 = (f32[2,5,2,64,128]{4,3,2,1,0:T(8,128)S(1)}, f32[2,5,2,64,128]{4,3,2,1,0:T(8,128)}, u32[]{:S(2)}) copy-start(f32[2,5,2,64,128]{4,3,2,1,0:T(8,128)} %source.1) | copy-start | bytes 1966084
  0.7 24.7 %copy-start.5 = (f32[2,64,128]{2,1,0:T(8,128)S(1)}, f32[2,64,128]{2,1,0:T(8,128)}, u32[]{:S(2)}) copy-start(f32[2,64,128]{2,1,0:T(8,128)} %radius.1) | copy-start | bytes 196612
  2.8 15.7 %collective-permute-start = (f32[2,5,64,128]{3,2,1,0:T(8,128)}, f32[2,5,64,128]{3,2,1,0:T(8,128)}, u32[]{:S(2)}, u32[]{:S(2)}) collective-permute-start(f32[2,5,64,128]{3,2,1,0:T(8,128)} %get-tuple-element.25), channel_id=1, source_target_pairs={{0,1},{1,2},{2,3},{3,4},{4,5},{5,6},{6,7},{7,8},{8,9},{9,10},{10,1... | collective-permute-start | bytes 983048 | tf_op jit(solution)/shard_map/ppermute | solution.py:205
  4.7 20.7 %collective-permute-start.1 = (f32[2,5,64,128]{3,2,1,0:T(8,128)}, f32[2,5,64,128]{3,2,1,0:T(8,128)}, u32[]{:S(2)}, u32[]{:S(2)}) collective-permute-start(f32[2,5,64,128]{3,2,1,0:T(8,128)} %get-tuple-element.24), channel_id=1, source_target_pairs={{1,0},{2,1},{3,2},{4,3},{5,4},{6,5},{7,6},{8,7},{9,8},{10,9},{11,1... | collective-permute-start | bytes 983048 | tf_op jit(solution)/shard_map/ppermute | solution.py:205
  13.4 0.9 copy-start.7
  14.3 0.8 copy-start.8
  33.1 9.6 %copy-start.17 = (f32[2,5,5]{2,0,1:T(2,128)S(1)}, f32[2,5,5]{2,0,1:T(2,128)}, u32[]{:S(2)}) copy-start(f32[2,5,5]{2,0,1:T(2,128)} %param.21) | copy-start | bytes 604
  33.1 25.1 %all-to-all-start = ((f32[16,6,2,8,128]{4,3,2,1,0:T(8,128)}), f32[16,6,2,8,128]{4,3,2,1,0:T(8,128)S(1)}, u32[]{:S(2)}, u32[]{:S(2)}) async-start(f32[16,6,2,8,128]{4,3,2,1,0:T(8,128)} %first_residual.1), calls=%async_computation | async-start | bytes 1572864 | tf_op jit(solution)/shard_map/all_to_all | solution.py:265
  60.9 7.2 %collective-permute-start.2 = (f32[5,8,8,128]{3,2,1,0:T(8,128)}, f32[5,8,8,128]{3,2,1,0:T(8,128)}, u32[]{:S(2)}, u32[]{:S(2)}) collective-permute-start(f32[5,8,8,128]{3,2,1,0:T(8,128)} %get-tuple-element.16), channel_id=1, source_target_pairs={{0,1},{1,4},{4,5},{5,8},{8,9},{9,12},{12,13},{2,3},{3,6},{6,7},{7,... | collective-permute-start | bytes 491528 | tf_op jit(solution)/shard_map/ppermute | solution.py:205
  62.9 7.1 %collective-permute-start.3 = (f32[5,8,8,128]{3,2,1,0:T(8,128)}, f32[5,8,8,128]{3,2,1,0:T(8,128)}, u32[]{:S(2)}, u32[]{:S(2)}) collective-permute-start(f32[5,8,8,128]{3,2,1,0:T(8,128)} %get-tuple-element.17), channel_id=1, source_target_pairs={{1,0},{4,1},{5,4},{8,5},{9,8},{12,9},{13,12},{3,2},{6,3},{7,6},{10... | collective-permute-start | bytes 491528 | tf_op jit(solution)/shard_map/ppermute | solution.py:205
  69.9 1.1 copy-start.2
  74.9 32.7 %copy-start.18 = (f32[2,3,5]{2,0,1:T(2,128)S(1)}, f32[2,3,5]{2,0,1:T(2,128)}, u32[]{:S(2)}) copy-start(f32[2,3,5]{2,0,1:T(2,128)} %param.23) | copy-start | bytes 364
  74.9 37.3 %copy-start.6 = (s32[2]{0:T(128)S(1)}, s32[2]{0:T(128)}, u32[]{:S(2)}) copy-start(s32[2]{0:T(128)} %weights.1) | copy-start | bytes 28
  97.3 13.2 %collective-permute-start.4 = (f32[2,5,64,128]{3,2,1,0:T(8,128)S(1)}, f32[2,5,64,128]{3,2,1,0:T(8,128)S(1)}, u32[]{:S(2)}, u32[]{:S(2)}) collective-permute-start(f32[2,5,64,128]{3,2,1,0:T(8,128)S(1)} %get-tuple-element.20), channel_id=1, source_target_pairs={{0,1},{1,2},{2,3},{3,4},{4,5},{5,6},{6,7},{7,8},{8,9},{9,10},{10,1... | collective-permute-start | bytes 983048 | tf_op jit(solution)/shard_map/ppermute | solution.py:205
  99.5 12.8 %collective-permute-start.5 = (f32[2,5,64,128]{3,2,1,0:T(8,128)S(1)}, f32[2,5,64,128]{3,2,1,0:T(8,128)S(1)}, u32[]{:S(2)}, u32[]{:S(2)}) collective-permute-start(f32[2,5,64,128]{3,2,1,0:T(8,128)S(1)} %get-tuple-element.21), channel_id=1, source_target_pairs={{1,0},{2,1},{3,2},{4,3},{5,4},{6,5},{7,6},{8,7},{9,8},{10,9},{11,1... | collective-permute-start | bytes 983048 | tf_op jit(solution)/shard_map/ppermute | solution.py:205
  112.2 1.1 copy-start.3
  (2 other events, 1.6 us)

commit v2 on v1

--- a/solution.py
+++ b/solution.py
@@ -14,7 +14,7 @@
 FIELDS = 5
 VMEM = pl.BlockSpec(memory_space=pltpu.VMEM)
 SMEM = pl.BlockSpec(memory_space=pltpu.SMEM)
-LIMIT = 40 * 1024 * 1024
+LIMIT = 20 * 1024 * 1024
 
 
 def dot(a, b):
@@ -73,15 +73,22 @@
         solve_zb[f] = solve_z[mine, f]
 
 
-def first_kernel(coupling, left, adjoint, low, high, source, radius, solve_z, solve_y, out, lapped):
-    blocks = adjoint.shape[3] // 8
+def spot(c, b):
+    return (b // 2) * 4 + c * 2 + b % 2
+
+
+def first_kernel(
+    core, coupling, left, left_coup, adjoint, inner, source, radius, solve_z, solve_y, out, lapped, stage
+):
+    ny = adjoint.shape[3]
+    blocks = ny // 8
+    me = core[0]
+    before, after = me.astype(F32), (1 - me).astype(F32)
     for c in range(2):
         for x in range(2):
             for f in range(FIELDS):
                 v = adjoint[c, f, x]
-                beside = (low[c, f] if x == 0 else adjoint[c, f, 0]) + (
-                    adjoint[c, f, 1] if x == 0 else high[c, f]
-                )
+                beside = adjoint[c, f, 1 - x] + inner[c, f] * (before if x == 0 else after)
                 beside = beside + shifted(v, 0, 1) + shifted(v, 0, -1)
                 beside = beside + shifted(v, 1, 1) + shifted(v, 1, -1)
                 lapped[f] = 6.0 * v - beside
@@ -96,22 +103,42 @@
                 r = left[c, f, 0] * residual[0]
                 for g in range(1, FIELDS):
                     r = r + left[c, f, g] * residual[g]
-                r = dot(solve_y[c, f], dot(r, solve_z[c, f]))
+                stage[f, x * ny : x * ny + ny] = r
+        outer = [adjoint[c, g, me] for g in range(FIELDS)]
+        for f in range(FIELDS):
+            r = left_coup[c, f, 0] * outer[0]
+            for g in range(1, FIELDS):
+                r = r + left_coup[c, f, g] * outer[g]
+            stage[f, 2 * ny : 3 * ny] = r
+        for f in range(FIELDS):
+            r = dot(stage[f], solve_z[c, f])
+            for p in range(3):
+                s = dot(solve_y[c, f], r[p * ny : p * ny + ny])
                 for b in range(blocks):
-                    out[(b // 2) * 4 + c * 2 + b % 2, f, x] = r[8 * b : 8 * b + 8]
+                    out[spot(c, b), 3 * f + p] = s[8 * b : 8 * b + 8]
+        for x in range(2):
             for b in range(blocks):
-                out[(b // 2) * 4 + c * 2 + b % 2, FIELDS, x] = sr[8 * b : 8 * b + 8]
-
-
-def across_kernel(lines, solve_x, solved, to_prev, to_next):
+                out[spot(c, b), 3 * FIELDS + x] = radius[x, 8 * b : 8 * b + 8]
+
+
+def across_kernel(core, lines, solve_x, adjoint, solved, to_prev, to_next, outer):
     n = solve_x.shape[1]
+    peers = lines.shape[0]
+    zero = jnp.zeros((1, 8, 128), F32)
     for f in range(FIELDS):
-        u = dot(solve_x[f], lines[:, f].reshape(n, 128)).reshape(n // 8, 8, 128)
+        w = lines[:, 3 * f : 3 * f + 3].reshape(peers // 2, 6, 8, 128)
+        plane_0 = w[:, 0] + jnp.concatenate([zero, w[:-1, 5]], axis=0)
+        plane_3 = w[:, 4] + jnp.concatenate([w[1:, 2], zero], axis=0)
+        w = jnp.stack([plane_0, w[:, 1], w[:, 3], plane_3], axis=1).reshape(n, 128)
+        u = dot(solve_x[f], w).reshape(n // 8, 8, 128)
         solved[f] = u
         quad = u.reshape(n // 32, 4, 8, 128)
         for j in range(4):
             to_prev[f, :, 2 * j : 2 * j + 2, :] = quad[:, j, 0:2, :]
             to_next[f, :, 2 * j : 2 * j + 2, :] = quad[:, j, 6:8, :]
+    for c in range(2):
+        for f in range(FIELDS):
+            outer[c, f] = adjoint[c, f, core[0]]
 
 
 def second_kernel(rates, inner, both, both_lap, solved, from_prev, from_next, lines, solve_x, solve_z,
@@ -141,7 +168,7 @@
         flat = u.reshape(nx * 8, 128)
         beside = beside + (shifted(flat, 1, 1) + shifted(flat, 1, -1)).reshape(full)
         lapped[f] = 4.0 * u + ku - beside
-    sr = lines[:, FIELDS].reshape(full)
+    sr = lines[:, 3 * FIELDS :].reshape(full)
     for f in range(FIELDS):
         near = both[f, 0] * solved[0]
         far = both_lap[f, 0] * lapped[0]
@@ -150,46 +177,91 @@
             far = far + both_lap[f, g] * lapped[g]
         v = (sr * near + far).reshape(nx * 8, 128)
         v = dot(solve_x[f], dot(v, solve_z[f]))
-        out[:, f] = (kept[f] - v.reshape(full)).reshape(nx // 2, 2, 8, 128)
-
-
-def update_kernel(right, adjoint, solved, solve_y, out, first, last, step):
+        q = kept[f] - v.reshape(full)
+        chips = q.reshape(nx // 4, 4, 8, 128)
+        zero = jnp.zeros((1, 8, 128), F32)
+        outer_0 = jnp.concatenate([zero, chips[:-1, 3]], axis=0)
+        outer_1 = jnp.concatenate([chips[1:, 0], zero], axis=0)
+        out[:, 3 * f : 3 * f + 3] = jnp.stack(
+            [chips[:, 0], chips[:, 1], outer_0, chips[:, 2], chips[:, 3], outer_1], axis=1
+        ).reshape(nx // 2, 3, 8, 128)
+
+
+def gathered(solved, c, tile, blocks):
+    return jnp.concatenate([solved[spot(c, b), tile] for b in range(blocks)], axis=0)
+
+
+def update_kernel(core, right, adjoint, solved, solve_y, out, inner, step):
     blocks = adjoint.shape[3] // 8
+    me = core[0]
     for c in range(2):
         for x in range(2):
             for f in range(FIELDS):
-                q = jnp.concatenate(
-                    [solved[(b // 2) * 4 + c * 2 + b % 2, f, x] for b in range(blocks)], axis=0
-                )
-                step[f] = dot(solve_y[c, f], q)
-            for f in range(FIELDS):
+                step[x, f] = dot(solve_y[c, f], gathered(solved, c, 3 * f + x, blocks))
+        for f in range(FIELDS):
+            planes = []
+            for x in range(2):
                 a = adjoint[c, f, x]
                 for g in range(FIELDS):
-                    a = a + right[c, f, g] * step[g]
+                    a = a + right[c, f, g] * step[x, g]
                 out[c, f, x] = a
-                if x == 0:
-                    first[c, f] = a
-                else:
-                    last[c, f] = a
-
-
-def terms_kernel(smap, weights, adjoint, low, high, out):
+                planes.append(a)
+            inner[c, f] = jnp.where(me == 0, planes[1], planes[0])
+
+
+def inside_kernel(right, smap, weights, adjoint, start_outer, solved, solve_y, outer, terms, step):
+    blocks = adjoint.shape[3] // 8
+    for c in range(2):
+        for f in range(FIELDS):
+            step[f] = dot(solve_y[c, f], gathered(solved, c, 3 * f + 2, blocks))
+        for f in range(FIELDS):
+            a = start_outer[c, f]
+            for g in range(FIELDS):
+                a = a + right[c, f, g] * step[g]
+            outer[c, f] = a
     for x in range(2):
-        total = [None, None, None]
+        total = [None, None]
         for c in range(2):
             w = weights[c].astype(F32)
             for f in range(FIELDS):
                 v = adjoint[c, f, x]
-                diffs = (
-                    (adjoint[c, f, 1] - low[c, f]) if x == 0 else (high[c, f] - adjoint[c, f, 0]),
-                    shifted(v, 0, 1) - shifted(v, 0, -1),
-                    shifted(v, 1, 1) - shifted(v, 1, -1),
-                )
-                for k in range(3):
-                    t = (w * smap[c, k, f]) * (v * diffs[k])
+                for k in range(2):
+                    diff = shifted(v, k, 1) - shifted(v, k, -1)
+                    t = (w * smap[c, k + 1, f]) * (v * diff)
                     total[k] = t if total[k] is None else total[k] + t
-        for k in range(3):
-            out[k, x] = total[k]
+        for k in range(2):
+            terms[k, x] = total[k]
+
+
+def terms_kernel(core, smap, weights, adjoint, inner, outer, inside, out):
+    me = core[0]
+    ny = adjoint.shape[3]
+    each = out.shape[1] // 8
+
+    def store(k, x, v):
+        for i in range(ny // 8):
+            piece, at = divmod((k * 2 + x) * (ny // 8) + i, each)
+            out[piece, 8 * at : 8 * at + 8] = v[8 * i : 8 * i + 8]
+
+    totals = [None, None]
+    for c in range(2):
+        w = weights[c].astype(F32)
+        for f in range(FIELDS):
+            low = jnp.where(me == 0, outer[c, f], inner[c, f])
+            high = jnp.where(me == 0, inner[c, f], outer[c, f])
+            s = w * smap[c, 0, f]
+            t = (
+                s * (adjoint[c, f, 0] * (adjoint[c, f, 1] - low)),
+                s * (adjoint[c, f, 1] * (high - adjoint[c, f, 0])),
+            )
+            totals = [t[x] if totals[x] is None else totals[x] + t[x] for x in range(2)]
+    for x in range(2):
+        store(0, x, totals[x])
+        for k in range(2):
+            store(k + 1, x, inside[k, x])
+    for tile in range(6 * ny // 8, out.shape[0] * each):
+        piece, at = divmod(tile, each)
+        out[piece, 8 * at : 8 * at + 8] = jnp.zeros((8, out.shape[2]), F32)
 
 
 def sum_kernel(scale, pieces, out):
@@ -199,10 +271,6 @@
     total = total * scale
     for i in range(out.shape[0]):
         out[i] = total
-
-
-def exchange(first, last, axis, up, down):
-    return lax.ppermute(last, axis, up), lax.ppermute(first, axis, down)
 
 
 def body(
@@ -231,9 +299,13 @@
     sine_x, spec_x = sine_tables(nx)
     left_x = np.repeat(sine_x, 8, axis=0)
 
-    up = [(i, i + 1) for i in range(peers - 1)]
-    down = [(j, i) for i, j in up]
-    low, high = exchange(adjoint_start[:, :, 0], adjoint_start[:, :, planes - 1], "grid", up, down)
+    core = me % 2
+    core_arg = core.reshape(1).astype(jnp.int32)
+    cores = [(i, i ^ 1) for i in range(peers)]
+    chips = [(i, i + 1) for i in range(1, peers - 1, 2)]
+    chips = chips + [(j, i) for i, j in chips]
+    inner = lax.dynamic_index_in_dim(adjoint_start, 1 - core, 2, keepdims=False)
+    inner = lax.ppermute(inner, "grid", cores)
 
     solve_z, solve_y, solve_x, solve_zb = call(
         tables_kernel,
@@ -253,72 +325,88 @@
         jnp.asarray(spec_x[None, :]),
     )
 
+    mix = lambda a, b: jnp.sum(a[..., :, :, None] * b[..., None, :, :], axis=-2)
+    left_coup = mix(left_vectors, coupling)
+
     lines = call(
         first_kernel,
-        shape(peers, fields + 1, planes, 8, nz),
-        [SMEM, SMEM] + [VMEM] * 7,
+        shape(peers, 3 * fields + planes, 8, nz),
+        [SMEM] * 4 + [VMEM] * 6,
         200_000_000,
         "first_residual",
-        [pltpu.VMEM((fields, ny, nz), F32)],
-    )(coupling, left_vectors, adjoint_start, low, high, adjoint_source, spectral_radius, solve_z, solve_y)
+        [pltpu.VMEM((fields, ny, nz), F32), pltpu.VMEM((fields, 3 * ny, nz), F32)],
+    )(
+        core_arg, coupling, left_vectors, left_coup,
+        adjoint_start, inner, adjoint_source, spectral_radius, solve_z, solve_y,
+    )
 
     lines = lax.all_to_all(lines, "grid", 0, 0, tiled=True)
 
-    solved, to_prev, to_next = call(
+    solved, to_prev, to_next, outer = call(
         across_kernel,
-        (shape(fields, nx, 8, nz), shape(fields, nx // 4, 8, nz), shape(fields, nx // 4, 8, nz)),
-        [VMEM, VMEM],
+        (
+            shape(fields, nx, 8, nz),
+            shape(fields, nx // 4, 8, nz),
+            shape(fields, nx // 4, 8, nz),
+            shape(2, fields, ny, nz),
+        ),
+        [SMEM, VMEM, VMEM, VMEM],
         100_000_000,
         "solve_across",
-    )(lines, solve_x)
-
-    spot = lambda s, b: (b // 2) * 4 + s * 2 + b % 2
+    )(core_arg, lines, solve_x, adjoint_start)
+
     blocks = peers // 2
-    up_b = [(spot(s, b), spot(s, b + 1)) for s in range(2) for b in range(blocks - 1)]
-    down_b = [(j, i) for i, j in up_b]
-    from_prev, from_next = exchange(to_prev, to_next, "grid", up_b, down_b)
+    up = [(spot(s, b), spot(s, b + 1)) for s in range(2) for b in range(blocks - 1)]
+    down = [(j, i) for i, j in up]
+    from_prev = lax.ppermute(to_next, "grid", up)
+    from_next = lax.ppermute(to_prev, "grid", down)
+    outer = lax.ppermute(outer, "grid", chips)
 
     pick = lambda v: lax.dynamic_index_in_dim(v, side, 0, keepdims=False)
-    left_b, coup_b, right_b = pick(left_vectors), pick(coupling), pick(right_vectors)
-    both = jnp.sum(left_b[:, :, None] * right_b[None, :, :], axis=1)
-    inner_mix = jnp.sum(coup_b[:, :, None] * right_b[None, :, :], axis=1)
-    both_lap = jnp.sum(left_b[:, :, None] * inner_mix[None, :, :], axis=1)
-    inner = jnp.stack([place > 0, place < blocks - 1]).astype(F32)
+    both = mix(pick(left_vectors), pick(right_vectors))
+    both_lap = mix(pick(left_coup), pick(right_vectors))
+    ends = jnp.stack([place > 0, place < blocks - 1]).astype(F32)
 
     step = call(
         second_kernel,
-        shape(peers, fields, planes, 8, nz),
+        shape(peers, 3 * fields, 8, nz),
         [SMEM] * 4 + [VMEM] * 6,
         300_000_000,
         "second_residual",
         [pltpu.VMEM((fields, nx, 8, nz), F32), pltpu.VMEM((fields, nx, 8, nz), F32)],
-    )(pick(implicit_scales), inner, both, both_lap, solved, from_prev, from_next, lines, solve_x, solve_zb)
+    )(pick(implicit_scales), ends, both, both_lap, solved, from_prev, from_next, lines, solve_x, solve_zb)
 
     step = lax.all_to_all(step, "grid", 0, 0, tiled=True)
 
-    adjoint, first, last = call(
+    adjoint, inner = call(
         update_kernel,
-        (shape(2, fields, planes, ny, nz), shape(2, fields, ny, nz), shape(2, fields, ny, nz)),
-        [SMEM] + [VMEM] * 3,
+        (shape(2, fields, planes, ny, nz), shape(2, fields, ny, nz)),
+        [SMEM, SMEM] + [VMEM] * 3,
         60_000_000,
         "update",
+        [pltpu.VMEM((2, fields, ny, nz), F32)],
+    )(core_arg, right_vectors, adjoint_start, step, solve_y)
+
+    inner = lax.ppermute(inner, "grid", cores)
+
+    outer, inside = call(
+        inside_kernel,
+        (shape(2, fields, ny, nz), shape(2, planes, ny, nz)),
+        [SMEM] * 3 + [VMEM] * 4,
+        60_000_000,
+        "inside_terms",
         [pltpu.VMEM((fields, ny, nz), F32)],
-    )(right_vectors, adjoint_start, step, solve_y)
-
-    low, high = exchange(first, last, "grid", up, down)
-
-    terms = call(
+    )(right_vectors, sensitivity_map, condition_weights, adjoint, outer, step, solve_y)
+
+    tiles = 3 * planes * ny // 8
+    each = -(-tiles // conds)
+    pieces = call(
         terms_kernel,
-        shape(3, planes, ny, nz),
-        [SMEM, SMEM] + [VMEM] * 3,
+        shape(conds, each * 8, nz),
+        [SMEM] * 3 + [VMEM] * 4,
         10_000_000,
         "terms",
-    )(sensitivity_map, condition_weights, adjoint, low, high)
-
-    tiles = 3 * planes * ny // 8
-    each = -(-tiles // conds)
-    pieces = terms.reshape(tiles * 8, nz)
-    pieces = jnp.pad(pieces, ((0, (conds * each - tiles) * 8), (0, 0))).reshape(conds, each * 8, nz)
+    )(core_arg, sensitivity_map, condition_weights, adjoint, inner, outer, inside)
     pieces = lax.all_to_all(pieces, "cond", 0, 0, tiled=True)
     scale = 1.0 / (conds * condition_weights.shape[0])
     pieces = call(

time: 168 us -> 170 us (1.012)
  blocking collectives: 72.5 us -> 44.9 us
  waiting for transfers between devices: 29.5 us -> 55.4 us
  local copies, waits for them, and re-layouts: 8.59 us -> 18.7 us
  starting transfers between devices: 36.2 us -> 31 us
  Pallas kernels: 19.5 us -> 16.7 us
    all_to_all x1 -> x0, blocking collectives: 20.1 us -> none  [body(): step = lax.all_to_all(step, 'grid', 0, 0, tiled=True)]
    all_to_all x1, waiting for transfers between devices: 15.3 us -> 26.1 us  [body(): lines = lax.all_to_all(lines, 'grid', 0, 0, tiled=True)]
    all_to_all x0 -> x1, waiting for transfers between devices: none -> 10.6 us  [body(): step = lax.all_to_all(step, 'grid', 0, 0, tiled=True)]
    unnamed x43 -> x53, local copies, waits for them, and re-layouts: 5.68 us -> 16.1 us
    ppermute x6 -> x5, starting transfers between devices: 26.5 us -> 16.4 us  [the longest x1 7.03 us: body(): outer = lax.ppermute(outer, 'grid', chips)]
    all_to_all x2, blocking collectives: 52.5 us -> 44.9 us  [body(): pieces = lax.all_to_all(pieces, 'cond', 0, 0, tiled=True)]
    ppermute x6 -> x5, waiting for transfers between devices: 14.2 us -> 18.7 us  [the longest x1 15.8 us: body(): outer = lax.ppermute(outer, 'grid', chips)]
    all_to_all x0 -> x1, starting transfers between devices: none -> 4.25 us  [body(): step = lax.all_to_all(step, 'grid', 0, 0, tiled=True)]
  transfers between devices with their start and end apart: 7 -> 7, of which waited for: 6 -> 5; matrix products, arithmetic and copies ran while one was open for 0% -> 2% of each run, Pallas kernels for 2% -> 4%
where the time goes in v2:
time: 170 us; the launch traced here: 169 us
  waiting for transfers between devices  55.4 us (33%)
  blocking collectives  44.9 us (26%)
  starting transfers between devices  31 us (18%)
  local copies, waits for them, and re-layouts  18.7 us (11%)
  Pallas kernels  16.7 us (10%)
    all_to_all x2, blocking collectives, body(): pieces = lax.all_to_all(pieces, 'cond', 0, 0, tiled=True)  44.9 us
    all_to_all x1, waiting for transfers between devices, body(): lines = lax.all_to_all(lines, 'grid', 0, 0, tiled=True)  26.1 us
    unnamed x53, local copies, waits for them, and re-layouts  16.1 us
    ppermute x1, waiting for transfers between devices, body(): outer = lax.ppermute(outer, 'grid', chips)  15.8 us
    all_to_all x1, waiting for transfers between devices, body(): step = lax.all_to_all(step, 'grid', 0, 0, tiled=True)  10.6 us
    all_to_all x1, starting transfers between devices, body(): lines = lax.all_to_all(lines, 'grid', 0, 0, tiled=True)  10.3 us
    ppermute x1, starting transfers between devices, body(): outer = lax.ppermute(outer, 'grid', chips)  7.03 us
    all_to_all x1, starting transfers between devices, body(): step = lax.all_to_all(step, 'grid', 0, 0, tiled=True)  4.25 us
  transfers between devices with their start and end apart: 7, of which 5 were waited for; matrix products, arithmetic and copies ran while one was open for 2% of the time, Pallas kernels for 4%

profile of v2, /device:TPU:2, one launch (start us, length us, event | category | flops | bytes accessed | tf_op | source)
XLA Modules:
  0.0 168.6 jit_solution(10606546461768608569)
XLA Ops:
  0.7 1.8 %dynamic-slice_bitcast_fusion = f32[2,5,64,128]{3,2,1,0:T(8,128)} fusion(f32[2,5,2,64,128]{4,3,2,1,0:T(8,128)} %adjoint.5, s32[]{:T(128)S(6)} %select_n.38), kind=kLoop, calls=%fused_computation | loop fusion | bytes 655364 | tf_op jit(solution)/shard_map/jit(dynamic_index_in_dim)/squeeze | solution.py:307
  2.5 1.9 %collective-permute-start = (f32[2,5,64,128]{3,2,1,0:T(8,128)}, f32[2,5,64,128]{3,2,1,0:T(8,128)}, u32[]{:S(2)}, u32[]{:S(2)}) collective-permute-start(f32[2,5,64,128]{3,2,1,0:T(8,128)} %dynamic-slice_bitcast_fusion), channel_id=1, source_target_pairs={{0,1},{1,0},{2,3},{3,2},{4,5},{5,4},{6,7},{7,6},{8,9},{9,8},{10,11... | collective-permute-start | bytes 983048 | tf_op jit(solution)/shard_map/ppermute | solution.py:308
  13.4 2.6 %solve_tables.1 = (f32[2,5,128,128]{3,2,1,0:T(8,128)S(1)}, f32[2,5,64,64]{3,2,1,0:T(8,128)S(1)}, f32[5,256,256]{2,1,0:T(8,128)S(1)}, f32[5,128,128]{2,1,0:T(8,128)S(1)}) custom-call(f32[2,5,3]{2,1,0:T(8,128)S(1)} %copy.45.rates, s32[1]{0:T(128)} %bitcast.7.side, f32[128,128]{1,0:T(8,128)S(1)} %copy-done.14, f32[1,128]{1,0:T(1,128)S(1)} %copy-done.17, ...), custom_call_target="tpu_custom_call" | custom-call | flops 100000000 | bytes 4000000 | tf_op jit(solution)/shard_map/solve_tables/pallas_call | solution.py:310
  16.1 1.2 copy-done.4
  17.3 3.6 %first_residual.1 = f32[16,17,8,128]{3,2,1,0:T(8,128)S(1)} custom-call(s32[1]{0:T(128)} %bitcast.core, f32[2,5,5]{2,1,0:T(8,128)S(1)} %copy.46.coupling, f32[2,5,5]{2,1,0:T(8,128)S(1)} %copy.42.left, f32[2,5,5]{2,1,0:T(8,128)S(1)} %copy.48.left_coup, f32[2,5,2,64,128]{4,3,2,1,0:T(8,128)S(1)} %copy-done, f32[2,5,64,128]{3,2,1,0:T(8,128)} %collective-permute-done.inner, ...), custom_call_target="tpu_custom_call" | custom-call | flops 200000000 | bytes 4000000 | tf_op jit(solution)/shard_map/first_residual/pallas_call | solution.py:331
  21.9 10.3 %all-to-all-start = ((f32[16,17,8,128]{3,2,1,0:T(8,128)}), f32[16,17,8,128]{3,2,1,0:T(8,128)S(1)}, u32[]{:S(2)}, u32[]{:S(2)}) async-start(f32[16,17,8,128]{3,2,1,0:T(8,128)} %copy-done.1), calls=%async_computation | async-start | bytes 2228224 | tf_op jit(solution)/shard_map/all_to_all | solution.py:343
  32.4 26.1 %all-to-all-done.lines = f32[16,17,8,128]{3,2,1,0:T(8,128)S(1)} async-done(((f32[16,17,8,128]{3,2,1,0:T(8,128)}), f32[16,17,8,128]{3,2,1,0:T(8,128)S(1)}, u32[]{:S(2)}, u32[]{:S(2)}) %all-to-all-start) | async-done | bytes 1114144 | tf_op jit(solution)/shard_map/all_to_all | solution.py:343
  58.5 1.9 %solve_across.1 = (f32[5,32,8,128]{3,2,1,0:T(8,128)S(1)}, f32[5,8,8,128]{3,2,1,0:T(8,128)}, f32[5,8,8,128]{3,2,1,0:T(8,128)}, f32[2,5,64,128]{3,2,1,0:T(8,128)S(1)}) custom-call(s32[1]{0:T(128)} %bitcast.core, f32[16,17,8,128]{3,2,1,0:T(8,128)S(1)} %all-to-all-done.lines, f32[5,256,256]{2,1,0:T(8,128)S(1)} %get-tuple-element.16.solve_x, ...), custom_call_target="tpu_custom_call" | custom-call | flops 100000000 | bytes 4000000 | tf_op jit(solution)/shard_map/solve_across/pallas_call | solution.py:345
  62.0 1.9 %collective-permute-start.1 = (f32[5,8,8,128]{3,2,1,0:T(8,128)}, f32[5,8,8,128]{3,2,1,0:T(8,128)}, u32[]{:S(2)}, u32[]{:S(2)}) collective-permute-start(f32[5,8,8,128]{3,2,1,0:T(8,128)} %get-tuple-element.18), channel_id=1, source_target_pairs={{0,1},{1,4},{4,5},{5,8},{8,9},{9,12},{12,13},{2,3},{3,6},{6,7},{7,... | collective-permute-start | bytes 491528 | tf_op jit(solution)/shard_map/ppermute | solution.py:361
  63.9 3.6 %collective-permute-start.2 = (f32[5,8,8,128]{3,2,1,0:T(8,128)}, f32[5,8,8,128]{3,2,1,0:T(8,128)}, u32[]{:S(2)}, u32[]{:S(2)}) collective-permute-start(f32[5,8,8,128]{3,2,1,0:T(8,128)} %get-tuple-element.19), channel_id=1, source_target_pairs={{1,0},{4,1},{5,4},{8,5},{9,8},{12,9},{13,12},{3,2},{6,3},{7,6},{10... | collective-permute-start | bytes 491528 | tf_op jit(solution)/shard_map/ppermute | solution.py:362
  67.8 1.1 collective-permute-done.1.from_prev
  68.9 1.8 %collective-permute-done.2.from_next = f32[5,8,8,128]{3,2,1,0:T(8,128)} collective-permute-done((f32[5,8,8,128]{3,2,1,0:T(8,128)}, f32[5,8,8,128]{3,2,1,0:T(8,128)}, u32[]{:S(2)}, u32[]{:S(2)}) %collective-permute-start.2) | collective-permute-done | bytes 163872 | tf_op jit(solution)/shard_map/ppermute | solution.py:362
  70.7 1.1 copy-done.6
  72.8 3.9 %second_residual.1 = f32[16,15,8,128]{3,2,1,0:T(8,128)S(1)} custom-call(f32[5,3]{1,0:T(8,128)S(1)} %bitcast.14, f32[2]{0:T(128)S(1)} %add_convert_fusion.inner, f32[5,5]{1,0:T(8,128)S(1)} %get-tuple-element.27.both, f32[5,5]{1,0:T(8,128)S(1)} %get-tuple-element.26.both_lap, f32[5,32,8,128]{3,2,1,0:T(8,128)S(1)} %copy-done.6, ...), custom_call_target="tpu_custom_call" | custom-call | flops 300000000 | bytes 4000000 | tf_op jit(solution)/shard_map/second_residual/pallas_call | solution.py:370
  77.6 4.2 %all-to-all-start.1 = ((f32[16,15,8,128]{3,2,1,0:T(8,128)}), f32[16,15,8,128]{3,2,1,0:T(8,128)S(1)}, u32[]{:S(2)}, u32[]{:S(2)}) async-start(f32[16,15,8,128]{3,2,1,0:T(8,128)} %copy-done.2), calls=%async_computation.1 | async-start | bytes 1966080 | tf_op jit(solution)/shard_map/all_to_all | solution.py:379
  81.9 7.0 %collective-permute-start.4 = (f32[2,5,64,128]{3,2,1,0:T(8,128)S(1)}, f32[2,5,64,128]{3,2,1,0:T(8,128)S(1)}, u32[]{:S(2)}, u32[]{:S(2)}) collective-permute-start(f32[2,5,64,128]{3,2,1,0:T(8,128)S(1)} %copy-done.12), channel_id=1, source_target_pairs={{1,2},{3,4},{5,6},{7,8},{9,10},{11,12},{13,14},{2,1},{4,3},{6,5},{... | collective-permute-start | bytes 983048 | tf_op jit(solution)/shard_map/ppermute | solution.py:363
  89.0 10.6 %all-to-all-done.1.solved = f32[16,15,8,128]{3,2,1,0:T(8,128)S(1)} async-done(((f32[16,15,8,128]{3,2,1,0:T(8,128)}), f32[16,15,8,128]{3,2,1,0:T(8,128)S(1)}, u32[]{:S(2)}, u32[]{:S(2)}) %all-to-all-start.1) | async-done | bytes 983072 | tf_op jit(solution)/shard_map/all_to_all | solution.py:379
  99.6 2.3 %update.1 = (f32[2,5,2,64,128]{4,3,2,1,0:T(8,128)}, f32[2,5,64,128]{3,2,1,0:T(8,128)S(1)}) custom-call(s32[1]{0:T(128)} %bitcast.core, f32[2,5,5]{2,1,0:T(8,128)S(1)} %copy.50.right, f32[2,5,2,64,128]{4,3,2,1,0:T(8,128)S(1)} %copy-done, f32[16,15,8,128]{3,2,1,0:T(8,128)S(1)} %all-to-all-done.1.solved, f32[2,5,64,64]{3,2,1,0:T(8,128)S(1)} %get-tuple-element.15.solve_y), custom_call_target="tpu_custom_call" | custom-call | flops 60000000 | bytes 4000000 | tf_op jit(solution)/shard_map/update/pallas_call | solution.py:381
  101.9 1.9 %collective-permute-start.3 = (f32[2,5,64,128]{3,2,1,0:T(8,128)S(1)}, f32[2,5,64,128]{3,2,1,0:T(8,128)S(1)}, u32[]{:S(2)}, u32[]{:S(2)}) collective-permute-start(f32[2,5,64,128]{3,2,1,0:T(8,128)S(1)} %get-tuple-element.22), channel_id=1, source_target_pairs={{0,1},{1,0},{2,3},{3,2},{4,5},{5,4},{6,7},{7,6},{8,9},{9,8},{10,11... | collective-permute-start | bytes 983048 | tf_op jit(solution)/shard_map/ppermute | solution.py:390
  103.8 15.8 %collective-permute-done.4.start_outer = f32[2,5,64,128]{3,2,1,0:T(8,128)S(1)} collective-permute-done((f32[2,5,64,128]{3,2,1,0:T(8,128)S(1)}, f32[2,5,64,128]{3,2,1,0:T(8,128)S(1)}, u32[]{:S(2)}, u32[]{:S(2)}) %collective-permute-start.4) | collective-permute-done | bytes 327712 | tf_op jit(solution)/shard_map/ppermute | solution.py:363
  119.7 1.1 copy-done.3
  120.8 1.4 inside_terms.1
  123.0 28.4 %all_to_all.20.pieces = f32[32,16,128]{2,1,0:T(8,128)S(1)} all-to-all(f32[32,16,128]{2,1,0:T(8,128)S(1)} %terms.1), channel_id=1, replica_groups=mesh['cond'=32,'grid'=16] {'cond'}, dimensions={0} | all-to-all | bytes 524288 | tf_op jit(solution)/shard_map/all_to_all | solution.py:410
  151.4 16.5 %all_to_all.21 = f32[32,16,128]{2,1,0:T(8,128)S(1)} all-to-all(f32[32,16,128]{2,1,0:T(8,128)S(1)} %sum_conditions.1), channel_id=1, replica_groups=mesh['cond'=32,'grid'=16] {'cond'}, dimensions={0} | all-to-all | bytes 524288 | tf_op jit(solution)/shard_map/all_to_all | solution.py:419
  (63 shorter events, 15.4 us)
Async XLA Ops:
  0.6 15.5 %copy-start = (f32[2,5,2,64,128]{4,3,2,1,0:T(8,128)S(1)}, f32[2,5,2,64,128]{4,3,2,1,0:T(8,128)}, u32[]{:S(2)}) copy-start(f32[2,5,2,64,128]{4,3,2,1,0:T(8,128)} %adjoint.5) | copy-start | bytes 1966084
  0.6 15.5 %copy-start.9 = (f32[2,64,128]{2,1,0:T(8,128)S(1)}, f32[2,64,128]{2,1,0:T(8,128)}, u32[]{:S(2)}) copy-start(f32[2,64,128]{2,1,0:T(8,128)} %radius.1) | copy-start | bytes 196612
  2.5 13.6 %collective-permute-start = (f32[2,5,64,128]{3,2,1,0:T(8,128)}, f32[2,5,64,128]{3,2,1,0:T(8,128)}, u32[]{:S(2)}, u32[]{:S(2)}) collective-permute-start(f32[2,5,64,128]{3,2,1,0:T(8,128)} %dynamic-slice_bitcast_fusion), channel_id=1, source_target_pairs={{0,1},{1,0},{2,3},{3,2},{4,5},{5,4},{6,7},{7,6},{8,9},{9,8},{10,11... | collective-permute-start | bytes 983048 | tf_op jit(solution)/shard_map/ppermute | solution.py:308
  8.2 0.9 copy-start.13
  9.1 0.8 copy-start.14
  16.1 4.9 %copy-start.7 = (f32[5,128,128]{2,1,0:T(8,128)}, f32[5,128,128]{2,1,0:T(8,128)S(1)}, u32[]{:S(2)}) copy-start(f32[5,128,128]{2,1,0:T(8,128)S(1)} %get-tuple-element.20.solve_z) | copy-start | bytes 983044
  16.1 1.2 copy-start.4
  20.9 1.0 copy-start.1
  21.9 10.4 %copy-start.21 = (f32[2,5,5]{2,0,1:T(2,128)S(1)}, f32[2,5,5]{2,0,1:T(2,128)}, u32[]{:S(2)}) copy-start(f32[2,5,5]{2,0,1:T(2,128)} %param.21) | copy-start | bytes 604
  21.9 10.4 %copy-start.20 = (f32[2,5,3]{1,0,2:T(2,128)S(1)}, f32[2,5,3]{1,0,2:T(2,128)}, u32[]{:S(2)}) copy-start(f32[2,5,3]{1,0,2:T(2,128)} %param.22) | copy-start | bytes 364
  21.9 36.5 %all-to-all-start = ((f32[16,17,8,128]{3,2,1,0:T(8,128)}), f32[16,17,8,128]{3,2,1,0:T(8,128)S(1)}, u32[]{:S(2)}, u32[]{:S(2)}) async-start(f32[16,17,8,128]{3,2,1,0:T(8,128)} %copy-done.1), calls=%async_computation | async-start | bytes 2228224 | tf_op jit(solution)/shard_map/all_to_all | solution.py:343
  60.4 0.8 copy-start.5
  62.0 6.9 %collective-permute-start.1 = (f32[5,8,8,128]{3,2,1,0:T(8,128)}, f32[5,8,8,128]{3,2,1,0:T(8,128)}, u32[]{:S(2)}, u32[]{:S(2)}) collective-permute-start(f32[5,8,8,128]{3,2,1,0:T(8,128)} %get-tuple-element.18), channel_id=1, source_target_pairs={{0,1},{1,4},{4,5},{5,8},{8,9},{9,12},{12,13},{2,3},{3,6},{6,7},{7,... | collective-permute-start | bytes 491528 | tf_op jit(solution)/shard_map/ppermute | solution.py:361
  63.9 6.8 %collective-permute-start.2 = (f32[5,8,8,128]{3,2,1,0:T(8,128)}, f32[5,8,8,128]{3,2,1,0:T(8,128)}, u32[]{:S(2)}, u32[]{:S(2)}) collective-permute-start(f32[5,8,8,128]{3,2,1,0:T(8,128)} %get-tuple-element.19), channel_id=1, source_target_pairs={{1,0},{4,1},{5,4},{8,5},{9,8},{12,9},{13,12},{3,2},{6,3},{7,6},{10... | collective-permute-start | bytes 491528 | tf_op jit(solution)/shard_map/ppermute | solution.py:362
  70.7 1.1 copy-start.6
  71.8 1.0 copy-start.8
  76.7 1.0 copy-start.2
  77.6 4.3 %copy-start.12 = (f32[2,5,64,128]{3,2,1,0:T(8,128)S(1)}, f32[2,5,64,128]{3,2,1,0:T(8,128)}, u32[]{:S(2)}) copy-start(f32[2,5,64,128]{3,2,1,0:T(8,128)} %copy-done.11) | copy-start | bytes 983044
  77.6 22.0 %all-to-all-start.1 = ((f32[16,15,8,128]{3,2,1,0:T(8,128)}), f32[16,15,8,128]{3,2,1,0:T(8,128)S(1)}, u32[]{:S(2)}, u32[]{:S(2)}) async-start(f32[16,15,8,128]{3,2,1,0:T(8,128)} %copy-done.2), calls=%async_computation.1 | async-start | bytes 1966080 | tf_op jit(solution)/shard_map/all_to_all | solution.py:379
  81.9 21.9 %copy-start.22 = (f32[2,3,5]{2,0,1:T(2,128)S(1)}, f32[2,3,5]{2,0,1:T(2,128)}, u32[]{:S(2)}) copy-start(f32[2,3,5]{2,0,1:T(2,128)} %param.23) | copy-start | bytes 364
  81.9 37.8 %copy-start.10 = (s32[2]{0:T(128)S(1)}, s32[2]{0:T(128)}, u32[]{:S(2)}) copy-start(s32[2]{0:T(128)} %weights.3) | copy-start | bytes 28
  81.9 37.8 %collective-permute-start.4 = (f32[2,5,64,128]{3,2,1,0:T(8,128)S(1)}, f32[2,5,64,128]{3,2,1,0:T(8,128)S(1)}, u32[]{:S(2)}, u32[]{:S(2)}) collective-permute-start(f32[2,5,64,128]{3,2,1,0:T(8,128)S(1)} %copy-done.12), channel_id=1, source_target_pairs={{1,2},{3,4},{5,6},{7,8},{9,10},{11,12},{13,14},{2,1},{4,3},{6,5},{... | collective-permute-start | bytes 983048 | tf_op jit(solution)/shard_map/ppermute | solution.py:363
  101.9 20.3 %collective-permute-start.3 = (f32[2,5,64,128]{3,2,1,0:T(8,128)S(1)}, f32[2,5,64,128]{3,2,1,0:T(8,128)S(1)}, u32[]{:S(2)}, u32[]{:S(2)}) collective-permute-start(f32[2,5,64,128]{3,2,1,0:T(8,128)S(1)} %get-tuple-element.22), channel_id=1, source_target_pairs={{0,1},{1,0},{2,3},{3,2},{4,5},{5,4},{6,7},{7,6},{8,9},{9,8},{10,11... | collective-permute-start | bytes 983048 | tf_op jit(solution)/shard_map/ppermute | solution.py:390
  119.7 1.1 copy-start.3
  (6 other events, 4.2 us)

commit v3 on v2

v3 whole, which is shorter than its diff:
```python
import functools
import math

import jax
import jax.numpy as jnp
import numpy as np
from jax import lax
from jax.experimental import pallas as pl
from jax.experimental.pallas import tpu as pltpu
from jax.sharding import PartitionSpec as P

F32 = jnp.float32
FIELDS = 5
VMEM = pl.BlockSpec(memory_space=pltpu.VMEM)
SMEM = pl.BlockSpec(memory_space=pltpu.SMEM)
LIMIT = 20 * 1024 * 1024
ANY = pl.BlockSpec(memory_space=pl.ANY)
COUP, LEFT, RIGHT, RATE, SENS = 0, 5, 10, 15, 18


def split(v):
    high = v.astype(jnp.bfloat16)
    return high, (v - high.astype(F32)).astype(jnp.bfloat16)


def dot(a, b):
    one = functools.partial(jnp.dot, preferred_element_type=F32)
    (a_high, a_low), (b_high, b_low) = split(a), split(b)
    return one(a_high, b_high) + (one(a_high, b_low) + one(a_low, b_high))


def exact(a, b):
    return jnp.dot(a, b, precision=lax.Precision.HIGHEST, preferred_element_type=F32)


def sine_tables(length):
    counter = np.arange(1, length + 1, dtype=np.float64)
    sine = math.sqrt(2.0 / (length + 1)) * np.sin(
        counter[:, None] * counter[None, :] * (math.pi / (length + 1))
    )
    spectrum = 2.0 - 2.0 * np.cos(counter * (math.pi / (length + 1)))
    return sine.astype(np.float32), (spectrum + spectrum * spectrum).astype(np.float32)


def call(kernel, outs, in_specs, flops, name, scratch=(), out_specs=None):
    return pl.pallas_call(
        kernel,
        out_shape=outs,
        in_specs=in_specs,
        out_specs=out_specs or jax.tree.map(lambda _: VMEM, outs),
        scratch_shapes=list(scratch),
        compiler_params=pltpu.CompilerParams(vmem_limit_bytes=LIMIT),
        cost_estimate=pl.CostEstimate(flops=flops, bytes_accessed=4_000_000, transcendentals=0),
        name=name,
    )


def shape(*dims):
    return jax.ShapeDtypeStruct(dims, F32)


def vmem(*dims):
    return pltpu.VMEM(dims, F32)


def fetch(sources, targets, sems):
    copies = [pltpu.make_async_copy(a, b, sems.at[i]) for i, (a, b) in enumerate(zip(sources, targets))]
    for copy in copies:
        copy.start()
    return copies


def shifted(v, axis, step):
    size = v.shape[axis]
    rolled = pltpu.roll(v, (-step) % size, axis)
    at = lax.broadcasted_iota(jnp.int32, v.shape, axis)
    return jnp.where(at == (size - 1 if step > 0 else 0), 0.0, rolled)


def mixed(weight, values):
    total = weight(0) * values[0]
    for g in range(1, FIELDS):
        total = total + weight(g) * values[g]
    return total


def spot(c, b):
    return (b // 2) * 4 + c * 2 + b % 2


def tables_kernel(pack, sine_z_in, sine_y_in, spec_in, solve_z, solve_y, sine_z, sine_y, spec, sems):
    for copy in fetch((sine_z_in, sine_y_in, spec_in), (sine_z, sine_y, spec), sems):
        copy.wait()
    ny = sine_y.shape[0]
    for c in range(2):
        for f in range(FIELDS):
            denom = 1.0 + pack[c, f, RATE + 2] * spec[0:1]
            solve_z[c, f] = exact(sine_z[...] / denom, sine_z[...])
            denom = 1.0 + pack[c, f, RATE + 1] * spec[1:2, :ny]
            solve_y[c, f] = exact(sine_y[...] / denom, sine_y[...])


def tables_y_kernel(pack, token, sine_y_in, spec_in, solve_y, sine_y, spec, sems):
    for copy in fetch((sine_y_in, spec_in), (sine_y, spec), sems):
        copy.wait()
    ny = sine_y.shape[0]
    for c in range(2):
        for f in range(FIELDS):
            denom = 1.0 + pack[c, f, RATE + 1] * spec[1:2, :ny]
            solve_y[c, f] = exact(sine_y[...] / denom, sine_y[...])


def tables_b_kernel(info, pack, token, sine_z_in, left_in, right_in, right_2_in, spec_in,
                    solve_x, ends_prev, ends_next, halo_prev, halo_next, solve_z, mixes,
                    sine_z, left, right, right_2, spec, sems):
    copies = fetch(
        (sine_z_in, left_in, right_in, right_2_in, spec_in), (sine_z, left, right, right_2, spec), sems
    )
    mine = info[1]
    for f in range(FIELDS):
        for g in range(FIELDS):
            near, far = 0.0, 0.0
            for h in range(FIELDS):
                near = near + pack[mine, f, LEFT + h] * pack[mine, h, RIGHT + g]
                inner = 0.0
                for i in range(FIELDS):
                    inner = inner + pack[mine, h, COUP + i] * pack[mine, i, RIGHT + g]
                far = far + pack[mine, f, LEFT + h] * inner
            mixes[0, f, g] = near
            mixes[1, f, g] = far
        mixes[2, f, 0] = pack[mine, f, RATE + 1]
    for copy in copies:
        copy.wait()
    n, nx = left.shape
    row, col = (lax.broadcasted_iota(jnp.int32, (n, n), i) for i in range(2))
    same = (row & 7) == (col & 7)
    row, col = (lax.broadcasted_iota(jnp.int32, (2 * nx, n), i) for i in range(2))
    prev_rows = (row & 1) == (col & 7)
    next_rows = (row & 1) + 6 == (col & 7)
    row, col = (lax.broadcasted_iota(jnp.int32, (2 * nx, 2 * nx), i) for i in range(2))
    from_last = ((row & 1) == 0) & ((col & 1) == 1)
    from_first = ((row & 1) == 1) & ((col & 1) == 0)
    for f in range(FIELDS):
        denom = 1.0 + pack[mine, f, RATE] * spec[2:3, :nx]
        scaled = left[...] / denom
        solve_x[f] = jnp.where(same, exact(scaled, right[...]), 0.0)
        scaled_2 = right_2[...].T / denom
        both = exact(scaled_2, right[...])
        ends_prev[f] = jnp.where(prev_rows, both, 0.0)
        ends_next[f] = jnp.where(next_rows, both, 0.0)
        both = exact(scaled_2, right_2[...])
        halo_prev[f] = jnp.where(from_last, both, 0.0)
        halo_next[f] = jnp.where(from_first, both, 0.0)
        denom = 1.0 + pack[mine, f, RATE + 2] * spec[0:1]
        solve_z[f] = exact(sine_z[...] / denom, sine_z[...])


def first_kernel(info, pack, adjoint, other, source_in, radius, solve_z, solve_y, out, token,
                 source, made, lapped, stage, sems, out_sems):
    copies = fetch([source_in.at[c] for c in range(2)], [source.at[c] for c in range(2)], sems)
    ny = adjoint.shape[3]
    blocks = ny // 8
    me = info[0]
    before, after = me.astype(F32), (1 - me).astype(F32)
    token[...] = jnp.zeros(token.shape, F32)
    stores = []
    for c in range(2):
        residual = {}
        for x in range(2):
            for f in range(FIELDS):
                v = adjoint[c, f, x]
                beside = adjoint[c, f, 1 - x]
                beside = beside + (other[c, f, 1] * before if x == 0 else other[c, f, 0] * after)
                beside = beside + shifted(v, 0, 1) + shifted(v, 0, -1)
                beside = beside + shifted(v, 1, 1) + shifted(v, 1, -1)
                lapped[x, f] = 6.0 * v - beside
        copies[c].wait()
        for x in range(2):
            sr = radius[x]
            residual = []
            for f in range(FIELDS):
                r = source[c, f, x] - sr * adjoint[c, f, x]
                for g in range(FIELDS):
                    r = r - pack[c, f, COUP + g] * lapped[x, g]
                residual.append(r)
            for f in range(FIELDS):
                stage[f, x * ny : x * ny + ny] = mixed(lambda g: pack[c, f, LEFT + g], residual)
        outer = [adjoint[c, g, me] for g in range(FIELDS)]
        outer = [mixed(lambda g: pack[c, f, COUP + g], outer) for f in range(FIELDS)]
        for f in range(FIELDS):
            stage[f, 2 * ny : 3 * ny] = mixed(lambda g: pack[c, f, LEFT + g], outer)
        for f in range(FIELDS):
            r = dot(stage[f], solve_z[c, f])
            r = jnp.concatenate([r[p * ny : p * ny + ny] for p in range(3)], axis=1)
            r = dot(solve_y[c, f], r)
            for p in range(3):
                for b in range(blocks):
                    made[b // 2, c, b % 2, 3 * f + p] = r[8 * b : 8 * b + 8, 128 * p : 128 * p + 128]
        for x in range(2):
            for b in range(blocks):
                made[b // 2, c, b % 2, 3 * FIELDS + x] = radius[x, 8 * b : 8 * b + 8]
        stores.append(pltpu.make_async_copy(made.at[:, c], out.at[:, c], out_sems.at[c]))
        stores[-1].start()
    for copy in stores:
        copy.wait()


def assembled(lines, f):
    zero = jnp.zeros((1, 8, 128), F32)
    w = lines[:, 3 * f : 3 * f + 3].reshape(lines.shape[0] // 2, 6, 8, 128)
    plane_0 = w[:, 0] + jnp.concatenate([zero, w[:-1, 5]], axis=0)
    plane_3 = w[:, 4] + jnp.concatenate([w[1:, 2], zero], axis=0)
    return jnp.stack([plane_0, w[:, 1], w[:, 3], plane_3], axis=1)


def ends_kernel(lines, ends_prev, ends_next, to_prev, to_next):
    for f in range(FIELDS):
        w = assembled(lines, f).reshape(-1, 128)
        to_prev[f] = dot(ends_prev[f], w)
        to_next[f] = dot(ends_next[f], w)


def second_kernel(info, mixes, lines, solve_x, solve_z, out, solved, lapped, kept):
    nx = out.shape[1]
    full = (nx, 8, 128)
    row = lax.broadcasted_iota(jnp.int32, full, 1)
    has_prev, has_next = info[2].astype(F32), info[3].astype(F32)
    zero = jnp.zeros((1, 8, 128), F32)
    for f in range(FIELDS):
        u = dot(solve_x[f], assembled(lines, f).reshape(nx * 8, 128)).reshape(full)
        solved[f] = u
        up = jnp.where(row == 7, 0.0, pltpu.roll(u, 7, 1))
        down = jnp.where(row == 0, 0.0, pltpu.roll(u, 1, 1))
        ku = 2.0 * u - up - down
        k_up = jnp.where(row == 7, -has_next * u, pltpu.roll(ku, 7, 1))
        k_down = jnp.where(row == 0, -has_prev * u, pltpu.roll(ku, 1, 1))
        kku = 2.0 * ku - k_up - k_down
        kept[f] = 2.0 * (u + mixes[2, f, 0] * (ku + kku))
        beside = jnp.concatenate([zero, u[:-1]], axis=0) + jnp.concatenate([u[1:], zero], axis=0)
        flat = u.reshape(nx * 8, 128)
        beside = beside + (shifted(flat, 1, 1) + shifted(flat, 1, -1)).reshape(full)
        lapped[f] = 4.0 * u + ku - beside
    sr = lines[:, 3 * FIELDS :].reshape(full)
    for f in range(FIELDS):
        near = mixed(lambda g: mixes[0, f, g], solved)
        far = mixed(lambda g: mixes[1, f, g], lapped)
        v = (sr * near + far).reshape(nx * 8, 128)
        v = dot(solve_x[f], dot(v, solve_z[f]))
        out[f] = kept[f] - v.reshape(full)


def halo_kernel(mixes, local, from_prev, from_next, halo_prev, halo_next, solve_z, out, token, made, sems):
    nx = local.shape[1]
    full = (nx, 8, 128)
    row = lax.broadcasted_iota(jnp.int32, full, 1)
    odd = (lax.broadcasted_iota(jnp.int32, (2 * nx, 128), 0) & 1) == 1
    zero = jnp.zeros((1, 8, 128), F32)
    token[...] = jnp.zeros(token.shape, F32)
    stores = []
    for f in range(FIELDS):
        first, last = from_prev[f], from_next[f]
        far = jnp.concatenate(
            [mixed(lambda g: mixes[1, f, g], from_prev), mixed(lambda g: mixes[1, f, g], from_next)], axis=0
        )
        far = dot(far, solve_z[f])
        far_prev, far_next = far[: 2 * nx], far[2 * nx :]
        scale = 2.0 * mixes[2, f, 0]
        add_prev = jnp.where(odd, first, first - 5.0 * pltpu.roll(first, 2 * nx - 1, 0))
        add_next = jnp.where(odd, last - 5.0 * pltpu.roll(last, 1, 0), last)
        add_prev = scale * add_prev + dot(halo_prev[f], far_prev)
        add_next = scale * add_next + dot(halo_next[f], far_next)
        spread = lambda v, at: jnp.stack(
            [pltpu.roll(v.reshape(nx // 4, 8, 128), (at - 2 * j) % 8, 1) for j in range(4)], axis=1
        ).reshape(full)
        q = local[f] + jnp.where(
            row < 2, spread(add_prev, 0), jnp.where(row >= 6, spread(add_next, 6), 0.0)
        )
        chips = q.reshape(nx // 4, 4, 8, 128)
        outer_0 = jnp.concatenate([zero, chips[:-1, 3]], axis=0)
        outer_1 = jnp.concatenate([chips[1:, 0], zero], axis=0)
        made[:, 3 * f : 3 * f + 3] = jnp.stack(
            [chips[:, 0], chips[:, 1], outer_0, chips[:, 2], chips[:, 3], outer_1], axis=1
        ).reshape(nx // 2, 3, 8, 128)
        part = pl.ds(3 * f, 3)
        stores.append(pltpu.make_async_copy(made.at[:, part], out.at[:, part], sems.at[f]))
        stores[-1].start()
    for copy in stores:
        copy.wait()


def gathered(solved, c, tile, blocks):
    return jnp.concatenate([solved[spot(c, b), tile] for b in range(blocks)], axis=0)


def update_kernel(info, pack, adjoint, solved, solve_y, out, inner, step):
    ny = adjoint.shape[3]
    me = info[0]
    for c in range(2):
        for f in range(FIELDS):
            q = jnp.concatenate([gathered(solved, c, 3 * f + x, ny // 8) for x in range(2)], axis=1)
            step[f] = dot(solve_y[c, f], q)
        steps = [[step[g, :, 128 * x : 128 * x + 128] for g in range(FIELDS)] for x in range(2)]
        for f in range(FIELDS):
            planes = [
                adjoint[c, f, x] + mixed(lambda g: pack[c, f, RIGHT + g], steps[x]) for x in range(2)
            ]
            for x in range(2):
                out[c, f, x] = planes[x]
            inner[c, f] = jnp.where(me == 0, planes[1], planes[0])


def inside_kernel(info, pack, adjoint, start_outer, solved, solve_y, terms, step):
    ny = adjoint.shape[3]
    me = info[0]
    totals = [[0.0, 0.0] for _ in range(3)]
    for c in range(2):
        for f in range(FIELDS):
            step[f] = dot(solve_y[c, f], gathered(solved, c, 3 * f + 2, ny // 8))
        for f in range(FIELDS):
            outer = start_outer[c, f] + mixed(lambda g: pack[c, f, RIGHT + g], step)
            w = [pack[c, f, SENS + k] for k in range(3)]
            v = [adjoint[c, f, x] for x in range(2)]
            pair = v[0] * v[1]
            edge = jnp.where(me == 0, v[0], v[1]) * outer
            at_0, at_1 = jnp.where(me == 0, edge, 0.0), jnp.where(me == 0, 0.0, edge)
            totals[0][0] += w[0] * (pair - at_0)
            totals[0][1] += w[0] * (at_1 - pair)
            for x in range(2):
                for k in range(2):
                    totals[k + 1][x] += w[k + 1] * (v[x] * (shifted(v[x], k, 1) - shifted(v[x], k, -1)))
    for k in range(3):
        for x in range(2):
            terms[k, x] = totals[k][x]


def terms_kernel(info, pack, mine, other, inside, out):
    me = info[0]
    ny = mine.shape[2]
    each = out.shape[1] // 8

    def store(k, x, v):
        for i in range(ny // 8):
            piece, at = divmod((k * 2 + x) * (ny // 8) + i, each)
            out[piece, 8 * at : 8 * at + 8] = v[8 * i : 8 * i + 8]

    total = 0.0
    for c in range(2):
        for f in range(FIELDS):
            total += pack[c, f, SENS] * (mine[c, f] * other[c, f])
    store(0, 0, inside[0, 0] - jnp.where(me == 0, 0.0, total))
    store(0, 1, inside[0, 1] + jnp.where(me == 0, total, 0.0))
    for k in range(1, 3):
        for x in range(2):
            store(k, x, inside[k, x])
    for tile in range(6 * ny // 8, out.shape[0] * each):
        piece, at = divmod(tile, each)
        out[piece, 8 * at : 8 * at + 8] = jnp.zeros((8, out.shape[2]), F32)


def sum_kernel(scale, pieces, out):
    total = pieces[0]
    for i in range(1, pieces.shape[0]):
        total = total + pieces[i]
    total = total * scale
    for i in range(out.shape[0]):
        out[i] = total


def body(
    adjoint_source,
    adjoint_start,
    spectral_radius,
    coupling,
    left_vectors,
    right_vectors,
    implicit_scales,
    sensitivity_map,
    condition_weights,
):
    peers = lax.axis_size("grid")
    conds = lax.axis_size("cond")
    _, fields, planes, ny, nz = adjoint_start.shape
    nx = peers * planes
    rows_b = nx * 8
    blocks = peers // 2
    sems = lambda n: pltpu.SemaphoreType.DMA((n,))

    me = lax.axis_index("grid")
    core = me % 2
    side = (me // 2) % 2
    place = (me // 4) * 2 + core
    info = jnp.stack([core, side, place > 0, place < blocks - 1]).astype(jnp.int32)

    cores = [(i, i ^ 1) for i in range(peers)]
    chips = [(i, i + 1) for i in range(1, peers - 1, 2)]
    chips = chips + [(j, i) for i, j in chips]
    other = lax.ppermute(adjoint_start, "grid", cores)
    outer = lax.dynamic_index_in_dim(adjoint_start, core, 2, keepdims=False)
    outer = lax.ppermute(outer, "grid", chips)

    sine_z, spec_z = sine_tables(nz)
    sine_y, spec_y = sine_tables(ny)
    sine_x, spec_x = sine_tables(nx)
    spec = np.zeros((8, nz), np.float32)
    spec[0], spec[1, :ny], spec[2, :nx] = spec_z, spec_y, spec_x
    left_x = np.repeat(sine_x, 8, axis=0)
    right_2 = np.repeat(sine_x, 2, axis=0).T.copy()
    spec, sine_z, sine_y = jnp.asarray(spec), jnp.asarray(sine_z), jnp.asarray(sine_y)

    weights = condition_weights.astype(F32)[:, None, None]
    pack = jnp.concatenate(
        [
            coupling,
            left_vectors,
            right_vectors,
            implicit_scales,
            jnp.swapaxes(sensitivity_map, 1, 2) * weights,
        ],
        axis=2,
    )

    solve_z, solve_y = call(
        tables_kernel,
        (shape(2, fields, nz, nz), shape(2, fields, ny, ny)),
        [SMEM, ANY, ANY, ANY],
        100_000_000,
        "solve_tables",
        [vmem(nz, nz), vmem(ny, ny), vmem(8, nz), sems(3)],
    )(pack, sine_z, sine_y, spec)

    lines, token = call(
        first_kernel,
        (shape(blocks // 2, 2, 2, 3 * fields + planes, 8, nz), shape(8, nz)),
        [SMEM, SMEM, VMEM, VMEM, ANY, VMEM, VMEM, VMEM],
        200_000_000,
        "first_residual",
        [
            vmem(2, fields, planes, ny, nz),
            vmem(blocks // 2, 2, 2, 3 * fields + planes, 8, nz),
            vmem(planes, fields, ny, nz),
            vmem(fields, 3 * ny, nz),
            sems(2),
            sems(2),
        ],
        (ANY, VMEM),
    )(info, pack, adjoint_start, other, adjoint_source, spectral_radius, solve_z, solve_y)

    lines = lines.reshape(peers, 3 * fields + planes, 8, nz)
    lines = lax.all_to_all(lines, "grid", 0, 0, tiled=True)

    solve_x, ends_prev, ends_next, halo_prev, halo_next, solve_zb, mixes = call(
        tables_b_kernel,
        (
            shape(fields, rows_b, rows_b),
            shape(fields, 2 * nx, rows_b),
            shape(fields, 2 * nx, rows_b),
            shape(fields, 2 * nx, 2 * nx),
            shape(fields, 2 * nx, 2 * nx),
            shape(fields, nz, nz),
            shape(3, fields, fields),
        ),
        [SMEM, SMEM, VMEM] + [ANY] * 5,
        100_000_000,
        "tables_b",
        [vmem(nz, nz), vmem(rows_b, nx), vmem(nx, rows_b), vmem(nx, 2 * nx), vmem(8, nz), sems(5)],
        (VMEM,) * 6 + (SMEM,),
    )(info, pack, token, sine_z, jnp.asarray(left_x), jnp.asarray(left_x.T.copy()), jnp.asarray(right_2), spec)

    to_prev, to_next = call(
        ends_kernel,
        (shape(fields, 2 * nx, nz), shape(fields, 2 * nx, nz)),
        [VMEM] * 3,
        50_000_000,
        "solve_ends",
    )(lines, ends_prev, ends_next)

    up = [(spot(s, b), spot(s, b + 1)) for s in range(2) for b in range(blocks - 1)]
    down = [(j, i) for i, j in up]
    from_prev = lax.ppermute(to_next, "grid", up)
    from_next = lax.ppermute(to_prev, "grid", down)

    local = call(
        second_kernel,
        shape(fields, nx, 8, nz),
        [SMEM, SMEM] + [VMEM] * 3,
        300_000_000,
        "second_residual",
        [vmem(fields, nx, 8, nz) for _ in range(3)],
    )(info, mixes, lines, solve_x, solve_zb)

    step, token = call(
        halo_kernel,
        (shape(peers, 3 * fields, 8, nz), shape(8, nz)),
        [SMEM] + [VMEM] * 6,
        50_000_000,
        "halo_rows",
        [vmem(peers, 3 * fields, 8, nz), sems(fields)],
        (ANY, VMEM),
    )(mixes, local, from_prev, from_next, halo_prev, halo_next, solve_zb)

    step = lax.all_to_all(step, "grid", 0, 0, tiled=True)

    solve_y = call(
        tables_y_kernel,
        shape(2, fields, ny, ny),
        [SMEM, VMEM, ANY, ANY],
        50_000_000,
        "tables_y",
        [vmem(ny, ny), vmem(8, nz), sems(2)],
    )(pack, token, sine_y, spec)

    adjoint, mine = call(
        update_kernel,
        (shape(2, fields, planes, ny, nz), shape(2, fields, ny, nz)),
        [SMEM, SMEM] + [VMEM] * 3,
        60_000_000,
        "update",
        [vmem(fields, ny, 2 * nz)],
    )(info, pack, adjoint_start, step, solve_y)

    other = lax.ppermute(mine, "grid", cores)

    inside = call(
        inside_kernel,
        shape(3, planes, ny, nz),
        [SMEM, SMEM] + [VMEM] * 4,
        60_000_000,
        "inside_terms",
        [vmem(fields, ny, nz)],
    )(info, pack, adjoint, outer, step, solve_y)

    tiles = 3 * planes * ny // 8
    each = -(-tiles // conds)
    pieces = call(
        terms_kernel,
        shape(conds, each * 8, nz),
        [SMEM, SMEM] + [VMEM] * 3,
        10_000_000,
        "terms",
    )(info, pack, mine, other, inside)
    pieces = lax.all_to_all(pieces, "cond", 0, 0, tiled=True)
    scale = 1.0 / (conds * condition_weights.shape[0])
    pieces = call(
        functools.partial(sum_kernel, scale),
        shape(conds, each * 8, nz),
        [VMEM],
        1_000_000,
        "sum_conditions",
    )(pieces)
    pieces = lax.all_to_all(pieces, "cond", 0, 0, tiled=True)
    total = pieces.reshape(conds * each * 8, nz)[: tiles * 8].reshape(3, planes, ny, nz)
    return (adjoint, total)


def solution(mesh):
    in_specs = (
        P("cond", None, "grid", None, None),
        P("cond", None, "grid", None, None),
        P("grid", None, None),
        P("cond", None, None),
        P("cond", None, None),
        P("cond", None, None),
        P("cond", None, None),
        P("cond", None, None),
        P("cond"),
    )
    out_specs = (P("cond", None, "grid", None, None), P(None, "grid", None, None))
    return jax.shard_map(body, mesh=mesh, in_specs=in_specs, out_specs=out_specs, check_vma=False)
```

time: 170 us -> 158 us (0.929)
  waiting for transfers between devices: 55.4 us -> 45 us
  local copies, waits for them, and re-layouts: 18.7 us -> 13.1 us
  Pallas kernels: 16.7 us -> 21.6 us
    all_to_all x1, waiting for transfers between devices: 26.1 us -> 19.3 us  [body(): lines = lax.all_to_all(lines, 'grid', 0, 0, tiled=True)]
    pallas_call x6 -> x9, Pallas kernels: 14.3 us -> 19.6 us  [the longest x1 4.55 us: body(): call(tables_b_kernel, (shape(fields, rows_b, rows_b), shape(fields, 2 * n...]
    unnamed x53 -> x41, local copies, waits for them, and re-layouts: 16.1 us -> 12.3 us
    squeeze x2 -> x1, local copies, waits for them, and re-layouts: 1.88 us -> 0.03 us  [body(): outer = lax.dynamic_index_in_dim(adjoint_start, core, 2, keepdims=False)]
    ppermute x1, waiting for transfers between devices: 1.76 us -> 0.01 us  [body(): from_next = lax.ppermute(to_prev, 'grid', down)]
  transfers between devices with their start and end apart: 7 -> 7, of which waited for: 5 -> 3; matrix products, arithmetic and copies ran while one was open for 2% -> 3% of each run, Pallas kernels for 4% -> 9%
where the time goes in v3:
time: 158 us; the launch traced here: 157 us
  waiting for transfers between devices  45 us (28%)
  blocking collectives  44.9 us (28%)
  starting transfers between devices  30.2 us (19%)
  Pallas kernels  21.6 us (14%)
  local copies, waits for them, and re-layouts  13.1 us (8%)
    all_to_all x2, blocking collectives, body(): pieces = lax.all_to_all(pieces, 'cond', 0, 0, tiled=True)  44.9 us
    all_to_all x1, waiting for transfers between devices, body(): lines = lax.all_to_all(lines, 'grid', 0, 0, tiled=True)  19.3 us
    ppermute x1, waiting for transfers between devices, body(): outer = lax.ppermute(outer, 'grid', chips)  16.2 us
    unnamed x41, local copies, waits for them, and re-layouts  12.3 us
    all_to_all x1, starting transfers between devices, body(): lines = lax.all_to_all(lines, 'grid', 0, 0, tiled=True)  10.4 us
    all_to_all x1, waiting for transfers between devices, body(): step = lax.all_to_all(step, 'grid', 0, 0, tiled=True)  9.47 us
    ppermute x1, starting transfers between devices, body(): outer = lax.ppermute(outer, 'grid', chips)  6.79 us
    pallas_call x1, Pallas kernels, body(): call(tables_b_kernel, (shape(fields, rows_b, rows_b), shape(fields, 2 * n...  4.55 us
  transfers between devices with their start and end apart: 7, of which 3 were waited for; matrix products, arithmetic and copies ran while one was open for 3% of the time, Pallas kernels for 9%

profile of v3, /device:TPU:2, one launch (start us, length us, event | category | flops | bytes accessed | tf_op | source)
XLA Modules:
  0.0 156.6 jit_solution(8797536227866734888)
XLA Ops:
  0.6 1.9 %collective-permute-start = (f32[2,5,2,64,128]{4,3,2,1,0:T(8,128)}, f32[2,5,2,64,128]{4,3,2,1,0:T(8,128)S(1)}, u32[]{:S(2)}, u32[]{:S(2)}) collective-permute-start(f32[2,5,2,64,128]{4,3,2,1,0:T(8,128)} %adjoint.3), channel_id=1, source_target_pairs={{0,1},{1,0},{2,3},{3,2},{4,5},{5,4},{6,7},{7,6},{8,9},{9,8},{10,11... | collective-permute-start | bytes 1966088 | tf_op jit(solution)/shard_map/ppermute | solution.py:397
  9.3 1.8 %solve_tables.1 = (f32[2,5,128,128]{3,2,1,0:T(8,128)S(1)}, f32[2,5,64,64]{3,2,1,0:T(8,128)S(1)}) custom-call(f32[2,5,21]{2,1,0:T(8,128)S(1)} %concatenate.3.pack, f32[128,128]{1,0:T(8,128)S(1)} %copy-done.14, f32[64,64]{1,0:T(8,128)S(1)} %copy-done.9, f32[8,128]{1,0:T(8,128)S(1)} %copy-done.11), custom_call_target="tpu_custom_call" | custom-call | flops 100000000 | bytes 4000000 | tf_op jit(solution)/shard_map/solve_tables/pallas_call | solution.py:422
  11.2 1.1 copy-done
  12.3 1.1 copy-done.2
  14.2 3.8 %first_residual.1 = (f32[4,2,2,17,8,128]{5,4,3,2,1,0:T(8,128)}, f32[8,128]{1,0:T(8,128)S(1)}) custom-call(s32[4]{0:T(128)S(1)} %pad_add_fusion.info, f32[2,5,21]{2,1,0:T(8,128)S(1)} %concatenate.3.pack, f32[2,5,2,64,128]{4,3,2,1,0:T(8,128)S(1)} %copy-done, f32[2,5,2,64,128]{4,3,2,1,0:T(8,128)S(1)} %collective-permute-done.other, ...), custom_call_target="tpu_custom_call" | custom-call | flops 200000000 | bytes 4000000 | tf_op jit(solution)/shard_map/first_residual/pallas_call | solution.py:431
  18.1 10.4 %all-to-all-start = ((f32[16,17,8,128]{3,2,1,0:T(8,128)}), f32[16,17,8,128]{3,2,1,0:T(8,128)S(1)}, u32[]{:S(2)}, u32[]{:S(2)}) async-start(f32[16,17,8,128]{3,2,1,0:T(8,128)} %bitcast.5), calls=%async_computation | async-start | bytes 2228224 | tf_op jit(solution)/shard_map/all_to_all | solution.py:449
  28.5 0.9 copy-done.13
  29.4 4.5 %tables_b.1 = (f32[5,256,256]{2,1,0:T(8,128)S(1)}, f32[5,64,256]{2,1,0:T(8,128)S(1)}, f32[5,64,256]{2,1,0:T(8,128)S(1)}, f32[5,64,64]{2,1,0:T(8,128)S(1)}, f32[5...) custom-call(s32[4]{0:T(128)S(1)} %pad_add_fusion.info, f32[2,5,21]{2,1,0:T(8,128)S(1)} %concatenate.3.pack, ...), custom_call_target="tpu_custom_call" | custom-call | flops 100000000 | bytes 4000000 | tf_op jit(solution)/shard_map/tables_b/pallas_call | solution.py:451
  35.3 19.3 %all-to-all-done.lines = f32[16,17,8,128]{3,2,1,0:T(8,128)S(1)} async-done(((f32[16,17,8,128]{3,2,1,0:T(8,128)}), f32[16,17,8,128]{3,2,1,0:T(8,128)S(1)}, u32[]{:S(2)}, u32[]{:S(2)}) %all-to-all-start) | async-done | bytes 1114144 | tf_op jit(solution)/shard_map/all_to_all | solution.py:449
  55.0 1.9 %collective-permute-start.1 = (f32[5,64,128]{2,1,0:T(8,128)S(1)}, f32[5,64,128]{2,1,0:T(8,128)S(1)}, u32[]{:S(2)}, u32[]{:S(2)}) collective-permute-start(f32[5,64,128]{2,1,0:T(8,128)S(1)} %get-tuple-element.28), channel_id=1, source_target_pairs={{0,1},{1,4},{4,5},{5,8},{8,9},{9,12},{12,13},{2,3},{3,6},{6,7},{7,... | collective-permute-start | bytes 491528 | tf_op jit(solution)/shard_map/ppermute | solution.py:479
  57.0 3.6 %collective-permute-start.2 = (f32[5,64,128]{2,1,0:T(8,128)S(1)}, f32[5,64,128]{2,1,0:T(8,128)S(1)}, u32[]{:S(2)}, u32[]{:S(2)}) collective-permute-start(f32[5,64,128]{2,1,0:T(8,128)S(1)} %get-tuple-element.29), channel_id=1, source_target_pairs={{1,0},{4,1},{5,4},{8,5},{9,8},{12,9},{13,12},{3,2},{6,3},{7,6},{10... | collective-permute-start | bytes 491528 | tf_op jit(solution)/shard_map/ppermute | solution.py:480
  60.6 3.7 %second_residual.1.local = f32[5,32,8,128]{3,2,1,0:T(8,128)S(1)} custom-call(s32[4]{0:T(128)S(1)} %pad_add_fusion.info, f32[3,5,5]{2,1,0:T(8,128)S(1)} %get-tuple-element.22.mixes, f32[16,17,8,128]{3,2,1,0:T(8,128)S(1)} %all-to-all-done.lines, f32[5,256,256]{2,1,0:T(8,128)S(1)} %get-tuple-element.24.solve_x, f32[5,128,128]{2,1,0:T(8,128)S(1)} %get-tuple-element.25.solve_z), custom_call_target="tpu_custom_call" | custom-call | flops 300000000 | bytes 4000000 | tf_op jit(solution)/shard_map/second_residual/pallas_call | solution.py:482
  64.4 2.1 %halo_rows.1 = (f32[16,15,8,128]{3,2,1,0:T(8,128)}, f32[8,128]{1,0:T(8,128)S(1)}) custom-call(f32[3,5,5]{2,1,0:T(8,128)S(1)} %get-tuple-element.22.mixes, f32[5,32,8,128]{3,2,1,0:T(8,128)S(1)} %second_residual.1.local, f32[5,64,128]{2,1,0:T(8,128)S(1)} %collective-permute-done.1.from_prev, f32[5,64,128]{2,1,0:T(8,128)S(1)} %collective-permute-done.2.from_next, ...), custom_call_target="tpu_custom_call" | custom-call | flops 50000000 | bytes 4000000 | tf_op jit(solution)/shard_map/halo_rows/pallas_call | solution.py:491
  66.5 3.7 %all-to-all-start.1 = ((f32[16,15,8,128]{3,2,1,0:T(8,128)}), f32[16,15,8,128]{3,2,1,0:T(8,128)S(1)}, u32[]{:S(2)}, u32[]{:S(2)}) async-start(f32[16,15,8,128]{3,2,1,0:T(8,128)} %get-tuple-element.32), calls=%async_computation.1 | async-start | bytes 1966080 | tf_op jit(solution)/shard_map/all_to_all | solution.py:501
  70.3 6.8 %collective-permute-start.4 = (f32[2,5,64,128]{3,2,1,0:T(8,128)S(1)}, f32[2,5,64,128]{3,2,1,0:T(8,128)S(1)}, u32[]{:S(2)}, u32[]{:S(2)}) collective-permute-start(f32[2,5,64,128]{3,2,1,0:T(8,128)S(1)} %dynamic-slice_bitcast_fusion), channel_id=1, source_target_pairs={{1,2},{3,4},{5,6},{7,8},{9,10},{11,12},{13,14},{2,1},{4,3},{6,5},{... | collective-permute-start | bytes 983048 | tf_op jit(solution)/shard_map/ppermute | solution.py:399
  77.1 1.1 tables_y.1.solve_y
  78.2 9.5 %all-to-all-done.1.solved = f32[16,15,8,128]{3,2,1,0:T(8,128)S(1)} async-done(((f32[16,15,8,128]{3,2,1,0:T(8,128)}), f32[16,15,8,128]{3,2,1,0:T(8,128)S(1)}, u32[]{:S(2)}, u32[]{:S(2)}) %all-to-all-start.1) | async-done | bytes 983072 | tf_op jit(solution)/shard_map/all_to_all | solution.py:501
  87.7 2.0 %update.1 = (f32[2,5,2,64,128]{4,3,2,1,0:T(8,128)}, f32[2,5,64,128]{3,2,1,0:T(8,128)S(1)}) custom-call(s32[4]{0:T(128)S(1)} %pad_add_fusion.info, f32[2,5,21]{2,1,0:T(8,128)S(1)} %concatenate.3.pack, f32[2,5,2,64,128]{4,3,2,1,0:T(8,128)S(1)} %copy-done.1, f32[16,15,8,128]{3,2,1,0:T(8,128)S(1)} %all-to-all-done.1.solved, f32[2,5,64,64]{3,2,1,0:T(8,128)S(1)} %tables_y.1.solve_y), custom_call_target="tpu_custom_call" | custom-call | flops 60000000 | bytes 4000000 | tf_op jit(solution)/shard_map/update/pallas_call | solution.py:512
  89.7 1.9 %collective-permute-start.3 = (f32[2,5,64,128]{3,2,1,0:T(8,128)S(1)}, f32[2,5,64,128]{3,2,1,0:T(8,128)S(1)}, u32[]{:S(2)}, u32[]{:S(2)}) collective-permute-start(f32[2,5,64,128]{3,2,1,0:T(8,128)S(1)} %get-tuple-element.35.mine), channel_id=1, source_target_pairs={{0,1},{1,0},{2,3},{3,2},{4,5},{5,4},{6,7},{7,6},{8,9},{9,8},{10,11... | collective-permute-start | bytes 983048 | tf_op jit(solution)/shard_map/ppermute | solution.py:521
  91.6 16.2 %collective-permute-done.4.start_outer = f32[2,5,64,128]{3,2,1,0:T(8,128)S(1)} collective-permute-done((f32[2,5,64,128]{3,2,1,0:T(8,128)S(1)}, f32[2,5,64,128]{3,2,1,0:T(8,128)S(1)}, u32[]{:S(2)}, u32[]{:S(2)}) %collective-permute-start.4) | collective-permute-done | bytes 327712 | tf_op jit(solution)/shard_map/ppermute | solution.py:399
  107.8 1.1 copy-done.3
  108.9 1.3 inside_terms.1.inside
  111.0 28.4 %all_to_all.20.pieces = f32[32,16,128]{2,1,0:T(8,128)S(1)} all-to-all(f32[32,16,128]{2,1,0:T(8,128)S(1)} %terms.1), channel_id=1, replica_groups=mesh['cond'=32,'grid'=16] {'cond'}, dimensions={0} | all-to-all | bytes 524288 | tf_op jit(solution)/shard_map/all_to_all | solution.py:541
  139.4 16.5 %all_to_all.21 = f32[32,16,128]{2,1,0:T(8,128)S(1)} all-to-all(f32[32,16,128]{2,1,0:T(8,128)S(1)} %sum_conditions.1), channel_id=1, replica_groups=mesh['cond'=32,'grid'=16] {'cond'}, dimensions={0} | all-to-all | bytes 524288 | tf_op jit(solution)/shard_map/all_to_all | solution.py:550
  (50 shorter events, 10.9 us)
Async XLA Ops:
  0.6 10.6 %collective-permute-start = (f32[2,5,2,64,128]{4,3,2,1,0:T(8,128)}, f32[2,5,2,64,128]{4,3,2,1,0:T(8,128)S(1)}, u32[]{:S(2)}, u32[]{:S(2)}) collective-permute-start(f32[2,5,2,64,128]{4,3,2,1,0:T(8,128)} %adjoint.3), channel_id=1, source_target_pairs={{0,1},{1,0},{2,3},{3,2},{4,5},{5,4},{6,7},{7,6},{8,9},{9,8},{10,11... | collective-permute-start | bytes 1966088 | tf_op jit(solution)/shard_map/ppermute | solution.py:397
  7.0 0.8 copy-start.9
  7.8 0.7 copy-start.11
  8.5 0.8 copy-start.14
  11.2 1.1 copy-start
  12.3 1.1 copy-start.2
  13.4 0.8 copy-start.8
  18.0 10.4 %copy-start.12 = (f32[8,128]{1,0:T(8,128)S(1)}, f32[8,128]{1,0:T(8,128)}, u32[]{:S(2)}) copy-start(f32[8,128]{1,0:T(8,128)} %constant.61.clone.spec_in) | copy-start | bytes 12292
  18.0 10.4 %copy-start.15 = (f32[128,128]{1,0:T(8,128)S(1)}, f32[128,128]{1,0:T(8,128)}, u32[]{:S(2)}) copy-start(f32[128,128]{1,0:T(8,128)} %constant.62.clone.sine_z_in) | copy-start | bytes 196612
  18.1 10.4 %copy-start.16 = (f32[32,256]{1,0:T(8,128)S(1)}, f32[32,256]{1,0:T(8,128)}, u32[]{:S(2)}) copy-start(f32[32,256]{1,0:T(8,128)} %constant.65.clone.right_in) | copy-start | bytes 98308
  18.1 10.4 %copy-start.17 = (f32[32,64]{1,0:T(8,128)S(1)}, f32[32,64]{1,0:T(8,128)}, u32[]{:S(2)}) copy-start(f32[32,64]{1,0:T(8,128)} %constant.66.clone.right_2_in) | copy-start | bytes 24580
  18.1 36.5 %all-to-all-start = ((f32[16,17,8,128]{3,2,1,0:T(8,128)}), f32[16,17,8,128]{3,2,1,0:T(8,128)S(1)}, u32[]{:S(2)}, u32[]{:S(2)}) async-start(f32[16,17,8,128]{3,2,1,0:T(8,128)} %bitcast.5), calls=%async_computation | async-start | bytes 2228224 | tf_op jit(solution)/shard_map/all_to_all | solution.py:449
  28.5 0.9 copy-start.13
  33.9 0.7 copy-start.4
  55.0 9.3 %collective-permute-start.1 = (f32[5,64,128]{2,1,0:T(8,128)S(1)}, f32[5,64,128]{2,1,0:T(8,128)S(1)}, u32[]{:S(2)}, u32[]{:S(2)}) collective-permute-start(f32[5,64,128]{2,1,0:T(8,128)S(1)} %get-tuple-element.28), channel_id=1, source_target_pairs={{0,1},{1,4},{4,5},{5,8},{8,9},{9,12},{12,13},{2,3},{3,6},{6,7},{7,... | collective-permute-start | bytes 491528 | tf_op jit(solution)/shard_map/ppermute | solution.py:479
  57.0 7.4 %collective-permute-start.2 = (f32[5,64,128]{2,1,0:T(8,128)S(1)}, f32[5,64,128]{2,1,0:T(8,128)S(1)}, u32[]{:S(2)}, u32[]{:S(2)}) collective-permute-start(f32[5,64,128]{2,1,0:T(8,128)S(1)} %get-tuple-element.29), channel_id=1, source_target_pairs={{1,0},{4,1},{5,4},{8,5},{9,8},{12,9},{13,12},{3,2},{6,3},{7,6},{10... | collective-permute-start | bytes 491528 | tf_op jit(solution)/shard_map/ppermute | solution.py:480
  60.6 3.7 %copy-start.5 = (f32[5,64,64]{2,1,0:T(8,128)S(1)}, f32[5,64,64]{2,1,0:T(8,128)}, u32[]{:S(2)}) copy-start(f32[5,64,64]{2,1,0:T(8,128)} %copy-done.4) | copy-start | bytes 245764
  60.6 3.7 %copy-start.7 = (f32[5,64,64]{2,1,0:T(8,128)S(1)}, f32[5,64,64]{2,1,0:T(8,128)}, u32[]{:S(2)}) copy-start(f32[5,64,64]{2,1,0:T(8,128)} %copy-done.6) | copy-start | bytes 245764
  66.5 3.7 %copy-start.1 = (f32[2,5,2,64,128]{4,3,2,1,0:T(8,128)S(1)}, f32[2,5,2,64,128]{4,3,2,1,0:T(8,128)}, u32[]{:S(2)}) copy-start(f32[2,5,2,64,128]{4,3,2,1,0:T(8,128)} %adjoint.3) | copy-start | bytes 1966084
  66.5 10.6 %copy-start.10 = (f32[64,64]{1,0:T(8,128)S(1)}, f32[64,64]{1,0:T(8,128)}, u32[]{:S(2)}) copy-start(f32[64,64]{1,0:T(8,128)} %constant.63.clone.sine_y_in) | copy-start | bytes 49156
  66.5 21.2 %all-to-all-start.1 = ((f32[16,15,8,128]{3,2,1,0:T(8,128)}), f32[16,15,8,128]{3,2,1,0:T(8,128)S(1)}, u32[]{:S(2)}, u32[]{:S(2)}) async-start(f32[16,15,8,128]{3,2,1,0:T(8,128)} %get-tuple-element.32), calls=%async_computation.1 | async-start | bytes 1966080 | tf_op jit(solution)/shard_map/all_to_all | solution.py:501
  70.3 37.5 %collective-permute-start.4 = (f32[2,5,64,128]{3,2,1,0:T(8,128)S(1)}, f32[2,5,64,128]{3,2,1,0:T(8,128)S(1)}, u32[]{:S(2)}, u32[]{:S(2)}) collective-permute-start(f32[2,5,64,128]{3,2,1,0:T(8,128)S(1)} %dynamic-slice_bitcast_fusion), channel_id=1, source_target_pairs={{1,2},{3,4},{5,6},{7,8},{9,10},{11,12},{13,14},{2,1},{4,3},{6,5},{... | collective-permute-start | bytes 983048 | tf_op jit(solution)/shard_map/ppermute | solution.py:399
  89.7 20.5 %collective-permute-start.3 = (f32[2,5,64,128]{3,2,1,0:T(8,128)S(1)}, f32[2,5,64,128]{3,2,1,0:T(8,128)S(1)}, u32[]{:S(2)}, u32[]{:S(2)}) collective-permute-start(f32[2,5,64,128]{3,2,1,0:T(8,128)S(1)} %get-tuple-element.35.mine), channel_id=1, source_target_pairs={{0,1},{1,0},{2,3},{3,2},{4,5},{5,4},{6,7},{7,6},{8,9},{9,8},{10,11... | collective-permute-start | bytes 983048 | tf_op jit(solution)/shard_map/ppermute | solution.py:521
  107.8 1.1 copy-start.3
  (1 other events, 0.7 us)

commit v4 on v3

--- a/solution.py
+++ b/solution.py
@@ -155,22 +155,23 @@
         solve_z[f] = exact(sine_z[...] / denom, sine_z[...])
 
 
-def first_kernel(info, pack, adjoint, other, source_in, radius, solve_z, solve_y, out, token,
-                 source, made, lapped, stage, sems, out_sems):
+def planes_kernel(info, adjoint, outer, inner, sems):
+    me = info[0]
+    for copy in fetch((adjoint.at[:, :, me], adjoint.at[:, :, 1 - me]), (outer, inner), sems):
+        copy.wait()
+
+
+def local_kernel(info, pack, adjoint, inner, source_in, radius, solve_z, solve_y, made, source, lapped, stage, sems):
     copies = fetch([source_in.at[c] for c in range(2)], [source.at[c] for c in range(2)], sems)
     ny = adjoint.shape[3]
     blocks = ny // 8
     me = info[0]
-    before, after = me.astype(F32), (1 - me).astype(F32)
-    token[...] = jnp.zeros(token.shape, F32)
-    stores = []
-    for c in range(2):
-        residual = {}
+    sides = (me.astype(F32), (1 - me).astype(F32))
+    for c in range(2):
         for x in range(2):
             for f in range(FIELDS):
                 v = adjoint[c, f, x]
-                beside = adjoint[c, f, 1 - x]
-                beside = beside + (other[c, f, 1] * before if x == 0 else other[c, f, 0] * after)
+                beside = adjoint[c, f, 1 - x] + inner[c, f] * sides[x]
                 beside = beside + shifted(v, 0, 1) + shifted(v, 0, -1)
                 beside = beside + shifted(v, 1, 1) + shifted(v, 1, -1)
                 lapped[x, f] = 6.0 * v - beside
@@ -185,37 +186,41 @@
                 residual.append(r)
             for f in range(FIELDS):
                 stage[f, x * ny : x * ny + ny] = mixed(lambda g: pack[c, f, LEFT + g], residual)
-        outer = [adjoint[c, g, me] for g in range(FIELDS)]
-        outer = [mixed(lambda g: pack[c, f, COUP + g], outer) for f in range(FIELDS)]
-        for f in range(FIELDS):
-            stage[f, 2 * ny : 3 * ny] = mixed(lambda g: pack[c, f, LEFT + g], outer)
         for f in range(FIELDS):
             r = dot(stage[f], solve_z[c, f])
-            r = jnp.concatenate([r[p * ny : p * ny + ny] for p in range(3)], axis=1)
+            r = jnp.concatenate([r[x * ny : x * ny + ny] for x in range(2)], axis=1)
             r = dot(solve_y[c, f], r)
-            for p in range(3):
+            for x in range(2):
                 for b in range(blocks):
-                    made[b // 2, c, b % 2, 3 * f + p] = r[8 * b : 8 * b + 8, 128 * p : 128 * p + 128]
+                    made[b // 2, c, b % 2, 2 * f + x] = r[8 * b : 8 * b + 8, 128 * x : 128 * x + 128]
         for x in range(2):
             for b in range(blocks):
-                made[b // 2, c, b % 2, 3 * FIELDS + x] = radius[x, 8 * b : 8 * b + 8]
-        stores.append(pltpu.make_async_copy(made.at[:, c], out.at[:, c], out_sems.at[c]))
+                made[b // 2, c, b % 2, 2 * FIELDS + x] = radius[x, 8 * b : 8 * b + 8]
+
+
+def outer_kernel(info, pack, local, outer, solve_z, solve_y, out, token, made, stage, sems):
+    ny = outer.shape[2]
+    me = info[0]
+    token[...] = jnp.zeros(token.shape, F32)
+    stores = []
+    for c in range(2):
+        made[:, c] = local[:, c]
+        parts = [mixed(lambda g: pack[c, f, COUP + g], [outer[c, g] for g in range(FIELDS)]) for f in range(FIELDS)]
+        for f in range(FIELDS):
+            r = mixed(lambda g: pack[c, f, LEFT + g], parts)
+            stage[f] = dot(solve_y[c, f], dot(r, solve_z[c, f]))
+        for f in range(FIELDS):
+            for b in range(ny // 8):
+                made[b // 2, c, b % 2, 2 * f + me] += stage[f, 8 * b : 8 * b + 8]
+        stores.append(pltpu.make_async_copy(made.at[:, c], out.at[:, c], sems.at[c]))
         stores[-1].start()
     for copy in stores:
         copy.wait()
 
 
-def assembled(lines, f):
-    zero = jnp.zeros((1, 8, 128), F32)
-    w = lines[:, 3 * f : 3 * f + 3].reshape(lines.shape[0] // 2, 6, 8, 128)
-    plane_0 = w[:, 0] + jnp.concatenate([zero, w[:-1, 5]], axis=0)
-    plane_3 = w[:, 4] + jnp.concatenate([w[1:, 2], zero], axis=0)
-    return jnp.stack([plane_0, w[:, 1], w[:, 3], plane_3], axis=1)
-
-
 def ends_kernel(lines, ends_prev, ends_next, to_prev, to_next):
     for f in range(FIELDS):
-        w = assembled(lines, f).reshape(-1, 128)
+        w = lines[:, 2 * f : 2 * f + 2].reshape(-1, 128)
         to_prev[f] = dot(ends_prev[f], w)
         to_next[f] = dot(ends_next[f], w)
 
@@ -227,7 +232,7 @@
     has_prev, has_next = info[2].astype(F32), info[3].astype(F32)
     zero = jnp.zeros((1, 8, 128), F32)
     for f in range(FIELDS):
-        u = dot(solve_x[f], assembled(lines, f).reshape(nx * 8, 128)).reshape(full)
+        u = dot(solve_x[f], lines[:, 2 * f : 2 * f + 2].reshape(nx * 8, 128)).reshape(full)
         solved[f] = u
         up = jnp.where(row == 7, 0.0, pltpu.roll(u, 7, 1))
         down = jnp.where(row == 0, 0.0, pltpu.roll(u, 1, 1))
@@ -240,7 +245,7 @@
         flat = u.reshape(nx * 8, 128)
         beside = beside + (shifted(flat, 1, 1) + shifted(flat, 1, -1)).reshape(full)
         lapped[f] = 4.0 * u + ku - beside
-    sr = lines[:, 3 * FIELDS :].reshape(full)
+    sr = lines[:, 2 * FIELDS :].reshape(full)
     for f in range(FIELDS):
         near = mixed(lambda g: mixes[0, f, g], solved)
         far = mixed(lambda g: mixes[1, f, g], lapped)
@@ -394,9 +399,17 @@
     cores = [(i, i ^ 1) for i in range(peers)]
     chips = [(i, i + 1) for i in range(1, peers - 1, 2)]
     chips = chips + [(j, i) for i, j in chips]
-    other = lax.ppermute(adjoint_start, "grid", cores)
-    outer = lax.dynamic_index_in_dim(adjoint_start, core, 2, keepdims=False)
+    outer, inner = call(
+        planes_kernel,
+        (shape(2, fields, ny, nz), shape(2, fields, ny, nz)),
+        [SMEM, ANY],
+        1000,
+        "planes",
+        [sems(2)],
+        (ANY, ANY),
+    )(info, adjoint_start)
     outer = lax.ppermute(outer, "grid", chips)
+    inner = lax.ppermute(inner, "grid", cores)
 
     sine_z, spec_z = sine_tables(nz)
     sine_y, spec_y = sine_tables(ny)
@@ -428,24 +441,32 @@
         [vmem(nz, nz), vmem(ny, ny), vmem(8, nz), sems(3)],
     )(pack, sine_z, sine_y, spec)
 
-    lines, token = call(
-        first_kernel,
-        (shape(blocks // 2, 2, 2, 3 * fields + planes, 8, nz), shape(8, nz)),
+    tiles = 2 * fields + planes
+    local = call(
+        local_kernel,
+        shape(blocks // 2, 2, 2, tiles, 8, nz),
         [SMEM, SMEM, VMEM, VMEM, ANY, VMEM, VMEM, VMEM],
         200_000_000,
         "first_residual",
         [
             vmem(2, fields, planes, ny, nz),
-            vmem(blocks // 2, 2, 2, 3 * fields + planes, 8, nz),
             vmem(planes, fields, ny, nz),
-            vmem(fields, 3 * ny, nz),
-            sems(2),
+            vmem(fields, 2 * ny, nz),
             sems(2),
         ],
+    )(info, pack, adjoint_start, inner, adjoint_source, spectral_radius, solve_z, solve_y)
+
+    lines, token = call(
+        outer_kernel,
+        (shape(blocks // 2, 2, 2, tiles, 8, nz), shape(8, nz)),
+        [SMEM, SMEM] + [VMEM] * 4,
+        50_000_000,
+        "outer_plane",
+        [vmem(blocks // 2, 2, 2, tiles, 8, nz), vmem(fields, ny, nz), sems(2)],
         (ANY, VMEM),
-    )(info, pack, adjoint_start, other, adjoint_source, spectral_radius, solve_z, solve_y)
-
-    lines = lines.reshape(peers, 3 * fields + planes, 8, nz)
+    )(info, pack, local, outer, solve_z, solve_y)
+
+    lines = lines.reshape(peers, tiles, 8, nz)
     lines = lax.all_to_all(lines, "grid", 0, 0, tiled=True)
 
     solve_x, ends_prev, ends_next, halo_prev, halo_next, solve_zb, mixes = call(

time: 158 us -> 159 us (level)
  the two profiles are of different devices: /device:TPU:2 before, /device:TPU:8 now
where the time goes in v4:
time: 159 us; the launch traced here: 158 us
  waiting for transfers between devices  45.8 us (29%)
  blocking collectives  40.1 us (25%)
  starting transfers between devices  31.5 us (20%)
  Pallas kernels  24.8 us (16%)
  local copies, waits for them, and re-layouts  14.3 us (9%)
    all_to_all x2, blocking collectives, body(): pieces = lax.all_to_all(pieces, 'cond', 0, 0, tiled=True)  40.1 us
    all_to_all x1, waiting for transfers between devices, body(): step = lax.all_to_all(step, 'grid', 0, 0, tiled=True)  27.1 us
    all_to_all x1, starting transfers between devices, body(): lines = lax.all_to_all(lines, 'grid', 0, 0, tiled=True)  18.7 us
    all_to_all x1, waiting for transfers between devices, body(): lines = lax.all_to_all(lines, 'grid', 0, 0, tiled=True)  18.7 us
    unnamed x45, local copies, waits for them, and re-layouts  13.5 us
    all_to_all x1, starting transfers between devices, body(): step = lax.all_to_all(step, 'grid', 0, 0, tiled=True)  4.99 us
    pallas_call x1, Pallas kernels, body(): call(tables_b_kernel, (shape(fields, rows_b, rows_b), shape(fields, 2 * n...  4.55 us
    pallas_call x1, Pallas kernels, body(): call(second_kernel, shape(fields, nx, 8, nz), [SMEM, SMEM] + [VMEM] * 3,...  3.69 us
  transfers between devices with their start and end apart: 7, of which 2 were waited for; matrix products, arithmetic and copies ran while one was open for 3% of the time, Pallas kernels for 10%

profile of v4, /device:TPU:8, one launch (start us, length us, event | category | flops | bytes accessed | tf_op | source)
XLA Modules:
  0.0 158.3 jit_solution(7267687929535678625)
XLA Ops:
  0.8 1.1 copy-done
  2.5 1.9 %collective-permute-start = (f32[2,5,64,128]{3,2,1,0:T(8,128)S(1)}, f32[2,5,64,128]{3,2,1,0:T(8,128)S(1)}, u32[]{:S(2)}, u32[]{:S(2)}) collective-permute-start(f32[2,5,64,128]{3,2,1,0:T(8,128)S(1)} %get-tuple-element.21), channel_id=1, source_target_pairs={{0,1},{1,0},{2,3},{3,2},{4,5},{5,4},{6,7},{7,6},{8,9},{9,8},{10,11... | collective-permute-start | bytes 983048 | tf_op jit(solution)/shard_map/ppermute | solution.py:412
  11.8 1.8 %solve_tables.1 = (f32[2,5,128,128]{3,2,1,0:T(8,128)S(1)}, f32[2,5,64,64]{3,2,1,0:T(8,128)S(1)}) custom-call(f32[2,5,21]{2,1,0:T(8,128)S(1)} %concatenate.3.pack, f32[128,128]{1,0:T(8,128)S(1)} %copy-done.16, f32[64,64]{1,0:T(8,128)S(1)} %copy-done.11, f32[8,128]{1,0:T(8,128)S(1)} %copy-done.13), custom_call_target="tpu_custom_call" | custom-call | flops 100000000 | bytes 4000000 | tf_op jit(solution)/shard_map/solve_tables/pallas_call | solution.py:435
  13.7 1.1 copy-done.4
  14.8 2.7 %first_residual.1.local = f32[4,2,2,12,8,128]{5,4,3,2,1,0:T(8,128)S(1)} custom-call(s32[4]{0:T(128)S(1)} %pad_add_fusion.info, f32[2,5,21]{2,1,0:T(8,128)S(1)} %concatenate.3.pack, f32[2,5,2,64,128]{4,3,2,1,0:T(8,128)S(1)} %copy-done.1, f32[2,5,64,128]{3,2,1,0:T(8,128)S(1)} %collective-permute-done.inner, f32[2,5,2,64,128]{4,3,2,1,0:T(8,128)S(1)} %copy-done.4, ...), custom_call_target="tpu_custom_call" | custom-call | flops 200000000 | bytes 4000000 | tf_op jit(solution)/shard_map/first_residual/pallas_call | solution.py:445
  17.5 3.6 %outer_plane.1 = (f32[4,2,2,12,8,128]{5,4,3,2,1,0:T(8,128)}, f32[8,128]{1,0:T(8,128)S(1)}) custom-call(s32[4]{0:T(128)S(1)} %pad_add_fusion.info, f32[2,5,21]{2,1,0:T(8,128)S(1)} %concatenate.3.pack, f32[4,2,2,12,8,128]{5,4,3,2,1,0:T(8,128)S(1)} %first_residual.1.local, f32[2,5,64,128]{3,2,1,0:T(8,128)S(1)} %collective-permute-done.1.outer.start_outer, ...), custom_call_target="tpu_custom_call" | custom-call | flops 50000000 | bytes 4000000 | tf_op jit(solution)/shard_map/outer_plane/pallas_call | solution.py:459
  21.2 18.7 %all-to-all-start = ((f32[16,12,8,128]{3,2,1,0:T(8,128)}), f32[16,12,8,128]{3,2,1,0:T(8,128)S(1)}, u32[]{:S(2)}, u32[]{:S(2)}) async-start(f32[16,12,8,128]{3,2,1,0:T(8,128)} %bitcast.5), calls=%async_computation | async-start | bytes 1572864 | tf_op jit(solution)/shard_map/all_to_all | solution.py:470
  40.8 4.5 %tables_b.1 = (f32[5,256,256]{2,1,0:T(8,128)S(1)}, f32[5,64,256]{2,1,0:T(8,128)S(1)}, f32[5,64,256]{2,1,0:T(8,128)S(1)}, f32[5,64,64]{2,1,0:T(8,128)S(1)}, f32[5...) custom-call(s32[4]{0:T(128)S(1)} %pad_add_fusion.info, f32[2,5,21]{2,1,0:T(8,128)S(1)} %concatenate.3.pack, ...), custom_call_target="tpu_custom_call" | custom-call | flops 100000000 | bytes 4000000 | tf_op jit(solution)/shard_map/tables_b/pallas_call | solution.py:472
  46.8 18.7 %all-to-all-done.lines = f32[16,12,8,128]{3,2,1,0:T(8,128)S(1)} async-done(((f32[16,12,8,128]{3,2,1,0:T(8,128)}), f32[16,12,8,128]{3,2,1,0:T(8,128)S(1)}, u32[]{:S(2)}, u32[]{:S(2)}) %all-to-all-start) | async-done | bytes 786464 | tf_op jit(solution)/shard_map/all_to_all | solution.py:470
  65.5 1.0 copy-done.7
  66.5 1.0 copy-done.9
  67.8 2.0 %collective-permute-start.2 = (f32[5,64,128]{2,1,0:T(8,128)S(1)}, f32[5,64,128]{2,1,0:T(8,128)S(1)}, u32[]{:S(2)}, u32[]{:S(2)}) collective-permute-start(f32[5,64,128]{2,1,0:T(8,128)S(1)} %get-tuple-element.32), channel_id=1, source_target_pairs={{0,1},{1,4},{4,5},{5,8},{8,9},{9,12},{12,13},{2,3},{3,6},{6,7},{7,... | collective-permute-start | bytes 491528 | tf_op jit(solution)/shard_map/ppermute | solution.py:500
  69.8 1.3 collective-permute-start.3
  71.1 3.7 %second_residual.1.local = f32[5,32,8,128]{3,2,1,0:T(8,128)S(1)} custom-call(s32[4]{0:T(128)S(1)} %pad_add_fusion.info, f32[3,5,5]{2,1,0:T(8,128)S(1)} %get-tuple-element.26.mixes, f32[16,12,8,128]{3,2,1,0:T(8,128)S(1)} %all-to-all-done.lines, f32[5,256,256]{2,1,0:T(8,128)S(1)} %get-tuple-element.28.solve_x, f32[5,128,128]{2,1,0:T(8,128)S(1)} %get-tuple-element.29.solve_z), custom_call_target="tpu_custom_call" | custom-call | flops 300000000 | bytes 4000000 | tf_op jit(solution)/shard_map/second_residual/pallas_call | solution.py:503
  74.8 2.2 %halo_rows.1 = (f32[16,15,8,128]{3,2,1,0:T(8,128)}, f32[8,128]{1,0:T(8,128)S(1)}) custom-call(f32[3,5,5]{2,1,0:T(8,128)S(1)} %get-tuple-element.26.mixes, f32[5,32,8,128]{3,2,1,0:T(8,128)S(1)} %second_residual.1.local, f32[5,64,128]{2,1,0:T(8,128)S(1)} %collective-permute-done.2.from_prev, f32[5,64,128]{2,1,0:T(8,128)S(1)} %collective-permute-done.3.from_next, ...), custom_call_target="tpu_custom_call" | custom-call | flops 50000000 | bytes 4000000 | tf_op jit(solution)/shard_map/halo_rows/pallas_call | solution.py:512
  77.0 5.0 %all-to-all-start.1 = ((f32[16,15,8,128]{3,2,1,0:T(8,128)}), f32[16,15,8,128]{3,2,1,0:T(8,128)S(1)}, u32[]{:S(2)}, u32[]{:S(2)}) async-start(f32[16,15,8,128]{3,2,1,0:T(8,128)} %get-tuple-element.36), calls=%async_computation.1 | async-start | bytes 1966080 | tf_op jit(solution)/shard_map/all_to_all | solution.py:522
  82.0 1.1 tables_y.1.solve_y
  83.2 27.1 %all-to-all-done.1.solved = f32[16,15,8,128]{3,2,1,0:T(8,128)S(1)} async-done(((f32[16,15,8,128]{3,2,1,0:T(8,128)}), f32[16,15,8,128]{3,2,1,0:T(8,128)S(1)}, u32[]{:S(2)}, u32[]{:S(2)}) %all-to-all-start.1) | async-done | bytes 983072 | tf_op jit(solution)/shard_map/all_to_all | solution.py:522
  110.3 2.0 %update.1 = (f32[2,5,2,64,128]{4,3,2,1,0:T(8,128)}, f32[2,5,64,128]{3,2,1,0:T(8,128)S(1)}) custom-call(s32[4]{0:T(128)S(1)} %pad_add_fusion.info, f32[2,5,21]{2,1,0:T(8,128)S(1)} %concatenate.3.pack, f32[2,5,2,64,128]{4,3,2,1,0:T(8,128)S(1)} %copy-done.1, f32[16,15,8,128]{3,2,1,0:T(8,128)S(1)} %all-to-all-done.1.solved, f32[2,5,64,64]{3,2,1,0:T(8,128)S(1)} %tables_y.1.solve_y), custom_call_target="tpu_custom_call" | custom-call | flops 60000000 | bytes 4000000 | tf_op jit(solution)/shard_map/update/pallas_call | solution.py:533
  112.3 2.0 %collective-permute-start.4 = (f32[2,5,64,128]{3,2,1,0:T(8,128)S(1)}, f32[2,5,64,128]{3,2,1,0:T(8,128)S(1)}, u32[]{:S(2)}, u32[]{:S(2)}) collective-permute-start(f32[2,5,64,128]{3,2,1,0:T(8,128)S(1)} %get-tuple-element.39.mine), channel_id=1, source_target_pairs={{0,1},{1,0},{2,3},{3,2},{4,5},{5,4},{6,7},{7,6},{8,9},{9,8},{10,11... | collective-permute-start | bytes 983048 | tf_op jit(solution)/shard_map/ppermute | solution.py:542
  114.3 1.1 copy-done.5
  115.4 1.3 inside_terms.1.inside
  117.5 23.7 %all_to_all.20.pieces = f32[32,16,128]{2,1,0:T(8,128)S(1)} all-to-all(f32[32,16,128]{2,1,0:T(8,128)S(1)} %terms.1), channel_id=1, replica_groups=mesh['cond'=32,'grid'=16] {'cond'}, dimensions={0} | all-to-all | bytes 524288 | tf_op jit(solution)/shard_map/all_to_all | solution.py:562
  141.2 16.4 %all_to_all.21 = f32[32,16,128]{2,1,0:T(8,128)S(1)} all-to-all(f32[32,16,128]{2,1,0:T(8,128)S(1)} %sum_conditions.1), channel_id=1, replica_groups=mesh['cond'=32,'grid'=16] {'cond'}, dimensions={0} | all-to-all | bytes 524288 | tf_op jit(solution)/shard_map/all_to_all | solution.py:571
  (55 shorter events, 12.4 us)
Async XLA Ops:
  0.6 13.0 %copy-start.10 = (f32[2,64,128]{2,1,0:T(8,128)S(1)}, f32[2,64,128]{2,1,0:T(8,128)}, u32[]{:S(2)}) copy-start(f32[2,64,128]{2,1,0:T(8,128)} %radius.1) | copy-start | bytes 196612
  0.8 1.1 copy-start
  1.9 11.8 %copy-start.1 = (f32[2,5,2,64,128]{4,3,2,1,0:T(8,128)S(1)}, f32[2,5,2,64,128]{4,3,2,1,0:T(8,128)}, u32[]{:S(2)}) copy-start(f32[2,5,2,64,128]{4,3,2,1,0:T(8,128)} %adjoint.5) | copy-start | bytes 1966084
  2.5 11.2 %collective-permute-start = (f32[2,5,64,128]{3,2,1,0:T(8,128)S(1)}, f32[2,5,64,128]{3,2,1,0:T(8,128)S(1)}, u32[]{:S(2)}, u32[]{:S(2)}) collective-permute-start(f32[2,5,64,128]{3,2,1,0:T(8,128)S(1)} %get-tuple-element.21), channel_id=1, source_target_pairs={{0,1},{1,0},{2,3},{3,2},{4,5},{5,4},{6,7},{7,6},{8,9},{9,8},{10,11... | collective-permute-start | bytes 983048 | tf_op jit(solution)/shard_map/ppermute | solution.py:412
  4.4 13.1 %collective-permute-start.1 = (f32[2,5,64,128]{3,2,1,0:T(8,128)S(1)}, f32[2,5,64,128]{3,2,1,0:T(8,128)S(1)}, u32[]{:S(2)}, u32[]{:S(2)}) collective-permute-start(f32[2,5,64,128]{3,2,1,0:T(8,128)S(1)} %get-tuple-element.24), channel_id=1, source_target_pairs={{1,2},{3,4},{5,6},{7,8},{9,10},{11,12},{13,14},{2,1},{4,3},{6,5},{... | collective-permute-start | bytes 983048 | tf_op jit(solution)/shard_map/ppermute | solution.py:411
  9.5 0.8 copy-start.11
  11.0 0.8 copy-start.16
  13.7 1.1 copy-start.4
  17.5 3.7 %copy-start.2 = (f32[2,5,64,128]{3,2,1,0:T(8,128)}, f32[2,5,64,128]{3,2,1,0:T(8,128)S(1)}, u32[]{:S(2)}) copy-start(f32[2,5,64,128]{3,2,1,0:T(8,128)S(1)} %collective-permute-done.1.outer.start_outer) | copy-start | bytes 983044
  21.1 18.8 %copy-start.14 = (f32[8,128]{1,0:T(8,128)S(1)}, f32[8,128]{1,0:T(8,128)}, u32[]{:S(2)}) copy-start(f32[8,128]{1,0:T(8,128)} %constant.57.clone.spec_in) | copy-start | bytes 12292
  21.1 18.8 %copy-start.17 = (f32[128,128]{1,0:T(8,128)S(1)}, f32[128,128]{1,0:T(8,128)}, u32[]{:S(2)}) copy-start(f32[128,128]{1,0:T(8,128)} %constant.58.clone.sine_z_in) | copy-start | bytes 196612
  21.1 18.8 %copy-start.18 = (f32[32,256]{1,0:T(8,128)S(1)}, f32[32,256]{1,0:T(8,128)}, u32[]{:S(2)}) copy-start(f32[32,256]{1,0:T(8,128)} %constant.61.clone.right_in) | copy-start | bytes 98308
  21.1 18.8 %copy-start.19 = (f32[32,64]{1,0:T(8,128)S(1)}, f32[32,64]{1,0:T(8,128)}, u32[]{:S(2)}) copy-start(f32[32,64]{1,0:T(8,128)} %constant.62.clone.right_2_in) | copy-start | bytes 24580
  21.2 44.3 %all-to-all-start = ((f32[16,12,8,128]{3,2,1,0:T(8,128)}), f32[16,12,8,128]{3,2,1,0:T(8,128)S(1)}, u32[]{:S(2)}, u32[]{:S(2)}) async-start(f32[16,12,8,128]{3,2,1,0:T(8,128)} %bitcast.5), calls=%async_computation | async-start | bytes 1572864 | tf_op jit(solution)/shard_map/all_to_all | solution.py:470
  39.9 0.9 copy-start.15
  65.5 1.0 copy-start.7
  66.5 1.0 copy-start.9
  67.8 7.0 %collective-permute-start.2 = (f32[5,64,128]{2,1,0:T(8,128)S(1)}, f32[5,64,128]{2,1,0:T(8,128)S(1)}, u32[]{:S(2)}, u32[]{:S(2)}) collective-permute-start(f32[5,64,128]{2,1,0:T(8,128)S(1)} %get-tuple-element.32), channel_id=1, source_target_pairs={{0,1},{1,4},{4,5},{5,8},{8,9},{9,12},{12,13},{2,3},{3,6},{6,7},{7,... | collective-permute-start | bytes 491528 | tf_op jit(solution)/shard_map/ppermute | solution.py:500
  69.8 5.0 %collective-permute-start.3 = (f32[5,64,128]{2,1,0:T(8,128)S(1)}, f32[5,64,128]{2,1,0:T(8,128)S(1)}, u32[]{:S(2)}, u32[]{:S(2)}) collective-permute-start(f32[5,64,128]{2,1,0:T(8,128)S(1)} %get-tuple-element.33), channel_id=1, source_target_pairs={{1,0},{4,1},{5,4},{8,5},{9,8},{12,9},{13,12},{3,2},{6,3},{7,6},{10... | collective-permute-start | bytes 491528 | tf_op jit(solution)/shard_map/ppermute | solution.py:501
  77.0 5.0 %copy-start.12 = (f32[64,64]{1,0:T(8,128)S(1)}, f32[64,64]{1,0:T(8,128)}, u32[]{:S(2)}) copy-start(f32[64,64]{1,0:T(8,128)} %constant.59.clone.sine_y_in) | copy-start | bytes 49156
  77.0 33.3 %all-to-all-start.1 = ((f32[16,15,8,128]{3,2,1,0:T(8,128)}), f32[16,15,8,128]{3,2,1,0:T(8,128)S(1)}, u32[]{:S(2)}, u32[]{:S(2)}) async-start(f32[16,15,8,128]{3,2,1,0:T(8,128)} %get-tuple-element.36), calls=%async_computation.1 | async-start | bytes 1966080 | tf_op jit(solution)/shard_map/all_to_all | solution.py:522
  82.0 32.3 %copy-start.3 = (f32[2,5,64,128]{3,2,1,0:T(8,128)S(1)}, f32[2,5,64,128]{3,2,1,0:T(8,128)}, u32[]{:S(2)}) copy-start(f32[2,5,64,128]{3,2,1,0:T(8,128)} %copy-done.2) | copy-start | bytes 983044
  112.3 4.4 %collective-permute-start.4 = (f32[2,5,64,128]{3,2,1,0:T(8,128)S(1)}, f32[2,5,64,128]{3,2,1,0:T(8,128)S(1)}, u32[]{:S(2)}, u32[]{:S(2)}) collective-permute-start(f32[2,5,64,128]{3,2,1,0:T(8,128)S(1)} %get-tuple-element.39.mine), channel_id=1, source_target_pairs={{0,1},{1,0},{2,3},{3,2},{4,5},{5,4},{6,7},{7,6},{8,9},{9,8},{10,11... | collective-permute-start | bytes 983048 | tf_op jit(solution)/shard_map/ppermute | solution.py:542
  114.3 1.1 copy-start.5
  (3 other events, 2.1 us)

commit v5 on v3

--- a/solution.py
+++ b/solution.py
@@ -3,7 +3,6 @@
 
 import jax
 import jax.numpy as jnp
-import numpy as np
 from jax import lax
 from jax.experimental import pallas as pl
 from jax.experimental.pallas import tpu as pltpu
@@ -15,6 +14,7 @@
 SMEM = pl.BlockSpec(memory_space=pltpu.SMEM)
 LIMIT = 20 * 1024 * 1024
 ANY = pl.BlockSpec(memory_space=pl.ANY)
+HBM = pl.BlockSpec(memory_space=pltpu.HBM)
 COUP, LEFT, RIGHT, RATE, SENS = 0, 5, 10, 15, 18
 
 
@@ -33,13 +33,20 @@
     return jnp.dot(a, b, precision=lax.Precision.HIGHEST, preferred_element_type=F32)
 
 
-def sine_tables(length):
-    counter = np.arange(1, length + 1, dtype=np.float64)
-    sine = math.sqrt(2.0 / (length + 1)) * np.sin(
-        counter[:, None] * counter[None, :] * (math.pi / (length + 1))
-    )
-    spectrum = 2.0 - 2.0 * np.cos(counter * (math.pi / (length + 1)))
-    return sine.astype(np.float32), (spectrum + spectrum * spectrum).astype(np.float32)
+def counters(length, repeat):
+    return lax.broadcasted_iota(jnp.int32, (length * repeat,), 0) // repeat + 1
+
+
+def sine_table(length, repeat_rows=1, repeat_columns=1):
+    product = counters(length, repeat_rows)[:, None] * counters(length, repeat_columns)[None, :]
+    product = product % (2 * (length + 1))
+    return math.sqrt(2.0 / (length + 1)) * jnp.sin(product.astype(F32) * (math.pi / (length + 1)))
+
+
+def spectrum(length):
+    half = jnp.sin(counters(length, 1).astype(F32) * (math.pi / (2 * (length + 1))))
+    lam = 4.0 * half * half
+    return (lam + lam * lam)[None, :]
 
 
 def call(kernel, outs, in_specs, flops, name, scratch=(), out_specs=None):
@@ -88,34 +95,24 @@
     return (b // 2) * 4 + c * 2 + b % 2
 
 
-def tables_kernel(pack, sine_z_in, sine_y_in, spec_in, solve_z, solve_y, sine_z, sine_y, spec, sems):
-    for copy in fetch((sine_z_in, sine_y_in, spec_in), (sine_z, sine_y, spec), sems):
-        copy.wait()
-    ny = sine_y.shape[0]
+def tables_kernel(pack, sine_z, spec_z, sine_y, spec_y, solve_z, solve_y):
     for c in range(2):
         for f in range(FIELDS):
-            denom = 1.0 + pack[c, f, RATE + 2] * spec[0:1]
+            denom = 1.0 + pack[c, f, RATE + 2] * spec_z[...]
             solve_z[c, f] = exact(sine_z[...] / denom, sine_z[...])
-            denom = 1.0 + pack[c, f, RATE + 1] * spec[1:2, :ny]
+            denom = 1.0 + pack[c, f, RATE + 1] * spec_y[...]
             solve_y[c, f] = exact(sine_y[...] / denom, sine_y[...])
 
 
-def tables_y_kernel(pack, token, sine_y_in, spec_in, solve_y, sine_y, spec, sems):
-    for copy in fetch((sine_y_in, spec_in), (sine_y, spec), sems):
-        copy.wait()
-    ny = sine_y.shape[0]
+def tables_y_kernel(pack, token, sine_y, spec_y, solve_y):
     for c in range(2):
         for f in range(FIELDS):
-            denom = 1.0 + pack[c, f, RATE + 1] * spec[1:2, :ny]
+            denom = 1.0 + pack[c, f, RATE + 1] * spec_y[...]
             solve_y[c, f] = exact(sine_y[...] / denom, sine_y[...])
 
 
-def tables_b_kernel(info, pack, token, sine_z_in, left_in, right_in, right_2_in, spec_in,
-                    solve_x, ends_prev, ends_next, halo_prev, halo_next, solve_z, mixes,
-                    sine_z, left, right, right_2, spec, sems):
-    copies = fetch(
-        (sine_z_in, left_in, right_in, right_2_in, spec_in), (sine_z, left, right, right_2, spec), sems
-    )
+def tables_b_kernel(info, pack, token, outer, sine_z, spec_z, left, right, left_2, right_2, spec_x,
+                    solve_x, ends_prev, ends_next, halo_prev, halo_next, solve_z, mixes):
     mine = info[1]
     for f in range(FIELDS):
         for g in range(FIELDS):
@@ -129,8 +126,6 @@
             mixes[0, f, g] = near
             mixes[1, f, g] = far
         mixes[2, f, 0] = pack[mine, f, RATE + 1]
-    for copy in copies:
-        copy.wait()
     n, nx = left.shape
     row, col = (lax.broadcasted_iota(jnp.int32, (n, n), i) for i in range(2))
     same = (row & 7) == (col & 7)
@@ -141,18 +136,24 @@
     from_last = ((row & 1) == 0) & ((col & 1) == 1)
     from_first = ((row & 1) == 1) & ((col & 1) == 0)
     for f in range(FIELDS):
-        denom = 1.0 + pack[mine, f, RATE] * spec[2:3, :nx]
+        denom = 1.0 + pack[mine, f, RATE] * spec_x[...]
         scaled = left[...] / denom
         solve_x[f] = jnp.where(same, exact(scaled, right[...]), 0.0)
-        scaled_2 = right_2[...].T / denom
+        scaled_2 = left_2[...] / denom
         both = exact(scaled_2, right[...])
         ends_prev[f] = jnp.where(prev_rows, both, 0.0)
         ends_next[f] = jnp.where(next_rows, both, 0.0)
         both = exact(scaled_2, right_2[...])
         halo_prev[f] = jnp.where(from_last, both, 0.0)
         halo_next[f] = jnp.where(from_first, both, 0.0)
-        denom = 1.0 + pack[mine, f, RATE + 2] * spec[0:1]
+        denom = 1.0 + pack[mine, f, RATE + 2] * spec_z[...]
         solve_z[f] = exact(sine_z[...] / denom, sine_z[...])
+
+
+def planes_kernel(info, adjoint, outer, inner, sems):
+    me = info[0]
+    for copy in fetch((adjoint.at[:, :, me], adjoint.at[:, :, 1 - me]), (outer, inner), sems):
+        copy.wait()
 
 
 def first_kernel(info, pack, adjoint, other, source_in, radius, solve_z, solve_y, out, token,
@@ -170,7 +171,7 @@
             for f in range(FIELDS):
                 v = adjoint[c, f, x]
                 beside = adjoint[c, f, 1 - x]
-                beside = beside + (other[c, f, 1] * before if x == 0 else other[c, f, 0] * after)
+                beside = beside + other[c, f] * (before if x == 0 else after)
                 beside = beside + shifted(v, 0, 1) + shifted(v, 0, -1)
                 beside = beside + shifted(v, 1, 1) + shifted(v, 1, -1)
                 lapped[x, f] = 6.0 * v - beside
@@ -336,12 +337,12 @@
 def terms_kernel(info, pack, mine, other, inside, out):
     me = info[0]
     ny = mine.shape[2]
-    each = out.shape[1] // 8
+    each = out.shape[1]
 
     def store(k, x, v):
-        for i in range(ny // 8):
-            piece, at = divmod((k * 2 + x) * (ny // 8) + i, each)
-            out[piece, 8 * at : 8 * at + 8] = v[8 * i : 8 * i + 8]
+        for i in range(ny // 4):
+            piece, at = divmod((k * 2 + x) * (ny // 4) + i, each)
+            out[piece, at] = v[4 * i : 4 * i + 4]
 
     total = 0.0
     for c in range(2):
@@ -352,9 +353,9 @@
     for k in range(1, 3):
         for x in range(2):
             store(k, x, inside[k, x])
-    for tile in range(6 * ny // 8, out.shape[0] * each):
-        piece, at = divmod(tile, each)
-        out[piece, 8 * at : 8 * at + 8] = jnp.zeros((8, out.shape[2]), F32)
+    for i in range(6 * ny // 4, out.shape[0] * each):
+        piece, at = divmod(i, each)
+        out[piece, at] = jnp.zeros(out.shape[2:], F32)
 
 
 def sum_kernel(scale, pieces, out):
@@ -394,44 +395,44 @@
     cores = [(i, i ^ 1) for i in range(peers)]
     chips = [(i, i + 1) for i in range(1, peers - 1, 2)]
     chips = chips + [(j, i) for i, j in chips]
-    other = lax.ppermute(adjoint_start, "grid", cores)
-    outer = lax.dynamic_index_in_dim(adjoint_start, core, 2, keepdims=False)
+    outer, other = call(
+        planes_kernel,
+        (shape(2, fields, ny, nz), shape(2, fields, ny, nz)),
+        [SMEM, ANY],
+        1000,
+        "planes",
+        [sems(2)],
+        (ANY, ANY),
+    )(info, adjoint_start)
+    other = lax.ppermute(other, "grid", cores)
     outer = lax.ppermute(outer, "grid", chips)
 
-    sine_z, spec_z = sine_tables(nz)
-    sine_y, spec_y = sine_tables(ny)
-    sine_x, spec_x = sine_tables(nx)
-    spec = np.zeros((8, nz), np.float32)
-    spec[0], spec[1, :ny], spec[2, :nx] = spec_z, spec_y, spec_x
-    left_x = np.repeat(sine_x, 8, axis=0)
-    right_2 = np.repeat(sine_x, 2, axis=0).T.copy()
-    spec, sine_z, sine_y = jnp.asarray(spec), jnp.asarray(sine_z), jnp.asarray(sine_y)
+    sine_z, spec_z = sine_table(nz), spectrum(nz)
+    sine_y, spec_y = sine_table(ny), spectrum(ny)
 
     weights = condition_weights.astype(F32)[:, None, None]
-    pack = jnp.concatenate(
-        [
-            coupling,
-            left_vectors,
-            right_vectors,
-            implicit_scales,
-            jnp.swapaxes(sensitivity_map, 1, 2) * weights,
-        ],
-        axis=2,
-    )
+    pack = jnp.zeros((2, fields, 24), F32)
+    for at, part in (
+        (COUP, coupling),
+        (LEFT, left_vectors),
+        (RIGHT, right_vectors),
+        (RATE, implicit_scales),
+        (SENS, jnp.swapaxes(sensitivity_map, 1, 2) * weights),
+    ):
+        pack = pack + jnp.pad(part, ((0, 0), (0, 0), (at, 24 - at - part.shape[2])))
 
     solve_z, solve_y = call(
         tables_kernel,
         (shape(2, fields, nz, nz), shape(2, fields, ny, ny)),
-        [SMEM, ANY, ANY, ANY],
+        [SMEM] + [VMEM] * 4,
         100_000_000,
         "solve_tables",
-        [vmem(nz, nz), vmem(ny, ny), vmem(8, nz), sems(3)],
-    )(pack, sine_z, sine_y, spec)
+    )(pack, sine_z, spec_z, sine_y, spec_y)
 
     lines, token = call(
         first_kernel,
         (shape(blocks // 2, 2, 2, 3 * fields + planes, 8, nz), shape(8, nz)),
-        [SMEM, SMEM, VMEM, VMEM, ANY, VMEM, VMEM, VMEM],
+        [SMEM, SMEM, VMEM, VMEM, HBM, VMEM, VMEM, VMEM],
         200_000_000,
         "first_residual",
         [
@@ -459,12 +460,15 @@
             shape(fields, nz, nz),
             shape(3, fields, fields),
         ),
-        [SMEM, SMEM, VMEM] + [ANY] * 5,
+        [SMEM, SMEM, VMEM, ANY] + [VMEM] * 7,
         100_000_000,
         "tables_b",
-        [vmem(nz, nz), vmem(rows_b, nx), vmem(nx, rows_b), vmem(nx, 2 * nx), vmem(8, nz), sems(5)],
+        (),
         (VMEM,) * 6 + (SMEM,),
-    )(info, pack, token, sine_z, jnp.asarray(left_x), jnp.asarray(left_x.T.copy()), jnp.asarray(right_2), spec)
+    )(
+        info, pack, token, outer, sine_z, spec_z,
+        sine_table(nx, 8, 1), sine_table(nx, 1, 8), sine_table(nx, 2, 1), sine_table(nx, 1, 2), spectrum(nx),
+    )
 
     to_prev, to_next = call(
         ends_kernel,
@@ -503,11 +507,10 @@
     solve_y = call(
         tables_y_kernel,
         shape(2, fields, ny, ny),
-        [SMEM, VMEM, ANY, ANY],
+        [SMEM, VMEM, VMEM, VMEM],
         50_000_000,
         "tables_y",
-        [vmem(ny, ny), vmem(8, nz), sems(2)],
-    )(pack, token, sine_y, spec)
+    )(pack, token, sine_y, spec_y)
 
     adjoint, mine = call(
         update_kernel,
@@ -529,11 +532,11 @@
         [vmem(fields, ny, nz)],
     )(info, pack, adjoint, outer, step, solve_y)
 
-    tiles = 3 * planes * ny // 8
+    tiles = 3 * planes * ny // 4
     each = -(-tiles // conds)
     pieces = call(
         terms_kernel,
-        shape(conds, each * 8, nz),
+        shape(conds, each, 4, nz),
         [SMEM, SMEM] + [VMEM] * 3,
         10_000_000,
         "terms",
@@ -542,13 +545,13 @@
     scale = 1.0 / (conds * condition_weights.shape[0])
     pieces = call(
         functools.partial(sum_kernel, scale),
-        shape(conds, each * 8, nz),
+        shape(conds, each, 4, nz),
         [VMEM],
         1_000_000,
         "sum_conditions",
     )(pieces)
     pieces = lax.all_to_all(pieces, "cond", 0, 0, tiled=True)
-    total = pieces.reshape(conds * each * 8, nz)[: tiles * 8].reshape(3, planes, ny, nz)
+    total = pieces.reshape(conds * each * 4, nz)[: tiles * 4].reshape(3, planes, ny, nz)
     return (adjoint, total)
 
 

time: 158 us -> 171 us (1.082)
  the two profiles are of different devices: /device:TPU:2 before, /device:TPU:1 now
where the time goes in v5:
time: 171 us; the launch traced here: 170 us
  waiting for transfers between devices  51.8 us (30%)
  blocking collectives  47.1 us (28%)
  starting transfers between devices  33 us (19%)
  Pallas kernels  21.7 us (13%)
  local copies, waits for them, and re-layouts  13.2 us (8%)
  other arithmetic  2.71 us (2%)
    all_to_all x2, blocking collectives, body(): pieces = lax.all_to_all(pieces, 'cond', 0, 0, tiled=True)  47.1 us
    ppermute x1, waiting for transfers between devices, body(): outer = lax.ppermute(outer, 'grid', chips)  30.7 us
    all_to_all x1, waiting for transfers between devices, body(): step = lax.all_to_all(step, 'grid', 0, 0, tiled=True)  18 us
    unnamed x36, local copies, waits for them, and re-layouts  13.1 us
    ppermute x1, starting transfers between devices, body(): other = lax.ppermute(other, 'grid', cores)  8.79 us
    ppermute x1, starting transfers between devices, body(): outer = lax.ppermute(outer, 'grid', chips)  7.44 us
    all_to_all x1, starting transfers between devices, body(): step = lax.all_to_all(step, 'grid', 0, 0, tiled=True)  4.53 us
    all_to_all x1, starting transfers between devices, body(): lines = lax.all_to_all(lines, 'grid', 0, 0, tiled=True)  4.33 us
  transfers between devices with their start and end apart: 7, of which 3 were waited for; matrix products, arithmetic and copies ran while one was open for 4% of the time, Pallas kernels for 7%

profile of v5, /device:TPU:1, one launch (start us, length us, event | category | flops | bytes accessed | tf_op | source)
XLA Modules:
  0.0 170.4 jit_solution(6085854598740946144)
XLA Ops:
  0.8 1.1 copy-done
  2.5 8.8 %collective-permute-start = (f32[2,5,64,128]{3,2,1,0:T(8,128)S(1)}, f32[2,5,64,128]{3,2,1,0:T(8,128)S(1)}, u32[]{:S(2)}, u32[]{:S(2)}) collective-permute-start(f32[2,5,64,128]{3,2,1,0:T(8,128)S(1)} %get-tuple-element.21), channel_id=1, source_target_pairs={{0,1},{1,0},{2,3},{3,2},{4,5},{5,4},{6,7},{7,6},{8,9},{9,8},{10,11... | collective-permute-start | bytes 983048 | tf_op jit(solution)/shard_map/ppermute | solution.py:407
  16.4 1.6 solve_tables.1
  18.1 1.1 copy-done.4
  19.2 3.8 %first_residual.1 = (f32[4,2,2,17,8,128]{5,4,3,2,1,0:T(8,128)}, f32[8,128]{1,0:T(8,128)S(1)}) custom-call(s32[4]{0:T(128)S(1)} %pad_add_fusion.1.info, f32[2,5,24]{2,1,0:T(8,128)S(1)} %pad_add_fusion.pack, f32[2,5,2,64,128]{4,3,2,1,0:T(8,128)S(1)} %copy-done.1, f32[2,5,64,128]{3,2,1,0:T(8,128)S(1)} %collective-permute-done.other, ...), custom_call_target="tpu_custom_call" | custom-call | flops 200000000 | bytes 4000000 | tf_op jit(solution)/shard_map/first_residual/pallas_call | solution.py:432
  22.9 4.3 %all-to-all-start = ((f32[16,17,8,128]{3,2,1,0:T(8,128)}), f32[16,17,8,128]{3,2,1,0:T(8,128)S(1)}, u32[]{:S(2)}, u32[]{:S(2)}) async-start(f32[16,17,8,128]{3,2,1,0:T(8,128)} %bitcast.5), calls=%async_computation | async-start | bytes 2228224 | tf_op jit(solution)/shard_map/all_to_all | solution.py:450
  27.3 7.4 %collective-permute-start.1 = (f32[2,5,64,128]{3,2,1,0:T(8,128)S(1)}, f32[2,5,64,128]{3,2,1,0:T(8,128)S(1)}, u32[]{:S(2)}, u32[]{:S(2)}) collective-permute-start(f32[2,5,64,128]{3,2,1,0:T(8,128)S(1)} %get-tuple-element.25), channel_id=1, source_target_pairs={{1,2},{3,4},{5,6},{7,8},{9,10},{11,12},{13,14},{2,1},{4,3},{6,5},{... | collective-permute-start | bytes 983048 | tf_op jit(solution)/shard_map/ppermute | solution.py:408
  36.0 30.7 %collective-permute-done.1.outer.start_outer = f32[2,5,64,128]{3,2,1,0:T(8,128)S(1)} collective-permute-done((f32[2,5,64,128]{3,2,1,0:T(8,128)S(1)}, f32[2,5,64,128]{3,2,1,0:T(8,128)S(1)}, u32[]{:S(2)}, u32[]{:S(2)}) %collective-permute-start.1) | collective-permute-done | bytes 327712 | tf_op jit(solution)/shard_map/ppermute | solution.py:408
  66.8 4.2 %tables_b.1 = (f32[5,256,256]{2,1,0:T(8,128)S(1)}, f32[5,64,256]{2,1,0:T(8,128)S(1)}, f32[5,64,256]{2,1,0:T(8,128)S(1)}, f32[5,64,64]{2,1,0:T(8,128)S(1)}, f32[5...) custom-call(s32[4]{0:T(128)S(1)} %pad_add_fusion.1.info, ...), custom_call_target="tpu_custom_call" | custom-call | flops 100000000 | bytes 4000000 | tf_op jit(solution)/shard_map/tables_b/pallas_call | solution.py:452
  74.5 1.0 copy-done.7
  76.9 3.2 %collective-permute-start.2 = (f32[5,64,128]{2,1,0:T(8,128)S(1)}, f32[5,64,128]{2,1,0:T(8,128)S(1)}, u32[]{:S(2)}, u32[]{:S(2)}) collective-permute-start(f32[5,64,128]{2,1,0:T(8,128)S(1)} %get-tuple-element.32), channel_id=1, source_target_pairs={{0,1},{1,4},{4,5},{5,8},{8,9},{9,12},{12,13},{2,3},{3,6},{6,7},{7,... | collective-permute-start | bytes 491528 | tf_op jit(solution)/shard_map/ppermute | solution.py:483
  80.1 1.9 %collective-permute-start.3 = (f32[5,64,128]{2,1,0:T(8,128)S(1)}, f32[5,64,128]{2,1,0:T(8,128)S(1)}, u32[]{:S(2)}, u32[]{:S(2)}) collective-permute-start(f32[5,64,128]{2,1,0:T(8,128)S(1)} %get-tuple-element.33), channel_id=1, source_target_pairs={{1,0},{4,1},{5,4},{8,5},{9,8},{12,9},{13,12},{3,2},{6,3},{7,6},{10... | collective-permute-start | bytes 491528 | tf_op jit(solution)/shard_map/ppermute | solution.py:484
  82.0 3.7 %second_residual.1.local = f32[5,32,8,128]{3,2,1,0:T(8,128)S(1)} custom-call(s32[4]{0:T(128)S(1)} %pad_add_fusion.1.info, f32[3,5,5]{2,1,0:T(8,128)S(1)} %get-tuple-element.26.mixes, f32[16,17,8,128]{3,2,1,0:T(8,128)S(1)} %all-to-all-done.lines, f32[5,256,256]{2,1,0:T(8,128)S(1)} %get-tuple-element.28.solve_x, f32[5,128,128]{2,1,0:T(8,128)S(1)} %copy-done.3), custom_call_target="tpu_custom_call" | custom-call | flops 300000000 | bytes 4000000 | tf_op jit(solution)/shard_map/second_residual/pallas_call | solution.py:486
  85.7 3.0 %collective-permute-done.3.from_next = f32[5,64,128]{2,1,0:T(8,128)S(1)} collective-permute-done((f32[5,64,128]{2,1,0:T(8,128)S(1)}, f32[5,64,128]{2,1,0:T(8,128)S(1)}, u32[]{:S(2)}, u32[]{:S(2)}) %collective-permute-start.3) | collective-permute-done | bytes 163872 | tf_op jit(solution)/shard_map/ppermute | solution.py:484
  88.8 2.2 %halo_rows.1 = (f32[16,15,8,128]{3,2,1,0:T(8,128)}, f32[8,128]{1,0:T(8,128)S(1)}) custom-call(f32[3,5,5]{2,1,0:T(8,128)S(1)} %get-tuple-element.26.mixes, f32[5,32,8,128]{3,2,1,0:T(8,128)S(1)} %second_residual.1.local, f32[5,64,128]{2,1,0:T(8,128)S(1)} %collective-permute-done.2.from_prev, f32[5,64,128]{2,1,0:T(8,128)S(1)} %collective-permute-done.3.from_next, ...), custom_call_target="tpu_custom_call" | custom-call | flops 50000000 | bytes 4000000 | tf_op jit(solution)/shard_map/halo_rows/pallas_call | solution.py:495
  91.0 4.5 %all-to-all-start.1 = ((f32[16,15,8,128]{3,2,1,0:T(8,128)}), f32[16,15,8,128]{3,2,1,0:T(8,128)S(1)}, u32[]{:S(2)}, u32[]{:S(2)}) async-start(f32[16,15,8,128]{3,2,1,0:T(8,128)} %get-tuple-element.36), calls=%async_computation.1 | async-start | bytes 1966080 | tf_op jit(solution)/shard_map/all_to_all | solution.py:505
  95.5 1.1 tables_y.1.solve_y
  96.6 18.0 %all-to-all-done.1.solved = f32[16,15,8,128]{3,2,1,0:T(8,128)S(1)} async-done(((f32[16,15,8,128]{3,2,1,0:T(8,128)}), f32[16,15,8,128]{3,2,1,0:T(8,128)S(1)}, u32[]{:S(2)}, u32[]{:S(2)}) %all-to-all-start.1) | async-done | bytes 983072 | tf_op jit(solution)/shard_map/all_to_all | solution.py:505
  114.6 2.0 %update.1 = (f32[2,5,2,64,128]{4,3,2,1,0:T(8,128)}, f32[2,5,64,128]{3,2,1,0:T(8,128)S(1)}) custom-call(s32[4]{0:T(128)S(1)} %pad_add_fusion.1.info, f32[2,5,24]{2,1,0:T(8,128)S(1)} %pad_add_fusion.pack, f32[2,5,2,64,128]{4,3,2,1,0:T(8,128)S(1)} %copy-done.1, f32[16,15,8,128]{3,2,1,0:T(8,128)S(1)} %all-to-all-done.1.solved, f32[2,5,64,64]{3,2,1,0:T(8,128)S(1)} %tables_y.1.solve_y), custom_call_target="tpu_custom_call" | custom-call | flops 60000000 | bytes 4000000 | tf_op jit(solution)/shard_map/update/pallas_call | solution.py:515
  116.6 2.8 %collective-permute-start.4 = (f32[2,5,64,128]{3,2,1,0:T(8,128)S(1)}, f32[2,5,64,128]{3,2,1,0:T(8,128)S(1)}, u32[]{:S(2)}, u32[]{:S(2)}) collective-permute-start(f32[2,5,64,128]{3,2,1,0:T(8,128)S(1)} %get-tuple-element.39.mine), channel_id=1, source_target_pairs={{0,1},{1,0},{2,3},{3,2},{4,5},{5,4},{6,7},{7,6},{8,9},{9,8},{10,11... | collective-permute-start | bytes 983048 | tf_op jit(solution)/shard_map/ppermute | solution.py:524
  119.4 1.1 copy-done.5
  120.4 1.3 inside_terms.1.inside
  122.5 32.7 %all_to_all.20.pieces = f32[32,3,4,128]{3,2,1,0:T(4,128)S(1)} all-to-all(f32[32,3,4,128]{3,2,1,0:T(4,128)S(1)} %terms.1), channel_id=1, replica_groups=mesh['cond'=32,'grid'=16] {'cond'}, dimensions={0} | all-to-all | bytes 393216 | tf_op jit(solution)/shard_map/all_to_all | solution.py:544
  155.3 14.3 %all_to_all.21 = f32[32,3,4,128]{3,2,1,0:T(4,128)S(1)} all-to-all(f32[32,3,4,128]{3,2,1,0:T(4,128)S(1)} %sum_conditions.1), channel_id=1, replica_groups=mesh['cond'=32,'grid'=16] {'cond'}, dimensions={0} | all-to-all | bytes 393216 | tf_op jit(solution)/shard_map/all_to_all | solution.py:553
  (60 shorter events, 13.4 us)
Async XLA Ops:
  0.6 17.4 %copy-start.14 = (f32[2,64,128]{2,1,0:T(8,128)S(1)}, f32[2,64,128]{2,1,0:T(8,128)}, u32[]{:S(2)}) copy-start(f32[2,64,128]{2,1,0:T(8,128)} %radius.1) | copy-start | bytes 196612
  0.8 1.1 copy-start
  1.9 16.2 %copy-start.1 = (f32[2,5,2,64,128]{4,3,2,1,0:T(8,128)S(1)}, f32[2,5,2,64,128]{4,3,2,1,0:T(8,128)}, u32[]{:S(2)}) copy-start(f32[2,5,2,64,128]{4,3,2,1,0:T(8,128)} %adjoint.5) | copy-start | bytes 1966084
  2.5 15.6 %collective-permute-start = (f32[2,5,64,128]{3,2,1,0:T(8,128)S(1)}, f32[2,5,64,128]{3,2,1,0:T(8,128)S(1)}, u32[]{:S(2)}, u32[]{:S(2)}) collective-permute-start(f32[2,5,64,128]{3,2,1,0:T(8,128)S(1)} %get-tuple-element.21), channel_id=1, source_target_pairs={{0,1},{1,0},{2,3},{3,2},{4,5},{5,4},{6,7},{7,6},{8,9},{9,8},{10,11... | collective-permute-start | bytes 983048 | tf_op jit(solution)/shard_map/ppermute | solution.py:407
  18.1 1.1 copy-start.4
  22.9 51.5 %all-to-all-start = ((f32[16,17,8,128]{3,2,1,0:T(8,128)}), f32[16,17,8,128]{3,2,1,0:T(8,128)S(1)}, u32[]{:S(2)}, u32[]{:S(2)}) async-start(f32[16,17,8,128]{3,2,1,0:T(8,128)} %bitcast.5), calls=%async_computation | async-start | bytes 2228224 | tf_op jit(solution)/shard_map/all_to_all | solution.py:450
  27.3 39.5 %collective-permute-start.1 = (f32[2,5,64,128]{3,2,1,0:T(8,128)S(1)}, f32[2,5,64,128]{3,2,1,0:T(8,128)S(1)}, u32[]{:S(2)}, u32[]{:S(2)}) collective-permute-start(f32[2,5,64,128]{3,2,1,0:T(8,128)S(1)} %get-tuple-element.25), channel_id=1, source_target_pairs={{1,2},{3,4},{5,6},{7,8},{9,10},{11,12},{13,14},{2,1},{4,3},{6,5},{... | collective-permute-start | bytes 983048 | tf_op jit(solution)/shard_map/ppermute | solution.py:408
  70.9 0.7 copy-start.2
  71.7 0.7 copy-start.6
  72.4 0.7 copy-start.8
  73.1 0.7 copy-start.10
  73.8 0.7 copy-start.12
  74.4 7.5 %copy-start.3 = (f32[5,128,128]{2,1,0:T(8,128)S(1)}, f32[5,128,128]{2,1,0:T(8,128)}, u32[]{:S(2)}) copy-start(f32[5,128,128]{2,1,0:T(8,128)} %copy-done.2) | copy-start | bytes 983044
  74.5 1.0 copy-start.7
  75.5 1.0 copy-start.9
  76.9 8.9 %collective-permute-start.2 = (f32[5,64,128]{2,1,0:T(8,128)S(1)}, f32[5,64,128]{2,1,0:T(8,128)S(1)}, u32[]{:S(2)}, u32[]{:S(2)}) collective-permute-start(f32[5,64,128]{2,1,0:T(8,128)S(1)} %get-tuple-element.32), channel_id=1, source_target_pairs={{0,1},{1,4},{4,5},{5,8},{8,9},{9,12},{12,13},{2,3},{3,6},{6,7},{7,... | collective-permute-start | bytes 491528 | tf_op jit(solution)/shard_map/ppermute | solution.py:483
  80.1 8.7 %collective-permute-start.3 = (f32[5,64,128]{2,1,0:T(8,128)S(1)}, f32[5,64,128]{2,1,0:T(8,128)S(1)}, u32[]{:S(2)}, u32[]{:S(2)}) collective-permute-start(f32[5,64,128]{2,1,0:T(8,128)S(1)} %get-tuple-element.33), channel_id=1, source_target_pairs={{1,0},{4,1},{5,4},{8,5},{9,8},{12,9},{13,12},{3,2},{6,3},{7,6},{10... | collective-permute-start | bytes 491528 | tf_op jit(solution)/shard_map/ppermute | solution.py:484
  82.0 6.8 %copy-start.11 = (f32[5,64,64]{2,1,0:T(8,128)S(1)}, f32[5,64,64]{2,1,0:T(8,128)}, u32[]{:S(2)}) copy-start(f32[5,64,64]{2,1,0:T(8,128)} %copy-done.10) | copy-start | bytes 245764
  82.0 6.8 %copy-start.13 = (f32[5,64,64]{2,1,0:T(8,128)S(1)}, f32[5,64,64]{2,1,0:T(8,128)}, u32[]{:S(2)}) copy-start(f32[5,64,64]{2,1,0:T(8,128)} %copy-done.12) | copy-start | bytes 245764
  91.0 23.6 %all-to-all-start.1 = ((f32[16,15,8,128]{3,2,1,0:T(8,128)}), f32[16,15,8,128]{3,2,1,0:T(8,128)S(1)}, u32[]{:S(2)}, u32[]{:S(2)}) async-start(f32[16,15,8,128]{3,2,1,0:T(8,128)} %get-tuple-element.36), calls=%async_computation.1 | async-start | bytes 1966080 | tf_op jit(solution)/shard_map/all_to_all | solution.py:505
  116.6 5.2 %collective-permute-start.4 = (f32[2,5,64,128]{3,2,1,0:T(8,128)S(1)}, f32[2,5,64,128]{3,2,1,0:T(8,128)S(1)}, u32[]{:S(2)}, u32[]{:S(2)}) collective-permute-start(f32[2,5,64,128]{3,2,1,0:T(8,128)S(1)} %get-tuple-element.39.mine), channel_id=1, source_target_pairs={{0,1},{1,0},{2,3},{3,2},{4,5},{5,4},{6,7},{7,6},{8,9},{9,8},{10,11... | collective-permute-start | bytes 983048 | tf_op jit(solution)/shard_map/ppermute | solution.py:524
  119.3 1.1 copy-start.5

commit v6 on v5

--- a/solution.py
+++ b/solution.py
@@ -15,7 +15,6 @@
 LIMIT = 20 * 1024 * 1024
 ANY = pl.BlockSpec(memory_space=pl.ANY)
 HBM = pl.BlockSpec(memory_space=pltpu.HBM)
-COUP, LEFT, RIGHT, RATE, SENS = 0, 5, 10, 15, 18
 
 
 def split(v):
@@ -95,37 +94,37 @@
     return (b // 2) * 4 + c * 2 + b % 2
 
 
-def tables_kernel(pack, sine_z, spec_z, sine_y, spec_y, solve_z, solve_y):
+def tables_kernel(rates, sine_z, spec_z, sine_y, spec_y, solve_z, solve_y):
     for c in range(2):
         for f in range(FIELDS):
-            denom = 1.0 + pack[c, f, RATE + 2] * spec_z[...]
+            denom = 1.0 + rates[2, c, f] * spec_z[...]
             solve_z[c, f] = exact(sine_z[...] / denom, sine_z[...])
-            denom = 1.0 + pack[c, f, RATE + 1] * spec_y[...]
+            denom = 1.0 + rates[1, c, f] * spec_y[...]
             solve_y[c, f] = exact(sine_y[...] / denom, sine_y[...])
 
 
-def tables_y_kernel(pack, token, sine_y, spec_y, solve_y):
+def tables_y_kernel(rates, token, sine_y, spec_y, solve_y):
     for c in range(2):
         for f in range(FIELDS):
-            denom = 1.0 + pack[c, f, RATE + 1] * spec_y[...]
+            denom = 1.0 + rates[1, c, f] * spec_y[...]
             solve_y[c, f] = exact(sine_y[...] / denom, sine_y[...])
 
 
-def tables_b_kernel(info, pack, token, outer, sine_z, spec_z, left, right, left_2, right_2, spec_x,
+def tables_b_kernel(info, coup, left_map, right_map, rates, token, sine_z, spec_z, left, right, left_2, right_2, spec_x,
                     solve_x, ends_prev, ends_next, halo_prev, halo_next, solve_z, mixes):
     mine = info[1]
     for f in range(FIELDS):
         for g in range(FIELDS):
             near, far = 0.0, 0.0
             for h in range(FIELDS):
-                near = near + pack[mine, f, LEFT + h] * pack[mine, h, RIGHT + g]
+                near = near + left_map[f, mine, h] * right_map[h, mine, g]
                 inner = 0.0
                 for i in range(FIELDS):
-                    inner = inner + pack[mine, h, COUP + i] * pack[mine, i, RIGHT + g]
-                far = far + pack[mine, f, LEFT + h] * inner
+                    inner = inner + coup[h, mine, i] * right_map[i, mine, g]
+                far = far + left_map[f, mine, h] * inner
             mixes[0, f, g] = near
             mixes[1, f, g] = far
-        mixes[2, f, 0] = pack[mine, f, RATE + 1]
+        mixes[2, f, 0] = rates[1, mine, f]
     n, nx = left.shape
     row, col = (lax.broadcasted_iota(jnp.int32, (n, n), i) for i in range(2))
     same = (row & 7) == (col & 7)
@@ -136,7 +135,7 @@
     from_last = ((row & 1) == 0) & ((col & 1) == 1)
     from_first = ((row & 1) == 1) & ((col & 1) == 0)
     for f in range(FIELDS):
-        denom = 1.0 + pack[mine, f, RATE] * spec_x[...]
+        denom = 1.0 + rates[0, mine, f] * spec_x[...]
         scaled = left[...] / denom
         solve_x[f] = jnp.where(same, exact(scaled, right[...]), 0.0)
         scaled_2 = left_2[...] / denom
@@ -146,17 +145,17 @@
         both = exact(scaled_2, right_2[...])
         halo_prev[f] = jnp.where(from_last, both, 0.0)
         halo_next[f] = jnp.where(from_first, both, 0.0)
-        denom = 1.0 + pack[mine, f, RATE + 2] * spec_z[...]
+        denom = 1.0 + rates[2, mine, f] * spec_z[...]
         solve_z[f] = exact(sine_z[...] / denom, sine_z[...])
 
 
-def planes_kernel(info, adjoint, outer, inner, sems):
-    me = info[0]
-    for copy in fetch((adjoint.at[:, :, me], adjoint.at[:, :, 1 - me]), (outer, inner), sems):
-        copy.wait()
-
-
-def first_kernel(info, pack, adjoint, other, source_in, radius, solve_z, solve_y, out, token,
+def plane_kernel(info, adjoint, inner, sem):
+    copy = pltpu.make_async_copy(adjoint.at[:, :, 1 - info[0]], inner, sem)
+    copy.start()
+    copy.wait()
+
+
+def first_kernel(info, coup, left, adjoint, other, source_in, radius, solve_z, solve_y, out, token,
                  source, made, lapped, stage, sems, out_sems):
     copies = fetch([source_in.at[c] for c in range(2)], [source.at[c] for c in range(2)], sems)
     ny = adjoint.shape[3]
@@ -182,14 +181,14 @@
             for f in range(FIELDS):
                 r = source[c, f, x] - sr * adjoint[c, f, x]
                 for g in range(FIELDS):
-                    r = r - pack[c, f, COUP + g] * lapped[x, g]
+                    r = r - coup[f, c, g] * lapped[x, g]
                 residual.append(r)
             for f in range(FIELDS):
-                stage[f, x * ny : x * ny + ny] = mixed(lambda g: pack[c, f, LEFT + g], residual)
+                stage[f, x * ny : x * ny + ny] = mixed(lambda g: left[f, c, g], residual)
         outer = [adjoint[c, g, me] for g in range(FIELDS)]
-        outer = [mixed(lambda g: pack[c, f, COUP + g], outer) for f in range(FIELDS)]
-        for f in range(FIELDS):
-            stage[f, 2 * ny : 3 * ny] = mixed(lambda g: pack[c, f, LEFT + g], outer)
+        outer = [mixed(lambda g: coup[f, c, g], outer) for f in range(FIELDS)]
+        for f in range(FIELDS):
+            stage[f, 2 * ny : 3 * ny] = mixed(lambda g: left[f, c, g], outer)
         for f in range(FIELDS):
             r = dot(stage[f], solve_z[c, f])
             r = jnp.concatenate([r[p * ny : p * ny + ny] for p in range(3)], axis=1)
@@ -255,7 +254,6 @@
     full = (nx, 8, 128)
     row = lax.broadcasted_iota(jnp.int32, full, 1)
     odd = (lax.broadcasted_iota(jnp.int32, (2 * nx, 128), 0) & 1) == 1
-    zero = jnp.zeros((1, 8, 128), F32)
     token[...] = jnp.zeros(token.shape, F32)
     stores = []
     for f in range(FIELDS):
@@ -276,13 +274,8 @@
         q = local[f] + jnp.where(
             row < 2, spread(add_prev, 0), jnp.where(row >= 6, spread(add_next, 6), 0.0)
         )
-        chips = q.reshape(nx // 4, 4, 8, 128)
-        outer_0 = jnp.concatenate([zero, chips[:-1, 3]], axis=0)
-        outer_1 = jnp.concatenate([chips[1:, 0], zero], axis=0)
-        made[:, 3 * f : 3 * f + 3] = jnp.stack(
-            [chips[:, 0], chips[:, 1], outer_0, chips[:, 2], chips[:, 3], outer_1], axis=1
-        ).reshape(nx // 2, 3, 8, 128)
-        part = pl.ds(3 * f, 3)
+        made[:, 2 * f : 2 * f + 2] = q.reshape(nx // 2, 2, 8, 128)
+        part = pl.ds(2 * f, 2)
         stores.append(pltpu.make_async_copy(made.at[:, part], out.at[:, part], sems.at[f]))
         stores[-1].start()
     for copy in stores:
@@ -293,39 +286,32 @@
     return jnp.concatenate([solved[spot(c, b), tile] for b in range(blocks)], axis=0)
 
 
-def update_kernel(info, pack, adjoint, solved, solve_y, out, inner, step):
+def update_kernel(info, right, adjoint, solved, solve_y, out, inner, outer, step):
     ny = adjoint.shape[3]
     me = info[0]
     for c in range(2):
         for f in range(FIELDS):
-            q = jnp.concatenate([gathered(solved, c, 3 * f + x, ny // 8) for x in range(2)], axis=1)
+            q = jnp.concatenate([gathered(solved, c, 2 * f + x, ny // 8) for x in range(2)], axis=1)
             step[f] = dot(solve_y[c, f], q)
         steps = [[step[g, :, 128 * x : 128 * x + 128] for g in range(FIELDS)] for x in range(2)]
         for f in range(FIELDS):
-            planes = [
-                adjoint[c, f, x] + mixed(lambda g: pack[c, f, RIGHT + g], steps[x]) for x in range(2)
-            ]
+            planes = [adjoint[c, f, x] + mixed(lambda g: right[f, c, g], steps[x]) for x in range(2)]
             for x in range(2):
                 out[c, f, x] = planes[x]
             inner[c, f] = jnp.where(me == 0, planes[1], planes[0])
-
-
-def inside_kernel(info, pack, adjoint, start_outer, solved, solve_y, terms, step):
-    ny = adjoint.shape[3]
-    me = info[0]
+            outer[c, f] = jnp.where(me == 0, planes[0], planes[1])
+
+
+def inside_kernel(smap, weights, adjoint, terms):
     totals = [[0.0, 0.0] for _ in range(3)]
     for c in range(2):
-        for f in range(FIELDS):
-            step[f] = dot(solve_y[c, f], gathered(solved, c, 3 * f + 2, ny // 8))
-        for f in range(FIELDS):
-            outer = start_outer[c, f] + mixed(lambda g: pack[c, f, RIGHT + g], step)
-            w = [pack[c, f, SENS + k] for k in range(3)]
+        weight = weights[c].astype(F32)
+        for f in range(FIELDS):
+            w = [weight * smap[k, c, f] for k in range(3)]
             v = [adjoint[c, f, x] for x in range(2)]
-            pair = v[0] * v[1]
-            edge = jnp.where(me == 0, v[0], v[1]) * outer
-            at_0, at_1 = jnp.where(me == 0, edge, 0.0), jnp.where(me == 0, 0.0, edge)
-            totals[0][0] += w[0] * (pair - at_0)
-            totals[0][1] += w[0] * (at_1 - pair)
+            pair = w[0] * (v[0] * v[1])
+            totals[0][0] += pair
+            totals[0][1] -= pair
             for x in range(2):
                 for k in range(2):
                     totals[k + 1][x] += w[k + 1] * (v[x] * (shifted(v[x], k, 1) - shifted(v[x], k, -1)))
@@ -334,9 +320,9 @@
             terms[k, x] = totals[k][x]
 
 
-def terms_kernel(info, pack, mine, other, inside, out):
+def terms_kernel(info, smap, weights, inner, other_inner, outer, other_outer, inside, out):
     me = info[0]
-    ny = mine.shape[2]
+    ny = inner.shape[2]
     each = out.shape[1]
 
     def store(k, x, v):
@@ -344,12 +330,15 @@
             piece, at = divmod((k * 2 + x) * (ny // 4) + i, each)
             out[piece, at] = v[4 * i : 4 * i + 4]
 
-    total = 0.0
+    with_core, with_chip = 0.0, 0.0
     for c in range(2):
-        for f in range(FIELDS):
-            total += pack[c, f, SENS] * (mine[c, f] * other[c, f])
-    store(0, 0, inside[0, 0] - jnp.where(me == 0, 0.0, total))
-    store(0, 1, inside[0, 1] + jnp.where(me == 0, total, 0.0))
+        weight = weights[c].astype(F32)
+        for f in range(FIELDS):
+            w = weight * smap[0, c, f]
+            with_core += w * (inner[c, f] * other_inner[c, f])
+            with_chip += w * (outer[c, f] * other_outer[c, f])
+    store(0, 0, inside[0, 0] - jnp.where(me == 0, with_chip, with_core))
+    store(0, 1, inside[0, 1] + jnp.where(me == 0, with_core, with_chip))
     for k in range(1, 3):
         for x in range(2):
             store(k, x, inside[k, x])
@@ -395,31 +384,24 @@
     cores = [(i, i ^ 1) for i in range(peers)]
     chips = [(i, i + 1) for i in range(1, peers - 1, 2)]
     chips = chips + [(j, i) for i, j in chips]
-    outer, other = call(
-        planes_kernel,
-        (shape(2, fields, ny, nz), shape(2, fields, ny, nz)),
+    other = call(
+        plane_kernel,
+        shape(2, fields, ny, nz),
         [SMEM, ANY],
         1000,
-        "planes",
-        [sems(2)],
-        (ANY, ANY),
+        "inner_plane",
+        [pltpu.SemaphoreType.DMA(())],
+        ANY,
     )(info, adjoint_start)
     other = lax.ppermute(other, "grid", cores)
-    outer = lax.ppermute(outer, "grid", chips)
 
     sine_z, spec_z = sine_table(nz), spectrum(nz)
     sine_y, spec_y = sine_table(ny), spectrum(ny)
 
-    weights = condition_weights.astype(F32)[:, None, None]
-    pack = jnp.zeros((2, fields, 24), F32)
-    for at, part in (
-        (COUP, coupling),
-        (LEFT, left_vectors),
-        (RIGHT, right_vectors),
-        (RATE, implicit_scales),
-        (SENS, jnp.swapaxes(sensitivity_map, 1, 2) * weights),
-    ):
-        pack = pack + jnp.pad(part, ((0, 0), (0, 0), (at, 24 - at - part.shape[2])))
+    coup, left_map, right_map, smap = (
+        jnp.swapaxes(v, 0, 1) for v in (coupling, left_vectors, right_vectors, sensitivity_map)
+    )
+    rates = jnp.transpose(implicit_scales, (2, 0, 1))
 
     solve_z, solve_y = call(
         tables_kernel,
@@ -427,12 +409,12 @@
         [SMEM] + [VMEM] * 4,
         100_000_000,
         "solve_tables",
-    )(pack, sine_z, spec_z, sine_y, spec_y)
+    )(rates, sine_z, spec_z, sine_y, spec_y)
 
     lines, token = call(
         first_kernel,
         (shape(blocks // 2, 2, 2, 3 * fields + planes, 8, nz), shape(8, nz)),
-        [SMEM, SMEM, VMEM, VMEM, HBM, VMEM, VMEM, VMEM],
+        [SMEM, SMEM, SMEM, VMEM, VMEM, HBM, VMEM, VMEM, VMEM],
         200_000_000,
         "first_residual",
         [
@@ -444,7 +426,7 @@
             sems(2),
         ],
         (ANY, VMEM),
-    )(info, pack, adjoint_start, other, adjoint_source, spectral_radius, solve_z, solve_y)
+    )(info, coup, left_map, adjoint_start, other, adjoint_source, spectral_radius, solve_z, solve_y)
 
     lines = lines.reshape(peers, 3 * fields + planes, 8, nz)
     lines = lax.all_to_all(lines, "grid", 0, 0, tiled=True)
@@ -460,13 +442,13 @@
             shape(fields, nz, nz),
             shape(3, fields, fields),
         ),
-        [SMEM, SMEM, VMEM, ANY] + [VMEM] * 7,
+        [SMEM] * 5 + [VMEM] * 8,
         100_000_000,
         "tables_b",
         (),
         (VMEM,) * 6 + (SMEM,),
     )(
-        info, pack, token, outer, sine_z, spec_z,
+        info, coup, left_map, right_map, rates, token, sine_z, spec_z,
         sine_table(nx, 8, 1), sine_table(nx, 1, 8), sine_table(nx, 2, 1), sine_table(nx, 1, 2), spectrum(nx),
     )
 
@@ -494,11 +476,11 @@
 
     step, token = call(
         halo_kernel,
-        (shape(peers, 3 * fields, 8, nz), shape(8, nz)),
+        (shape(peers, planes * fields, 8, nz), shape(8, nz)),
         [SMEM] + [VMEM] * 6,
         50_000_000,
         "halo_rows",
-        [vmem(peers, 3 * fields, 8, nz), sems(fields)],
+        [vmem(peers, planes * fields, 8, nz), sems(fields)],
         (ANY, VMEM),
     )(mixes, local, from_prev, from_next, halo_prev, halo_next, solve_zb)
 
@@ -510,37 +492,38 @@
         [SMEM, VMEM, VMEM, VMEM],
         50_000_000,
         "tables_y",
-    )(pack, token, sine_y, spec_y)
-
-    adjoint, mine = call(
+    )(rates, token, sine_y, spec_y)
+
+    slab = shape(2, fields, ny, nz)
+    adjoint, inner, outer = call(
         update_kernel,
-        (shape(2, fields, planes, ny, nz), shape(2, fields, ny, nz)),
+        (shape(2, fields, planes, ny, nz), slab, slab),
         [SMEM, SMEM] + [VMEM] * 3,
         60_000_000,
         "update",
         [vmem(fields, ny, 2 * nz)],
-    )(info, pack, adjoint_start, step, solve_y)
-
-    other = lax.ppermute(mine, "grid", cores)
+    )(info, right_map, adjoint_start, step, solve_y)
+
+    other_outer = lax.ppermute(outer, "grid", chips)
+    other_inner = lax.ppermute(inner, "grid", cores)
 
     inside = call(
         inside_kernel,
         shape(3, planes, ny, nz),
-        [SMEM, SMEM] + [VMEM] * 4,
+        [SMEM, SMEM, VMEM],
         60_000_000,
         "inside_terms",
-        [vmem(fields, ny, nz)],
-    )(info, pack, adjoint, outer, step, solve_y)
+    )(smap, condition_weights, adjoint)
 
     tiles = 3 * planes * ny // 4
     each = -(-tiles // conds)
     pieces = call(
         terms_kernel,
         shape(conds, each, 4, nz),
-        [SMEM, SMEM] + [VMEM] * 3,
+        [SMEM] * 3 + [VMEM] * 5,
         10_000_000,
         "terms",
-    )(info, pack, mine, other, inside)
+    )(info, smap, condition_weights, inner, other_inner, outer, other_outer, inside)
     pieces = lax.all_to_all(pieces, "cond", 0, 0, tiled=True)
     scale = 1.0 / (conds * condition_weights.shape[0])
     pieces = call(

time: 171 us -> 146 us (0.85)
  the two profiles are of different devices: /device:TPU:1 before, /device:TPU:2 now
where the time goes in v6:
time: 146 us
  blocking collectives  47 us (32%)
  waiting for transfers between devices  36.6 us (25%)
  starting transfers between devices  28.2 us (19%)
  Pallas kernels  21.1 us (14%)
  local copies, waits for them, and re-layouts  9.65 us (7%)
  other arithmetic  1.89 us (1%)
    all_to_all x2, blocking collectives, body(): pieces = lax.all_to_all(pieces, 'cond', 0, 0, tiled=True)  47 us
    all_to_all x1, waiting for transfers between devices, body(): lines = lax.all_to_all(lines, 'grid', 0, 0, tiled=True)  16.5 us
    all_to_all x1, waiting for transfers between devices, body(): step = lax.all_to_all(step, 'grid', 0, 0, tiled=True)  12.3 us
    all_to_all x1, starting transfers between devices, body(): lines = lax.all_to_all(lines, 'grid', 0, 0, tiled=True)  10.3 us
    unnamed x47, local copies, waits for them, and re-layouts  9.55 us
    ppermute x1, waiting for transfers between devices, body(): other_outer = lax.ppermute(outer, 'grid', chips)  7.81 us
    ppermute x1, starting transfers between devices, body(): other_outer = lax.ppermute(outer, 'grid', chips)  4.82 us
    pallas_call x1, Pallas kernels, body(): call(tables_b_kernel, (shape(fields, rows_b, rows_b), shape(fields, 2 * n...  4.28 us
  transfers between devices with their start and end apart: 7, of which 3 were waited for; matrix products, arithmetic and copies ran while one was open for 1% of the time, Pallas kernels for 8%

profile of v6, /device:TPU:2, one launch (start us, length us, event | category | flops | bytes accessed | tf_op | source)
XLA Modules:
  0.0 145.6 jit_solution(14131244807674637879)
XLA Ops:
  0.8 1.1 copy-done
  2.5 1.9 %collective-permute-start = (f32[2,5,64,128]{3,2,1,0:T(8,128)S(1)}, f32[2,5,64,128]{3,2,1,0:T(8,128)S(1)}, u32[]{:S(2)}, u32[]{:S(2)}) collective-permute-start(f32[2,5,64,128]{3,2,1,0:T(8,128)S(1)} %inner_plane.1), channel_id=1, source_target_pairs={{0,1},{1,0},{2,3},{3,2},{4,5},{5,4},{6,7},{7,6},{8,9},{9,8},{10,11... | collective-permute-start | bytes 983048 | tf_op jit(solution)/shard_map/ppermute | solution.py:396
  5.1 1.6 %solve_tables.1 = (f32[2,5,128,128]{3,2,1,0:T(8,128)S(1)}, f32[2,5,64,64]{3,2,1,0:T(8,128)S(1)}) custom-call(f32[3,2,5]{2,1,0:T(2,128)S(1)} %bitcast.19, f32[128,128]{1,0:T(8,128)S(1)} %fusion.3.sine_z, f32[1,128]{1,0:T(1,128)S(1)} %multiply_add_fusion.2.spec_z, f32[64,64]{1,0:T(8,128)S(1)} %fusion.10.sine_y, f32[1,64]{1,0:T(1,128)S(1)} %multiply_add_fusion.1.spec_y), custom_call_target="tpu_custom_call" | custom-call | flops 100000000 | bytes 4000000 | tf_op jit(solution)/shard_map/solve_tables/pallas_call | solution.py:406
  6.7 3.9 %first_residual.1 = (f32[4,2,2,17,8,128]{5,4,3,2,1,0:T(8,128)}, f32[8,128]{1,0:T(8,128)S(1)}) custom-call(s32[4]{0:T(128)S(1)} %pad_add_fusion.info, f32[5,2,5]{2,1,0:T(2,128)S(1)} %bitcast.13, f32[5,2,5]{2,1,0:T(2,128)S(1)} %bitcast.15, f32[2,5,2,64,128]{4,3,2,1,0:T(8,128)S(1)} %copy-done.1, f32[2,5,64,128]{3,2,1,0:T(8,128)S(1)} %collective-permute-done.other, ...), custom_call_target="tpu_custom_call" | custom-call | flops 200000000 | bytes 4000000 | tf_op jit(solution)/shard_map/first_residual/pallas_call | solution.py:414
  11.2 10.3 %all-to-all-start = ((f32[16,17,8,128]{3,2,1,0:T(8,128)}), f32[16,17,8,128]{3,2,1,0:T(8,128)S(1)}, u32[]{:S(2)}, u32[]{:S(2)}) async-start(f32[16,17,8,128]{3,2,1,0:T(8,128)} %bitcast.8), calls=%async_computation | async-start | bytes 2228224 | tf_op jit(solution)/shard_map/all_to_all | solution.py:432
  24.2 4.3 %tables_b.1 = (f32[5,256,256]{2,1,0:T(8,128)S(1)}, f32[5,64,256]{2,1,0:T(8,128)S(1)}, f32[5,64,256]{2,1,0:T(8,128)S(1)}, f32[5,64,64]{2,1,0:T(8,128)S(1)}, f32[5...) custom-call(s32[4]{0:T(128)S(1)} %pad_add_fusion.info, f32[5,2,5]{2,1,0:T(2,128)S(1)} %bitcast.14, ...), custom_call_target="tpu_custom_call" | custom-call | flops 100000000 | bytes 4000000 | tf_op jit(solution)/shard_map/tables_b/pallas_call | solution.py:434
  31.3 16.5 %all-to-all-done.lines = f32[16,17,8,128]{3,2,1,0:T(8,128)S(1)} async-done(((f32[16,17,8,128]{3,2,1,0:T(8,128)}), f32[16,17,8,128]{3,2,1,0:T(8,128)S(1)}, u32[]{:S(2)}, u32[]{:S(2)}) %all-to-all-start) | async-done | bytes 1114144 | tf_op jit(solution)/shard_map/all_to_all | solution.py:432
  47.7 1.0 copy-done.5
  48.7 1.0 copy-done.7
  50.1 1.9 %collective-permute-start.1 = (f32[5,64,128]{2,1,0:T(8,128)S(1)}, f32[5,64,128]{2,1,0:T(8,128)S(1)}, u32[]{:S(2)}, u32[]{:S(2)}) collective-permute-start(f32[5,64,128]{2,1,0:T(8,128)S(1)} %get-tuple-element.29), channel_id=1, source_target_pairs={{0,1},{1,4},{4,5},{5,8},{8,9},{9,12},{12,13},{2,3},{3,6},{6,7},{7,... | collective-permute-start | bytes 491528 | tf_op jit(solution)/shard_map/ppermute | solution.py:465
  52.0 3.6 %collective-permute-start.2 = (f32[5,64,128]{2,1,0:T(8,128)S(1)}, f32[5,64,128]{2,1,0:T(8,128)S(1)}, u32[]{:S(2)}, u32[]{:S(2)}) collective-permute-start(f32[5,64,128]{2,1,0:T(8,128)S(1)} %get-tuple-element.30), channel_id=1, source_target_pairs={{1,0},{4,1},{5,4},{8,5},{9,8},{12,9},{13,12},{3,2},{6,3},{7,6},{10... | collective-permute-start | bytes 491528 | tf_op jit(solution)/shard_map/ppermute | solution.py:466
  55.7 3.7 %second_residual.1.local = f32[5,32,8,128]{3,2,1,0:T(8,128)S(1)} custom-call(s32[4]{0:T(128)S(1)} %pad_add_fusion.info, f32[3,5,5]{2,1,0:T(8,128)S(1)} %get-tuple-element.23.mixes, f32[16,17,8,128]{3,2,1,0:T(8,128)S(1)} %all-to-all-done.lines, f32[5,256,256]{2,1,0:T(8,128)S(1)} %get-tuple-element.25.solve_x, f32[5,128,128]{2,1,0:T(8,128)S(1)} %get-tuple-element.26.solve_z), custom_call_target="tpu_custom_call" | custom-call | flops 300000000 | bytes 4000000 | tf_op jit(solution)/shard_map/second_residual/pallas_call | solution.py:468
  59.4 2.0 %halo_rows.1 = (f32[16,10,8,128]{3,2,1,0:T(8,128)}, f32[8,128]{1,0:T(8,128)S(1)}) custom-call(f32[3,5,5]{2,1,0:T(8,128)S(1)} %get-tuple-element.23.mixes, f32[5,32,8,128]{3,2,1,0:T(8,128)S(1)} %second_residual.1.local, f32[5,64,128]{2,1,0:T(8,128)S(1)} %collective-permute-done.1.from_prev, f32[5,64,128]{2,1,0:T(8,128)S(1)} %collective-permute-done.2.from_next, ...), custom_call_target="tpu_custom_call" | custom-call | flops 50000000 | bytes 4000000 | tf_op jit(solution)/shard_map/halo_rows/pallas_call | solution.py:477
  61.5 3.7 %all-to-all-start.1 = ((f32[16,10,8,128]{3,2,1,0:T(8,128)}), f32[16,10,8,128]{3,2,1,0:T(8,128)S(1)}, u32[]{:S(2)}, u32[]{:S(2)}) async-start(f32[16,10,8,128]{3,2,1,0:T(8,128)} %get-tuple-element.33), calls=%async_computation.1 | async-start | bytes 1310720 | tf_op jit(solution)/shard_map/all_to_all | solution.py:487
  65.2 1.0 tables_y.1.solve_y
  66.2 12.3 %all-to-all-done.1.solved = f32[16,10,8,128]{3,2,1,0:T(8,128)S(1)} async-done(((f32[16,10,8,128]{3,2,1,0:T(8,128)}), f32[16,10,8,128]{3,2,1,0:T(8,128)S(1)}, u32[]{:S(2)}, u32[]{:S(2)}) %all-to-all-start.1) | async-done | bytes 655392 | tf_op jit(solution)/shard_map/all_to_all | solution.py:487
  78.5 2.0 %update.1 = (f32[2,5,2,64,128]{4,3,2,1,0:T(8,128)}, f32[2,5,64,128]{3,2,1,0:T(8,128)S(1)}, f32[2,5,64,128]{3,2,1,0:T(8,128)S(1)}) custom-call(s32[4]{0:T(128)S(1)} %pad_add_fusion.info, f32[5,2,5]{2,1,0:T(2,128)S(1)} %bitcast.18, f32[2,5,2,64,128]{4,3,2,1,0:T(8,128)S(1)} %copy-done.1, f32[16,10,8,128]{3,2,1,0:T(8,128)S(1)} %all-to-all-done.1.solved, ...), custom_call_target="tpu_custom_call" | custom-call | flops 60000000 | bytes 4000000 | tf_op jit(solution)/shard_map/update/pallas_call | solution.py:498
  80.5 1.9 %collective-permute-start.3 = (f32[2,5,64,128]{3,2,1,0:T(8,128)S(1)}, f32[2,5,64,128]{3,2,1,0:T(8,128)S(1)}, u32[]{:S(2)}, u32[]{:S(2)}) collective-permute-start(f32[2,5,64,128]{3,2,1,0:T(8,128)S(1)} %get-tuple-element.36.inner), channel_id=1, source_target_pairs={{0,1},{1,0},{2,3},{3,2},{4,5},{5,4},{6,7},{7,6},{8,9},{9,8},{10,11... | collective-permute-start | bytes 983048 | tf_op jit(solution)/shard_map/ppermute | solution.py:508
  82.4 4.8 %collective-permute-start.4 = (f32[2,5,64,128]{3,2,1,0:T(8,128)S(1)}, f32[2,5,64,128]{3,2,1,0:T(8,128)S(1)}, u32[]{:S(2)}, u32[]{:S(2)}) collective-permute-start(f32[2,5,64,128]{3,2,1,0:T(8,128)S(1)} %get-tuple-element.37.outer), channel_id=1, source_target_pairs={{1,2},{3,4},{5,6},{7,8},{9,10},{11,12},{13,14},{2,1},{4,3},{6,5},{... | collective-permute-start | bytes 983048 | tf_op jit(solution)/shard_map/ppermute | solution.py:507
  87.2 1.1 copy-done.3
  88.3 1.0 inside_terms.1.inside
  89.3 7.8 %collective-permute-done.4.other_outer = f32[2,5,64,128]{3,2,1,0:T(8,128)S(1)} collective-permute-done((f32[2,5,64,128]{3,2,1,0:T(8,128)S(1)}, f32[2,5,64,128]{3,2,1,0:T(8,128)S(1)}, u32[]{:S(2)}, u32[]{:S(2)}) %collective-permute-start.4) | collective-permute-done | bytes 327712 | tf_op jit(solution)/shard_map/ppermute | solution.py:507
  97.8 31.8 %all_to_all.20.pieces = f32[32,3,4,128]{3,2,1,0:T(4,128)S(1)} all-to-all(f32[32,3,4,128]{3,2,1,0:T(4,128)S(1)} %terms.1), channel_id=1, replica_groups=mesh['cond'=32,'grid'=16] {'cond'}, dimensions={0} | all-to-all | bytes 393216 | tf_op jit(solution)/shard_map/all_to_all | solution.py:527
  129.7 15.2 %all_to_all.21 = f32[32,3,4,128]{3,2,1,0:T(4,128)S(1)} all-to-all(f32[32,3,4,128]{3,2,1,0:T(4,128)S(1)} %sum_conditions.1), channel_id=1, replica_groups=mesh['cond'=32,'grid'=16] {'cond'}, dimensions={0} | all-to-all | bytes 393216 | tf_op jit(solution)/shard_map/all_to_all | solution.py:536
  (68 shorter events, 9.2 us)
Async XLA Ops:
  0.6 4.5 %copy-start.17 = (f32[2,5,3]{1,0,2:T(2,128)S(1)}, f32[2,5,3]{1,0,2:T(2,128)}, u32[]{:S(2)}) copy-start(f32[2,5,3]{1,0,2:T(2,128)} %param.15) | copy-start | bytes 364
  0.6 6.0 %copy-start.15 = (f32[2,5,5]{2,0,1:T(2,128)S(1)}, f32[2,5,5]{2,0,1:T(2,128)}, u32[]{:S(2)}) copy-start(f32[2,5,5]{2,0,1:T(2,128)} %param.13) | copy-start | bytes 604
  0.7 6.0 %copy-start.14 = (f32[2,5,5]{2,0,1:T(2,128)S(1)}, f32[2,5,5]{2,0,1:T(2,128)}, u32[]{:S(2)}) copy-start(f32[2,5,5]{2,0,1:T(2,128)} %param.12) | copy-start | bytes 604
  0.7 6.0 %copy-start.12 = (f32[2,64,128]{2,1,0:T(8,128)S(1)}, f32[2,64,128]{2,1,0:T(8,128)}, u32[]{:S(2)}) copy-start(f32[2,64,128]{2,1,0:T(8,128)} %radius.1) | copy-start | bytes 196612
  0.8 1.1 copy-start
  1.9 4.8 %copy-start.1 = (f32[2,5,2,64,128]{4,3,2,1,0:T(8,128)S(1)}, f32[2,5,2,64,128]{4,3,2,1,0:T(8,128)}, u32[]{:S(2)}) copy-start(f32[2,5,2,64,128]{4,3,2,1,0:T(8,128)} %adjoint.5) | copy-start | bytes 1966084
  1.9 4.8 %copy-start.2 = (f32[2,5,2,64,128]{4,3,2,1,0:T(8,128)S(1)}, f32[2,5,2,64,128]{4,3,2,1,0:T(8,128)}, u32[]{:S(2)}) copy-start(f32[2,5,2,64,128]{4,3,2,1,0:T(8,128)} %source_in.1) | copy-start | bytes 1966084
  2.5 4.2 %collective-permute-start = (f32[2,5,64,128]{3,2,1,0:T(8,128)S(1)}, f32[2,5,64,128]{3,2,1,0:T(8,128)S(1)}, u32[]{:S(2)}, u32[]{:S(2)}) collective-permute-start(f32[2,5,64,128]{3,2,1,0:T(8,128)S(1)} %inner_plane.1), channel_id=1, source_target_pairs={{0,1},{1,0},{2,3},{3,2},{4,5},{5,4},{6,7},{7,6},{8,9},{9,8},{10,11... | collective-permute-start | bytes 983048 | tf_op jit(solution)/shard_map/ppermute | solution.py:396
  4.5 6.1 %copy-start.21 = (f32[1,128]{1,0:T(1,128)}, f32[1,128]{1,0:T(1,128)S(1)}, u32[]{:S(2)}) copy-start(f32[1,128]{1,0:T(1,128)S(1)} %multiply_add_fusion.2.spec_z) | copy-start | bytes 1540
  11.2 11.7 %copy-start.16 = (f32[2,5,5]{2,0,1:T(2,128)S(1)}, f32[2,5,5]{2,0,1:T(2,128)}, u32[]{:S(2)}) copy-start(f32[2,5,5]{2,0,1:T(2,128)} %param.14) | copy-start | bytes 604
  11.2 36.5 %all-to-all-start = ((f32[16,17,8,128]{3,2,1,0:T(8,128)}), f32[16,17,8,128]{3,2,1,0:T(8,128)S(1)}, u32[]{:S(2)}, u32[]{:S(2)}) async-start(f32[16,17,8,128]{3,2,1,0:T(8,128)} %bitcast.8), calls=%async_computation | async-start | bytes 2228224 | tf_op jit(solution)/shard_map/all_to_all | solution.py:432
  29.2 0.7 copy-start.6
  47.7 1.0 copy-start.5
  48.7 1.0 copy-start.7
  50.1 9.3 %collective-permute-start.1 = (f32[5,64,128]{2,1,0:T(8,128)S(1)}, f32[5,64,128]{2,1,0:T(8,128)S(1)}, u32[]{:S(2)}, u32[]{:S(2)}) collective-permute-start(f32[5,64,128]{2,1,0:T(8,128)S(1)} %get-tuple-element.29), channel_id=1, source_target_pairs={{0,1},{1,4},{4,5},{5,8},{8,9},{9,12},{12,13},{2,3},{3,6},{6,7},{7,... | collective-permute-start | bytes 491528 | tf_op jit(solution)/shard_map/ppermute | solution.py:465
  52.0 7.4 %collective-permute-start.2 = (f32[5,64,128]{2,1,0:T(8,128)S(1)}, f32[5,64,128]{2,1,0:T(8,128)S(1)}, u32[]{:S(2)}, u32[]{:S(2)}) collective-permute-start(f32[5,64,128]{2,1,0:T(8,128)S(1)} %get-tuple-element.30), channel_id=1, source_target_pairs={{1,0},{4,1},{5,4},{8,5},{9,8},{12,9},{13,12},{3,2},{6,3},{7,6},{10... | collective-permute-start | bytes 491528 | tf_op jit(solution)/shard_map/ppermute | solution.py:466
  55.7 3.7 %copy-start.9 = (f32[5,64,64]{2,1,0:T(8,128)S(1)}, f32[5,64,64]{2,1,0:T(8,128)}, u32[]{:S(2)}) copy-start(f32[5,64,64]{2,1,0:T(8,128)} %copy-done.8) | copy-start | bytes 245764
  55.7 3.7 %copy-start.11 = (f32[5,64,64]{2,1,0:T(8,128)S(1)}, f32[5,64,64]{2,1,0:T(8,128)}, u32[]{:S(2)}) copy-start(f32[5,64,64]{2,1,0:T(8,128)} %copy-done.10) | copy-start | bytes 245764
  61.5 17.0 %all-to-all-start.1 = ((f32[16,10,8,128]{3,2,1,0:T(8,128)}), f32[16,10,8,128]{3,2,1,0:T(8,128)S(1)}, u32[]{:S(2)}, u32[]{:S(2)}) async-start(f32[16,10,8,128]{3,2,1,0:T(8,128)} %get-tuple-element.33), calls=%async_computation.1 | async-start | bytes 1310720 | tf_op jit(solution)/shard_map/all_to_all | solution.py:487
  65.2 22.0 %copy-start.13 = (f32[2,3,5]{2,0,1:T(2,128)S(1)}, f32[2,3,5]{2,0,1:T(2,128)}, u32[]{:S(2)}) copy-start(f32[2,3,5]{2,0,1:T(2,128)} %param.16) | copy-start | bytes 364
  65.2 22.0 %copy-start.18 = (s32[2]{0:T(128)S(1)}, s32[2]{0:T(128)}, u32[]{:S(2)}) copy-start(s32[2]{0:T(128)} %weights.3) | copy-start | bytes 28
  80.5 8.9 %collective-permute-start.3 = (f32[2,5,64,128]{3,2,1,0:T(8,128)S(1)}, f32[2,5,64,128]{3,2,1,0:T(8,128)S(1)}, u32[]{:S(2)}, u32[]{:S(2)}) collective-permute-start(f32[2,5,64,128]{3,2,1,0:T(8,128)S(1)} %get-tuple-element.36.inner), channel_id=1, source_target_pairs={{0,1},{1,0},{2,3},{3,2},{4,5},{5,4},{6,7},{7,6},{8,9},{9,8},{10,11... | collective-permute-start | bytes 983048 | tf_op jit(solution)/shard_map/ppermute | solution.py:508
  82.4 14.8 %collective-permute-start.4 = (f32[2,5,64,128]{3,2,1,0:T(8,128)S(1)}, f32[2,5,64,128]{3,2,1,0:T(8,128)S(1)}, u32[]{:S(2)}, u32[]{:S(2)}) collective-permute-start(f32[2,5,64,128]{3,2,1,0:T(8,128)S(1)} %get-tuple-element.37.outer), channel_id=1, source_target_pairs={{1,2},{3,4},{5,6},{7,8},{9,10},{11,12},{13,14},{2,1},{4,3},{6,5},{... | collective-permute-start | bytes 983048 | tf_op jit(solution)/shard_map/ppermute | solution.py:507
  87.2 1.1 copy-start.3
  (6 other events, 4.0 us)

commit v7 on v6

--- a/solution.py
+++ b/solution.py
@@ -103,11 +103,10 @@
             solve_y[c, f] = exact(sine_y[...] / denom, sine_y[...])
 
 
-def tables_y_kernel(rates, token, sine_y, spec_y, solve_y):
-    for c in range(2):
-        for f in range(FIELDS):
-            denom = 1.0 + rates[1, c, f] * spec_y[...]
-            solve_y[c, f] = exact(sine_y[...] / denom, sine_y[...])
+def tables_y_kernel(info, rates, token, sine_y, spec_y, solve_y):
+    for f in range(FIELDS):
+        denom = 1.0 + rates[1, info[1], f] * spec_y[...]
+        solve_y[f] = exact(sine_y[...] / denom, sine_y[...])
 
 
 def tables_b_kernel(info, coup, left_map, right_map, rates, token, sine_z, spec_z, left, right, left_2, right_2, spec_x,
@@ -213,11 +212,14 @@
     return jnp.stack([plane_0, w[:, 1], w[:, 3], plane_3], axis=1)
 
 
-def ends_kernel(lines, ends_prev, ends_next, to_prev, to_next):
+def ends_kernel(info, lines, ends_prev, ends_next, adjoint, to_prev, to_next, give, sem):
+    copy = pltpu.make_async_copy(adjoint.at[1 - info[1]], give, sem)
+    copy.start()
     for f in range(FIELDS):
         w = assembled(lines, f).reshape(-1, 128)
         to_prev[f] = dot(ends_prev[f], w)
         to_next[f] = dot(ends_next[f], w)
+    copy.wait()
 
 
 def second_kernel(info, mixes, lines, solve_x, solve_z, out, solved, lapped, kept):
@@ -274,77 +276,97 @@
         q = local[f] + jnp.where(
             row < 2, spread(add_prev, 0), jnp.where(row >= 6, spread(add_next, 6), 0.0)
         )
-        made[:, 2 * f : 2 * f + 2] = q.reshape(nx // 2, 2, 8, 128)
-        part = pl.ds(2 * f, 2)
-        stores.append(pltpu.make_async_copy(made.at[:, part], out.at[:, part], sems.at[f]))
+        q = q.reshape(nx // 8, 2, 2, 2, 8, 128)
+        for core in range(2):
+            for half in range(2):
+                at = 4 * f + 2 * half
+                made[:, core, at : at + 2] = q[:, half, core]
+        part = pl.ds(4 * f, 4)
+        stores.append(pltpu.make_async_copy(made.at[:, :, part], out.at[:, :, part], sems.at[f]))
         stores[-1].start()
     for copy in stores:
         copy.wait()
 
 
-def gathered(solved, c, tile, blocks):
-    return jnp.concatenate([solved[spot(c, b), tile] for b in range(blocks)], axis=0)
-
-
-def update_kernel(info, right, adjoint, solved, solve_y, out, inner, outer, step):
+def update_kernel(info, right, adjoint, got, solved, solve_y, new, own, back, inner, outer, step):
     ny = adjoint.shape[3]
-    me = info[0]
-    for c in range(2):
-        for f in range(FIELDS):
-            q = jnp.concatenate([gathered(solved, c, 2 * f + x, ny // 8) for x in range(2)], axis=1)
-            step[f] = dot(solve_y[c, f], q)
-        steps = [[step[g, :, 128 * x : 128 * x + 128] for g in range(FIELDS)] for x in range(2)]
-        for f in range(FIELDS):
-            planes = [adjoint[c, f, x] + mixed(lambda g: right[f, c, g], steps[x]) for x in range(2)]
-            for x in range(2):
-                out[c, f, x] = planes[x]
-            inner[c, f] = jnp.where(me == 0, planes[1], planes[0])
-            outer[c, f] = jnp.where(me == 0, planes[0], planes[1])
-
-
-def inside_kernel(smap, weights, adjoint, terms):
-    totals = [[0.0, 0.0] for _ in range(3)]
-    for c in range(2):
-        weight = weights[c].astype(F32)
-        for f in range(FIELDS):
-            w = [weight * smap[k, c, f] for k in range(3)]
-            v = [adjoint[c, f, x] for x in range(2)]
-            pair = w[0] * (v[0] * v[1])
-            totals[0][0] += pair
-            totals[0][1] -= pair
-            for x in range(2):
-                for k in range(2):
-                    totals[k + 1][x] += w[k + 1] * (v[x] * (shifted(v[x], k, 1) - shifted(v[x], k, -1)))
+    core, side = info[0], info[1]
+    for f in range(FIELDS):
+        q = [
+            jnp.concatenate([solved[b, 4 * f + p] for b in range(ny // 8)], axis=0) for p in range(4)
+        ]
+        step[f] = dot(solve_y[f], jnp.concatenate(q, axis=1))
+    steps = [[step[g, :, 128 * p : 128 * p + 128] for g in range(FIELDS)] for p in range(4)]
+    for f in range(FIELDS):
+        a = []
+        for p in range(4):
+            start = jnp.where(side == p // 2, adjoint[side, f, p % 2], got[f, p % 2])
+            a.append(start + mixed(lambda g: right[f, side, g], steps[p]))
+            new[f, p] = a[p]
+        for i in range(2):
+            own[f, i] = jnp.where(side == 0, a[i], a[2 + i])
+            back[f, i] = jnp.where(side == 0, a[2 + i], a[i])
+        for i in range(3):
+            inner[f, i] = jnp.where(core == 0, a[i + 1], a[i])
+        outer[f] = jnp.where(core == 0, a[0], a[3])
+
+
+def inside_kernel(info, smap, weights, new, terms):
+    side = info[1]
+    weight = weights[side].astype(F32)
+    totals = [[0.0] * 4 for _ in range(3)]
+    for f in range(FIELDS):
+        w = [weight * smap[k, side, f] for k in range(3)]
+        v = [new[f, p] for p in range(4)]
+        for h in range(2):
+            pair = w[0] * (v[2 * h] * v[2 * h + 1])
+            totals[0][2 * h] += pair
+            totals[0][2 * h + 1] -= pair
+        for p in range(4):
+            for k in range(2):
+                totals[k + 1][p] += w[k + 1] * (v[p] * (shifted(v[p], k, 1) - shifted(v[p], k, -1)))
     for k in range(3):
-        for x in range(2):
-            terms[k, x] = totals[k][x]
-
-
-def terms_kernel(info, smap, weights, inner, other_inner, outer, other_outer, inside, out):
-    me = info[0]
+        for p in range(4):
+            terms[k, p] = totals[k][p]
+
+
+def terms_kernel(info, smap, weights, inner, other_inner, outer, other_outer, inside, back, out, give, sem):
+    copy = pltpu.make_async_copy(back, give, sem)
+    copy.start()
+    core, side = info[0], info[1]
     ny = inner.shape[2]
     each = out.shape[1]
-
-    def store(k, x, v):
+    half = out.shape[0] // 2
+
+    def store(k, p, v):
         for i in range(ny // 4):
-            piece, at = divmod((k * 2 + x) * (ny // 4) + i, each)
-            out[piece, at] = v[4 * i : 4 * i + 4]
-
-    with_core, with_chip = 0.0, 0.0
-    for c in range(2):
-        weight = weights[c].astype(F32)
-        for f in range(FIELDS):
-            w = weight * smap[0, c, f]
-            with_core += w * (inner[c, f] * other_inner[c, f])
-            with_chip += w * (outer[c, f] * other_outer[c, f])
-    store(0, 0, inside[0, 0] - jnp.where(me == 0, with_chip, with_core))
-    store(0, 1, inside[0, 1] + jnp.where(me == 0, with_core, with_chip))
-    for k in range(1, 3):
-        for x in range(2):
-            store(k, x, inside[k, x])
-    for i in range(6 * ny // 4, out.shape[0] * each):
+            piece, at = divmod((k * 2 + p % 2) * (ny // 4) + i, each)
+            out[(p // 2) * half + piece, at] = v[4 * i : 4 * i + 4]
+
+    weight = weights[side].astype(F32)
+    between, beyond = [0.0] * 3, 0.0
+    for f in range(FIELDS):
+        w = weight * smap[0, side, f]
+        for i in range(3):
+            between[i] += w * (inner[f, i] * other_inner[f, i])
+        beyond += w * (outer[f] * other_outer[f])
+    edges = ((beyond, between[0]), (between[0], between[1]), (between[1], between[2]), (between[2], beyond))
+    for p in range(4):
+        edge = jnp.where(core == 0, edges[p][0], edges[p][1])
+        store(0, p, inside[0, p] + edge if p % 2 else inside[0, p] - edge)
+        for k in range(1, 3):
+            store(k, p, inside[k, p])
+    for i in range(6 * ny // 4, half * each):
         piece, at = divmod(i, each)
-        out[piece, at] = jnp.zeros(out.shape[2:], F32)
+        for h in range(2):
+            out[h * half + piece, at] = jnp.zeros(out.shape[2:], F32)
+    copy.wait()
+
+
+def join_kernel(info, own, got, token, out, sems):
+    side = info[1]
+    for copy in fetch((own, got), (out.at[side], out.at[1 - side]), sems):
+        copy.wait()
 
 
 def sum_kernel(scale, pieces, out):
@@ -382,8 +404,10 @@
     info = jnp.stack([core, side, place > 0, place < blocks - 1]).astype(jnp.int32)
 
     cores = [(i, i ^ 1) for i in range(peers)]
-    chips = [(i, i + 1) for i in range(1, peers - 1, 2)]
+    halves = [(i, i ^ 2) for i in range(peers)]
+    chips = [(i, i + 3) for i in range(peers - 4) if i % 2 == 1]
     chips = chips + [(j, i) for i, j in chips]
+    half_groups = [[i for i in range(peers) if i // 2 % 2 == half] for half in range(2)]
     other = call(
         plane_kernel,
         shape(2, fields, ny, nz),
@@ -452,13 +476,16 @@
         sine_table(nx, 8, 1), sine_table(nx, 1, 8), sine_table(nx, 2, 1), sine_table(nx, 1, 2), spectrum(nx),
     )
 
-    to_prev, to_next = call(
+    to_prev, to_next, give = call(
         ends_kernel,
-        (shape(fields, 2 * nx, nz), shape(fields, 2 * nx, nz)),
-        [VMEM] * 3,
+        (shape(fields, 2 * nx, nz), shape(fields, 2 * nx, nz), shape(fields, planes, ny, nz)),
+        [SMEM] + [VMEM] * 3 + [ANY],
         50_000_000,
         "solve_ends",
-    )(lines, ends_prev, ends_next)
+        [pltpu.SemaphoreType.DMA(())],
+        (VMEM, VMEM, ANY),
+    )(info, lines, ends_prev, ends_next, adjoint_start)
+    got = lax.ppermute(give, "grid", halves)
 
     up = [(spot(s, b), spot(s, b + 1)) for s in range(2) for b in range(blocks - 1)]
     down = [(j, i) for i, j in up]
@@ -476,55 +503,70 @@
 
     step, token = call(
         halo_kernel,
-        (shape(peers, planes * fields, 8, nz), shape(8, nz)),
+        (shape(nx // 8, 2, 4 * fields, 8, nz), shape(8, nz)),
         [SMEM] + [VMEM] * 6,
         50_000_000,
         "halo_rows",
-        [vmem(peers, planes * fields, 8, nz), sems(fields)],
+        [vmem(nx // 8, 2, 4 * fields, 8, nz), sems(fields)],
         (ANY, VMEM),
     )(mixes, local, from_prev, from_next, halo_prev, halo_next, solve_zb)
 
-    step = lax.all_to_all(step, "grid", 0, 0, tiled=True)
+    step = step.reshape(blocks, 4 * fields, 8, nz)
+    step = lax.all_to_all(step, "grid", 0, 0, axis_index_groups=half_groups, tiled=True)
 
     solve_y = call(
         tables_y_kernel,
-        shape(2, fields, ny, ny),
-        [SMEM, VMEM, VMEM, VMEM],
+        shape(fields, ny, ny),
+        [SMEM, SMEM, VMEM, VMEM, VMEM],
         50_000_000,
         "tables_y",
-    )(rates, token, sine_y, spec_y)
-
-    slab = shape(2, fields, ny, nz)
-    adjoint, inner, outer = call(
+    )(info, rates, token, sine_y, spec_y)
+
+    new, own, back, inner, outer = call(
         update_kernel,
-        (shape(2, fields, planes, ny, nz), slab, slab),
-        [SMEM, SMEM] + [VMEM] * 3,
+        (
+            shape(fields, 4, ny, nz),
+            shape(fields, planes, ny, nz),
+            shape(fields, planes, ny, nz),
+            shape(fields, 3, ny, nz),
+            shape(fields, ny, nz),
+        ),
+        [SMEM, SMEM] + [VMEM] * 4,
         60_000_000,
         "update",
-        [vmem(fields, ny, 2 * nz)],
-    )(info, right_map, adjoint_start, step, solve_y)
+        [vmem(fields, ny, 4 * nz)],
+    )(info, right_map, adjoint_start, got, step, solve_y)
 
     other_outer = lax.ppermute(outer, "grid", chips)
     other_inner = lax.ppermute(inner, "grid", cores)
 
     inside = call(
         inside_kernel,
-        shape(3, planes, ny, nz),
-        [SMEM, SMEM, VMEM],
+        shape(3, 4, ny, nz),
+        [SMEM, SMEM, SMEM, VMEM],
         60_000_000,
         "inside_terms",
-    )(smap, condition_weights, adjoint)
+    )(info, smap, condition_weights, new)
 
     tiles = 3 * planes * ny // 4
     each = -(-tiles // conds)
-    pieces = call(
+    pieces, back = call(
         terms_kernel,
-        shape(conds, each, 4, nz),
-        [SMEM] * 3 + [VMEM] * 5,
+        (shape(2 * conds, each, 4, nz), shape(fields, planes, ny, nz)),
+        [SMEM] * 3 + [VMEM] * 5 + [ANY],
         10_000_000,
         "terms",
-    )(info, smap, condition_weights, inner, other_inner, outer, other_outer, inside)
-    pieces = lax.all_to_all(pieces, "cond", 0, 0, tiled=True)
+        [pltpu.SemaphoreType.DMA(())],
+        (VMEM, ANY),
+    )(info, smap, condition_weights, inner, other_inner, outer, other_outer, inside, back)
+
+    groups = [
+        [i * peers + x + 2 * half for half in range(2) for i in range(conds)]
+        for x in range(peers)
+        if x // 2 % 2 == 0
+    ]
+    pieces = lax.all_to_all(pieces, ("cond", "grid"), 0, 0, axis_index_groups=groups, tiled=True)
+    back = lax.ppermute(back, "grid", halves)
     scale = 1.0 / (conds * condition_weights.shape[0])
     pieces = call(
         functools.partial(sum_kernel, scale),
@@ -533,7 +575,17 @@
         1_000_000,
         "sum_conditions",
     )(pieces)
+    token = pieces
     pieces = lax.all_to_all(pieces, "cond", 0, 0, tiled=True)
+    adjoint = call(
+        join_kernel,
+        shape(2, fields, planes, ny, nz),
+        [SMEM, ANY, ANY, ANY],
+        1000,
+        "join",
+        [sems(2)],
+        ANY,
+    )(info, own, back, token)
     total = pieces.reshape(conds * each * 4, nz)[: tiles * 4].reshape(3, planes, ny, nz)
     return (adjoint, total)
 

time: 146 us -> 159 us (1.089)
  the two profiles are of different devices: /device:TPU:2 before, /device:TPU:19 now
where the time goes in v7:
time: 159 us
  waiting for transfers between devices  56.6 us (36%)
  starting transfers between devices  38.1 us (24%)
  blocking collectives  28.4 us (18%)
  Pallas kernels  23.2 us (15%)
  local copies, waits for them, and re-layouts  9.29 us (6%)
  other arithmetic  1.89 us (1%)
    all_to_all x1, blocking collectives, body(): lax.all_to_all(pieces, ('cond', 'grid'), 0, 0, axis_index_groups=groups,...  28.4 us
    all_to_all x1, waiting for transfers between devices, body(): lines = lax.all_to_all(lines, 'grid', 0, 0, tiled=True)  20.2 us
    ppermute x1, waiting for transfers between devices, body(): back = lax.ppermute(back, 'grid', halves)  18.2 us
    ppermute x1, waiting for transfers between devices, body(): got = lax.ppermute(give, 'grid', halves)  14.6 us
    unnamed x49, local copies, waits for them, and re-layouts  9.2 us
    all_to_all x1, starting transfers between devices, body(): lines = lax.all_to_all(lines, 'grid', 0, 0, tiled=True)  8.2 us
    all_to_all x1, starting transfers between devices, body(): pieces = lax.all_to_all(pieces, 'cond', 0, 0, tiled=True)  5.08 us
    all_to_all x1, starting transfers between devices, body(): lax.all_to_all(step, 'grid', 0, 0, axis_index_groups=half_groups, tiled=T...  4.57 us
  transfers between devices with their start and end apart: 10, of which 5 were waited for; matrix products, arithmetic and copies ran while one was open for 1% of the time, Pallas kernels for 8%

profile of v7, /device:TPU:19, one launch (start us, length us, event | category | flops | bytes accessed | tf_op | source)
XLA Modules:
  0.0 158.6 jit_solution(13820969898599278991)
XLA Ops:
  0.8 1.1 copy-done
  2.5 2.6 %collective-permute-start = (f32[2,5,64,128]{3,2,1,0:T(8,128)S(1)}, f32[2,5,64,128]{3,2,1,0:T(8,128)S(1)}, u32[]{:S(2)}, u32[]{:S(2)}) collective-permute-start(f32[2,5,64,128]{3,2,1,0:T(8,128)S(1)} %inner_plane.1), channel_id=1, source_target_pairs={{0,1},{1,0},{2,3},{3,2},{4,5},{5,4},{6,7},{7,6},{8,9},{9,8},{10,11... | collective-permute-start | bytes 983048 | tf_op jit(solution)/shard_map/ppermute | solution.py:420
  5.8 1.6 solve_tables.1
  7.4 3.9 %first_residual.1 = (f32[4,2,2,17,8,128]{5,4,3,2,1,0:T(8,128)}, f32[8,128]{1,0:T(8,128)S(1)}) custom-call(s32[4]{0:T(128)S(1)} %pad_add_fusion.info, f32[5,2,5]{2,1,0:T(2,128)S(1)} %bitcast.14, f32[5,2,5]{2,1,0:T(2,128)S(1)} %bitcast.16, f32[2,5,2,64,128]{4,3,2,1,0:T(8,128)S(1)} %copy-done.1, f32[2,5,64,128]{3,2,1,0:T(8,128)S(1)} %collective-permute-done.other, ...), custom_call_target="tpu_custom_call" | custom-call | flops 200000000 | bytes 4000000 | tf_op jit(solution)/shard_map/first_residual/pallas_call | solution.py:438
  11.9 8.2 %all-to-all-start = ((f32[16,17,8,128]{3,2,1,0:T(8,128)}), f32[16,17,8,128]{3,2,1,0:T(8,128)S(1)}, u32[]{:S(2)}, u32[]{:S(2)}) async-start(f32[16,17,8,128]{3,2,1,0:T(8,128)} %bitcast.8), calls=%async_computation | async-start | bytes 2228224 | tf_op jit(solution)/shard_map/all_to_all | solution.py:456
  22.7 4.3 %tables_b.1 = (f32[5,256,256]{2,1,0:T(8,128)S(1)}, f32[5,64,256]{2,1,0:T(8,128)S(1)}, f32[5,64,256]{2,1,0:T(8,128)S(1)}, f32[5,64,64]{2,1,0:T(8,128)S(1)}, f32[5...) custom-call(s32[4]{0:T(128)S(1)} %pad_add_fusion.info, f32[5,2,5]{2,1,0:T(2,128)S(1)} %bitcast.15, ...), custom_call_target="tpu_custom_call" | custom-call | flops 100000000 | bytes 4000000 | tf_op jit(solution)/shard_map/tables_b/pallas_call | solution.py:458
  29.8 20.2 %all-to-all-done.lines = f32[16,17,8,128]{3,2,1,0:T(8,128)S(1)} async-done(((f32[16,17,8,128]{3,2,1,0:T(8,128)}), f32[16,17,8,128]{3,2,1,0:T(8,128)S(1)}, u32[]{:S(2)}, u32[]{:S(2)}) %all-to-all-start) | async-done | bytes 1114144 | tf_op jit(solution)/shard_map/all_to_all | solution.py:456
  51.9 1.1 solve_ends.1
  53.8 3.8 %collective-permute-start.2 = (f32[5,64,128]{2,1,0:T(8,128)S(1)}, f32[5,64,128]{2,1,0:T(8,128)S(1)}, u32[]{:S(2)}, u32[]{:S(2)}) collective-permute-start(f32[5,64,128]{2,1,0:T(8,128)S(1)} %get-tuple-element.35), channel_id=1, source_target_pairs={{0,1},{1,4},{4,5},{5,8},{8,9},{9,12},{12,13},{2,3},{3,6},{6,7},{7,... | collective-permute-start | bytes 491528 | tf_op jit(solution)/shard_map/ppermute | solution.py:492
  57.6 1.9 %collective-permute-start.3 = (f32[5,64,128]{2,1,0:T(8,128)S(1)}, f32[5,64,128]{2,1,0:T(8,128)S(1)}, u32[]{:S(2)}, u32[]{:S(2)}) collective-permute-start(f32[5,64,128]{2,1,0:T(8,128)S(1)} %get-tuple-element.36), channel_id=1, source_target_pairs={{1,0},{4,1},{5,4},{8,5},{9,8},{12,9},{13,12},{3,2},{6,3},{7,6},{10... | collective-permute-start | bytes 491528 | tf_op jit(solution)/shard_map/ppermute | solution.py:493
  59.6 3.7 %second_residual.1.local = f32[5,32,8,128]{3,2,1,0:T(8,128)S(1)} custom-call(s32[4]{0:T(128)S(1)} %pad_add_fusion.info, f32[3,5,5]{2,1,0:T(8,128)S(1)} %get-tuple-element.32.mixes, f32[16,17,8,128]{3,2,1,0:T(8,128)S(1)} %all-to-all-done.lines, f32[5,256,256]{2,1,0:T(8,128)S(1)} %get-tuple-element.33.solve_x, f32[5,128,128]{2,1,0:T(8,128)S(1)} %get-tuple-element.34.solve_z), custom_call_target="tpu_custom_call" | custom-call | flops 300000000 | bytes 4000000 | tf_op jit(solution)/shard_map/second_residual/pallas_call | solution.py:495
  64.3 2.0 %halo_rows.1 = (f32[4,2,20,8,128]{4,3,2,1,0:T(8,128)}, f32[8,128]{1,0:T(8,128)S(1)}) custom-call(f32[3,5,5]{2,1,0:T(8,128)S(1)} %get-tuple-element.32.mixes, f32[5,32,8,128]{3,2,1,0:T(8,128)S(1)} %second_residual.1.local, f32[5,64,128]{2,1,0:T(8,128)S(1)} %collective-permute-done.2.from_prev, f32[5,64,128]{2,1,0:T(8,128)S(1)} %collective-permute-done.3.from_next, ...), custom_call_target="tpu_custom_call" | custom-call | flops 50000000 | bytes 4000000 | tf_op jit(solution)/shard_map/halo_rows/pallas_call | solution.py:504
  66.3 4.6 %all-to-all-start.1 = ((f32[8,20,8,128]{3,2,1,0:T(8,128)}), f32[8,20,8,128]{3,2,1,0:T(8,128)S(1)}, u32[]{:S(2)}, u32[]{:S(2)}) async-start(f32[8,20,8,128]{3,2,1,0:T(8,128)} %bitcast.9), calls=%async_computation.1 | async-start | bytes 1310720 | tf_op jit(solution)/shard_map/all_to_all | solution.py:515
  70.9 2.3 %collective-permute-start.1 = (f32[5,2,64,128]{3,2,1,0:T(8,128)S(1)}, f32[5,2,64,128]{3,2,1,0:T(8,128)S(1)}, u32[]{:S(2)}, u32[]{:S(2)}) collective-permute-start(f32[5,2,64,128]{3,2,1,0:T(8,128)S(1)} %copy-done.19), channel_id=1, source_target_pairs={{0,2},{1,3},{2,0},{3,1},{4,6},{5,7},{6,4},{7,5},{8,10},{9,11},{10,... | collective-permute-start | bytes 983048 | tf_op jit(solution)/shard_map/ppermute | solution.py:488
  74.1 14.6 %collective-permute-done.1.got = f32[5,2,64,128]{3,2,1,0:T(8,128)S(1)} collective-permute-done((f32[5,2,64,128]{3,2,1,0:T(8,128)S(1)}, f32[5,2,64,128]{3,2,1,0:T(8,128)S(1)}, u32[]{:S(2)}, u32[]{:S(2)}) %collective-permute-start.1) | collective-permute-done | bytes 327712 | tf_op jit(solution)/shard_map/ppermute | solution.py:488
  88.7 1.3 update.1
  90.0 2.4 %collective-permute-start.4 = (f32[5,3,64,128]{3,2,1,0:T(8,128)S(1)}, f32[5,3,64,128]{3,2,1,0:T(8,128)S(1)}, u32[]{:S(2)}, u32[]{:S(2)}) collective-permute-start(f32[5,3,64,128]{3,2,1,0:T(8,128)S(1)} %get-tuple-element.42.inner), channel_id=1, source_target_pairs={{0,1},{1,0},{2,3},{3,2},{4,5},{5,4},{6,7},{7,6},{8,9},{9,8},{10,11... | collective-permute-start | bytes 1474568 | tf_op jit(solution)/shard_map/ppermute | solution.py:541
  92.4 3.0 %collective-permute-start.5 = (f32[5,64,128]{2,1,0:T(8,128)S(1)}, f32[5,64,128]{2,1,0:T(8,128)S(1)}, u32[]{:S(2)}, u32[]{:S(2)}) collective-permute-start(f32[5,64,128]{2,1,0:T(8,128)S(1)} %get-tuple-element.43.outer), channel_id=1, source_target_pairs={{1,4},{3,6},{5,8},{7,10},{9,12},{11,14},{4,1},{6,3},{8,5},{10,7},{... | collective-permute-start | bytes 491528 | tf_op jit(solution)/shard_map/ppermute | solution.py:540
  96.5 2.6 %collective-permute-done.5.other_outer = f32[5,64,128]{2,1,0:T(8,128)S(1)} collective-permute-done((f32[5,64,128]{2,1,0:T(8,128)S(1)}, f32[5,64,128]{2,1,0:T(8,128)S(1)}, u32[]{:S(2)}, u32[]{:S(2)}) %collective-permute-start.5) | collective-permute-done | bytes 163872 | tf_op jit(solution)/shard_map/ppermute | solution.py:540
  99.9 28.4 %all_to_all.20.pieces = f32[64,3,4,128]{3,2,1,0:T(4,128)S(1)} all-to-all(f32[64,3,4,128]{3,2,1,0:T(4,128)S(1)} %get-tuple-element.47), channel_id=1, replica_groups={{0,16,32,48,64,80,96,112,128,144,160,176,192,208,224,240,256,272,288,30..., dimensions={0} | all-to-all | bytes 786432 | tf_op jit(solution)/shard_map/all_to_all | solution.py:568
  129.1 5.1 %all-to-all-start.3 = ((f32[32,3,4,128]{3,2,1,0:T(4,128)}), f32[32,3,4,128]{3,2,1,0:T(4,128)S(1)}, u32[]{:S(2)}, u32[]{:S(2)}) async-start(f32[32,3,4,128]{3,2,1,0:T(4,128)} %sum_conditions.1.token), calls=%async_computation.3 | async-start | bytes 393216 | tf_op jit(solution)/shard_map/all_to_all | solution.py:579
  134.1 4.2 %collective-permute-start.6 = (f32[5,2,64,128]{3,2,1,0:T(8,128)S(1)}, f32[5,2,64,128]{3,2,1,0:T(8,128)S(1)}, u32[]{:S(2)}, u32[]{:S(2)}) collective-permute-start(f32[5,2,64,128]{3,2,1,0:T(8,128)S(1)} %get-tuple-element.46), channel_id=1, source_target_pairs={{0,2},{1,3},{2,0},{3,1},{4,6},{5,7},{6,4},{7,5},{8,10},{9,11},{10,... | collective-permute-start | bytes 983048 | tf_op jit(solution)/shard_map/ppermute | solution.py:569
  138.4 18.2 %collective-permute-done.6.got = f32[5,2,64,128]{3,2,1,0:T(8,128)S(1)} collective-permute-done((f32[5,2,64,128]{3,2,1,0:T(8,128)S(1)}, f32[5,2,64,128]{3,2,1,0:T(8,128)S(1)}, u32[]{:S(2)}, u32[]{:S(2)}) %collective-permute-start.6) | collective-permute-done | bytes 327712 | tf_op jit(solution)/shard_map/ppermute | solution.py:569
  156.5 1.4 join.1
  (76 shorter events, 15.2 us)
Async XLA Ops:
  0.6 5.1 %copy-start.16 = (f32[2,5,3]{1,0,2:T(2,128)S(1)}, f32[2,5,3]{1,0,2:T(2,128)}, u32[]{:S(2)}) copy-start(f32[2,5,3]{1,0,2:T(2,128)} %param.15) | copy-start | bytes 364
  0.6 6.7 %copy-start.14 = (f32[2,5,5]{2,0,1:T(2,128)S(1)}, f32[2,5,5]{2,0,1:T(2,128)}, u32[]{:S(2)}) copy-start(f32[2,5,5]{2,0,1:T(2,128)} %param.13) | copy-start | bytes 604
  0.7 6.7 %copy-start.13 = (f32[2,5,5]{2,0,1:T(2,128)S(1)}, f32[2,5,5]{2,0,1:T(2,128)}, u32[]{:S(2)}) copy-start(f32[2,5,5]{2,0,1:T(2,128)} %param.12) | copy-start | bytes 604
  0.7 6.7 %copy-start.11 = (f32[2,64,128]{2,1,0:T(8,128)S(1)}, f32[2,64,128]{2,1,0:T(8,128)}, u32[]{:S(2)}) copy-start(f32[2,64,128]{2,1,0:T(8,128)} %radius.1) | copy-start | bytes 196612
  0.8 1.1 copy-start
  1.9 5.5 %copy-start.1 = (f32[2,5,2,64,128]{4,3,2,1,0:T(8,128)S(1)}, f32[2,5,2,64,128]{4,3,2,1,0:T(8,128)}, u32[]{:S(2)}) copy-start(f32[2,5,2,64,128]{4,3,2,1,0:T(8,128)} %adjoint.7) | copy-start | bytes 1966084
  1.9 5.5 %copy-start.2 = (f32[2,5,2,64,128]{4,3,2,1,0:T(8,128)S(1)}, f32[2,5,2,64,128]{4,3,2,1,0:T(8,128)}, u32[]{:S(2)}) copy-start(f32[2,5,2,64,128]{4,3,2,1,0:T(8,128)} %source_in.1) | copy-start | bytes 1966084
  2.5 4.8 %collective-permute-start = (f32[2,5,64,128]{3,2,1,0:T(8,128)S(1)}, f32[2,5,64,128]{3,2,1,0:T(8,128)S(1)}, u32[]{:S(2)}, u32[]{:S(2)}) collective-permute-start(f32[2,5,64,128]{3,2,1,0:T(8,128)S(1)} %inner_plane.1), channel_id=1, source_target_pairs={{0,1},{1,0},{2,3},{3,2},{4,5},{5,4},{6,7},{7,6},{8,9},{9,8},{10,11... | collective-permute-start | bytes 983048 | tf_op jit(solution)/shard_map/ppermute | solution.py:420
  5.1 6.1 %copy-start.22 = (f32[1,128]{1,0:T(1,128)}, f32[1,128]{1,0:T(1,128)S(1)}, u32[]{:S(2)}) copy-start(f32[1,128]{1,0:T(1,128)S(1)} %multiply_add_fusion.2.spec_z) | copy-start | bytes 1540
  11.9 9.5 %copy-start.15 = (f32[2,5,5]{2,0,1:T(2,128)S(1)}, f32[2,5,5]{2,0,1:T(2,128)}, u32[]{:S(2)}) copy-start(f32[2,5,5]{2,0,1:T(2,128)} %param.14) | copy-start | bytes 604
  11.9 38.1 %all-to-all-start = ((f32[16,17,8,128]{3,2,1,0:T(8,128)}), f32[16,17,8,128]{3,2,1,0:T(8,128)S(1)}, u32[]{:S(2)}, u32[]{:S(2)}) async-start(f32[16,17,8,128]{3,2,1,0:T(8,128)} %bitcast.8), calls=%async_computation | async-start | bytes 2228224 | tf_op jit(solution)/shard_map/all_to_all | solution.py:456
  53.8 9.5 %collective-permute-start.2 = (f32[5,64,128]{2,1,0:T(8,128)S(1)}, f32[5,64,128]{2,1,0:T(8,128)S(1)}, u32[]{:S(2)}, u32[]{:S(2)}) collective-permute-start(f32[5,64,128]{2,1,0:T(8,128)S(1)} %get-tuple-element.35), channel_id=1, source_target_pairs={{0,1},{1,4},{4,5},{5,8},{8,9},{9,12},{12,13},{2,3},{3,6},{6,7},{7,... | collective-permute-start | bytes 491528 | tf_op jit(solution)/shard_map/ppermute | solution.py:492
  57.6 6.6 %collective-permute-start.3 = (f32[5,64,128]{2,1,0:T(8,128)S(1)}, f32[5,64,128]{2,1,0:T(8,128)S(1)}, u32[]{:S(2)}, u32[]{:S(2)}) collective-permute-start(f32[5,64,128]{2,1,0:T(8,128)S(1)} %get-tuple-element.36), channel_id=1, source_target_pairs={{1,0},{4,1},{5,4},{8,5},{9,8},{12,9},{13,12},{3,2},{6,3},{7,6},{10... | collective-permute-start | bytes 491528 | tf_op jit(solution)/shard_map/ppermute | solution.py:493
  59.5 4.7 %copy-start.8 = (f32[5,64,64]{2,1,0:T(8,128)S(1)}, f32[5,64,64]{2,1,0:T(8,128)}, u32[]{:S(2)}) copy-start(f32[5,64,64]{2,1,0:T(8,128)} %copy-done.7) | copy-start | bytes 245764
  59.6 4.7 %copy-start.10 = (f32[5,64,64]{2,1,0:T(8,128)S(1)}, f32[5,64,64]{2,1,0:T(8,128)}, u32[]{:S(2)}) copy-start(f32[5,64,64]{2,1,0:T(8,128)} %copy-done.9) | copy-start | bytes 245764
  64.3 6.6 %copy-start.19 = (f32[5,2,64,128]{3,2,1,0:T(8,128)S(1)}, f32[5,2,64,128]{3,2,1,0:T(8,128)}, u32[]{:S(2)}) copy-start(f32[5,2,64,128]{3,2,1,0:T(8,128)} %copy-done.18) | copy-start | bytes 983044
  66.3 22.5 %all-to-all-start.1 = ((f32[8,20,8,128]{3,2,1,0:T(8,128)}), f32[8,20,8,128]{3,2,1,0:T(8,128)S(1)}, u32[]{:S(2)}, u32[]{:S(2)}) async-start(f32[8,20,8,128]{3,2,1,0:T(8,128)} %bitcast.9), calls=%async_computation.1 | async-start | bytes 1310720 | tf_op jit(solution)/shard_map/all_to_all | solution.py:515
  70.9 24.6 %copy-start.12 = (f32[2,3,5]{2,0,1:T(2,128)S(1)}, f32[2,3,5]{2,0,1:T(2,128)}, u32[]{:S(2)}) copy-start(f32[2,3,5]{2,0,1:T(2,128)} %param.16) | copy-start | bytes 364
  70.9 24.6 %copy-start.17 = (s32[2]{0:T(128)S(1)}, s32[2]{0:T(128)}, u32[]{:S(2)}) copy-start(s32[2]{0:T(128)} %weights.3) | copy-start | bytes 28
  70.9 17.9 %collective-permute-start.1 = (f32[5,2,64,128]{3,2,1,0:T(8,128)S(1)}, f32[5,2,64,128]{3,2,1,0:T(8,128)S(1)}, u32[]{:S(2)}, u32[]{:S(2)}) collective-permute-start(f32[5,2,64,128]{3,2,1,0:T(8,128)S(1)} %copy-done.19), channel_id=1, source_target_pairs={{0,2},{1,3},{2,0},{3,1},{4,6},{5,7},{6,4},{7,5},{8,10},{9,11},{10,... | collective-permute-start | bytes 983048 | tf_op jit(solution)/shard_map/ppermute | solution.py:488
  90.0 9.0 %collective-permute-start.4 = (f32[5,3,64,128]{3,2,1,0:T(8,128)S(1)}, f32[5,3,64,128]{3,2,1,0:T(8,128)S(1)}, u32[]{:S(2)}, u32[]{:S(2)}) collective-permute-start(f32[5,3,64,128]{3,2,1,0:T(8,128)S(1)} %get-tuple-element.42.inner), channel_id=1, source_target_pairs={{0,1},{1,0},{2,3},{3,2},{4,5},{5,4},{6,7},{7,6},{8,9},{9,8},{10,11... | collective-permute-start | bytes 1474568 | tf_op jit(solution)/shard_map/ppermute | solution.py:541
  92.4 6.6 %collective-permute-start.5 = (f32[5,64,128]{2,1,0:T(8,128)S(1)}, f32[5,64,128]{2,1,0:T(8,128)S(1)}, u32[]{:S(2)}, u32[]{:S(2)}) collective-permute-start(f32[5,64,128]{2,1,0:T(8,128)S(1)} %get-tuple-element.43.outer), channel_id=1, source_target_pairs={{1,4},{3,6},{5,8},{7,10},{9,12},{11,14},{4,1},{6,3},{8,5},{10,7},{... | collective-permute-start | bytes 491528 | tf_op jit(solution)/shard_map/ppermute | solution.py:540
  129.1 28.9 %all-to-all-start.3 = ((f32[32,3,4,128]{3,2,1,0:T(4,128)}), f32[32,3,4,128]{3,2,1,0:T(4,128)S(1)}, u32[]{:S(2)}, u32[]{:S(2)}) async-start(f32[32,3,4,128]{3,2,1,0:T(4,128)} %sum_conditions.1.token), calls=%async_computation.3 | async-start | bytes 393216 | tf_op jit(solution)/shard_map/all_to_all | solution.py:579
  134.1 22.4 %collective-permute-start.6 = (f32[5,2,64,128]{3,2,1,0:T(8,128)S(1)}, f32[5,2,64,128]{3,2,1,0:T(8,128)S(1)}, u32[]{:S(2)}, u32[]{:S(2)}) collective-permute-start(f32[5,2,64,128]{3,2,1,0:T(8,128)S(1)} %get-tuple-element.46), channel_id=1, source_target_pairs={{0,2},{1,3},{2,0},{3,1},{4,6},{5,7},{6,4},{7,5},{8,10},{9,11},{10,... | collective-permute-start | bytes 983048 | tf_op jit(solution)/shard_map/ppermute | solution.py:569
  (10 other events, 7.4 us)

commit v8 on v6

--- a/solution.py
+++ b/solution.py
@@ -111,7 +111,7 @@
 
 
 def tables_b_kernel(info, coup, left_map, right_map, rates, token, sine_z, spec_z, left, right, left_2, right_2, spec_x,
-                    solve_x, ends_prev, ends_next, halo_prev, halo_next, solve_z, mixes):
+                    solve_x, halo_prev, halo_next, solve_z, mixes):
     mine = info[1]
     for f in range(FIELDS):
         for g in range(FIELDS):
@@ -128,9 +128,6 @@
     n, nx = left.shape
     row, col = (lax.broadcasted_iota(jnp.int32, (n, n), i) for i in range(2))
     same = (row & 7) == (col & 7)
-    row, col = (lax.broadcasted_iota(jnp.int32, (2 * nx, n), i) for i in range(2))
-    prev_rows = (row & 1) == (col & 7)
-    next_rows = (row & 1) + 6 == (col & 7)
     row, col = (lax.broadcasted_iota(jnp.int32, (2 * nx, 2 * nx), i) for i in range(2))
     from_last = ((row & 1) == 0) & ((col & 1) == 1)
     from_first = ((row & 1) == 1) & ((col & 1) == 0)
@@ -139,20 +136,11 @@
         scaled = left[...] / denom
         solve_x[f] = jnp.where(same, exact(scaled, right[...]), 0.0)
         scaled_2 = left_2[...] / denom
-        both = exact(scaled_2, right[...])
-        ends_prev[f] = jnp.where(prev_rows, both, 0.0)
-        ends_next[f] = jnp.where(next_rows, both, 0.0)
         both = exact(scaled_2, right_2[...])
         halo_prev[f] = jnp.where(from_last, both, 0.0)
         halo_next[f] = jnp.where(from_first, both, 0.0)
         denom = 1.0 + rates[2, mine, f] * spec_z[...]
         solve_z[f] = exact(sine_z[...] / denom, sine_z[...])
-
-
-def plane_kernel(info, adjoint, inner, sem):
-    copy = pltpu.make_async_copy(adjoint.at[:, :, 1 - info[0]], inner, sem)
-    copy.start()
-    copy.wait()
 
 
 def first_kernel(info, coup, left, adjoint, other, source_in, radius, solve_z, solve_y, out, token,
@@ -170,7 +158,7 @@
             for f in range(FIELDS):
                 v = adjoint[c, f, x]
                 beside = adjoint[c, f, 1 - x]
-                beside = beside + other[c, f] * (before if x == 0 else after)
+                beside = beside + (other[c, f, 1] * before if x == 0 else other[c, f, 0] * after)
                 beside = beside + shifted(v, 0, 1) + shifted(v, 0, -1)
                 beside = beside + shifted(v, 1, 1) + shifted(v, 1, -1)
                 lapped[x, f] = 6.0 * v - beside
@@ -213,11 +201,14 @@
     return jnp.stack([plane_0, w[:, 1], w[:, 3], plane_3], axis=1)
 
 
-def ends_kernel(lines, ends_prev, ends_next, to_prev, to_next):
+def ends_kernel(lines, solve_x, to_prev, to_next):
+    n = solve_x.shape[1]
     for f in range(FIELDS):
-        w = assembled(lines, f).reshape(-1, 128)
-        to_prev[f] = dot(ends_prev[f], w)
-        to_next[f] = dot(ends_next[f], w)
+        u = dot(solve_x[f], assembled(lines, f).reshape(n, 128))
+        quad = u.reshape(n // 32, 4, 8, 128)
+        for j in range(4):
+            to_prev[f, :, 2 * j : 2 * j + 2, :] = quad[:, j, 0:2, :]
+            to_next[f, :, 2 * j : 2 * j + 2, :] = quad[:, j, 6:8, :]
 
 
 def second_kernel(info, mixes, lines, solve_x, solve_z, out, solved, lapped, kept):
@@ -320,7 +311,7 @@
             terms[k, x] = totals[k][x]
 
 
-def terms_kernel(info, smap, weights, inner, other_inner, outer, other_outer, inside, out):
+def terms_kernel(info, smap, weights, outer, other_outer, inner, other_inner, inside, out):
     me = info[0]
     ny = inner.shape[2]
     each = out.shape[1]
@@ -384,16 +375,7 @@
     cores = [(i, i ^ 1) for i in range(peers)]
     chips = [(i, i + 1) for i in range(1, peers - 1, 2)]
     chips = chips + [(j, i) for i, j in chips]
-    other = call(
-        plane_kernel,
-        shape(2, fields, ny, nz),
-        [SMEM, ANY],
-        1000,
-        "inner_plane",
-        [pltpu.SemaphoreType.DMA(())],
-        ANY,
-    )(info, adjoint_start)
-    other = lax.ppermute(other, "grid", cores)
+    other = lax.ppermute(adjoint_start, "grid", cores)
 
     sine_z, spec_z = sine_table(nz), spectrum(nz)
     sine_y, spec_y = sine_table(ny), spectrum(ny)
@@ -431,12 +413,10 @@
     lines = lines.reshape(peers, 3 * fields + planes, 8, nz)
     lines = lax.all_to_all(lines, "grid", 0, 0, tiled=True)
 
-    solve_x, ends_prev, ends_next, halo_prev, halo_next, solve_zb, mixes = call(
+    solve_x, halo_prev, halo_next, solve_zb, mixes = call(
         tables_b_kernel,
         (
             shape(fields, rows_b, rows_b),
-            shape(fields, 2 * nx, rows_b),
-            shape(fields, 2 * nx, rows_b),
             shape(fields, 2 * nx, 2 * nx),
             shape(fields, 2 * nx, 2 * nx),
             shape(fields, nz, nz),
@@ -446,7 +426,7 @@
         100_000_000,
         "tables_b",
         (),
-        (VMEM,) * 6 + (SMEM,),
+        (VMEM,) * 4 + (SMEM,),
     )(
         info, coup, left_map, right_map, rates, token, sine_z, spec_z,
         sine_table(nx, 8, 1), sine_table(nx, 1, 8), sine_table(nx, 2, 1), sine_table(nx, 1, 2), spectrum(nx),
@@ -454,11 +434,12 @@
 
     to_prev, to_next = call(
         ends_kernel,
-        (shape(fields, 2 * nx, nz), shape(fields, 2 * nx, nz)),
-        [VMEM] * 3,
-        50_000_000,
+        (shape(fields, nx // 4, 8, nz), shape(fields, nx // 4, 8, nz)),
+        [VMEM] * 2,
+        100_000_000,
         "solve_ends",
-    )(lines, ends_prev, ends_next)
+    )(lines, solve_x)
+    to_prev, to_next = (v.reshape(fields, 2 * nx, nz) for v in (to_prev, to_next))
 
     up = [(spot(s, b), spot(s, b + 1)) for s in range(2) for b in range(blocks - 1)]
     down = [(j, i) for i, j in up]
@@ -504,8 +485,8 @@
         [vmem(fields, ny, 2 * nz)],
     )(info, right_map, adjoint_start, step, solve_y)
 
+    other_inner = lax.ppermute(inner, "grid", cores)
     other_outer = lax.ppermute(outer, "grid", chips)
-    other_inner = lax.ppermute(inner, "grid", cores)
 
     inside = call(
         inside_kernel,
@@ -523,7 +504,7 @@
         [SMEM] * 3 + [VMEM] * 5,
         10_000_000,
         "terms",
-    )(info, smap, condition_weights, inner, other_inner, outer, other_outer, inside)
+    )(info, smap, condition_weights, outer, other_outer, inner, other_inner, inside)
     pieces = lax.all_to_all(pieces, "cond", 0, 0, tiled=True)
     scale = 1.0 / (conds * condition_weights.shape[0])
     pieces = call(

time: 146 us -> 144 us (0.986)
  waiting for transfers between devices: 36.6 us -> 41.5 us
  local copies, waits for them, and re-layouts: 9.65 us -> 6.97 us
  blocking collectives: 47 us -> 44.7 us
    all_to_all x1, waiting for transfers between devices: 16.5 us -> 20.8 us  [body(): lines = lax.all_to_all(lines, 'grid', 0, 0, tiled=True)]
    unnamed x47 -> x29, local copies, waits for them, and re-layouts: 9.55 us -> 6.87 us
    all_to_all x2, blocking collectives: 47 us -> 44.7 us  [body(): pieces = lax.all_to_all(pieces, 'cond', 0, 0, tiled=True)]
    ppermute x1, starting transfers between devices: 3.64 us -> 1.92 us  [body(): from_next = lax.ppermute(to_prev, 'grid', down)]
  transfers between devices with their start and end apart: 7 -> 7, of which waited for: 3 -> 4; matrix products, arithmetic and copies ran while one was open for 1% -> 1% of each run, Pallas kernels for 8% -> 8%
where the time goes in v8:
time: 144 us
  blocking collectives  44.7 us (31%)
  waiting for transfers between devices  41.5 us (29%)
  starting transfers between devices  26.9 us (19%)
  Pallas kernels  20.6 us (14%)
  local copies, waits for them, and re-layouts  6.97 us (5%)
  other arithmetic  1.89 us (1%)
    all_to_all x2, blocking collectives, body(): pieces = lax.all_to_all(pieces, 'cond', 0, 0, tiled=True)  44.7 us
    all_to_all x1, waiting for transfers between devices, body(): lines = lax.all_to_all(lines, 'grid', 0, 0, tiled=True)  20.8 us
    all_to_all x1, waiting for transfers between devices, body(): step = lax.all_to_all(step, 'grid', 0, 0, tiled=True)  12.7 us
    all_to_all x1, starting transfers between devices, body(): lines = lax.all_to_all(lines, 'grid', 0, 0, tiled=True)  10.4 us
    ppermute x1, waiting for transfers between devices, body(): other_outer = lax.ppermute(outer, 'grid', chips)  7.5 us
    unnamed x29, local copies, waits for them, and re-layouts  6.87 us
    ppermute x1, starting transfers between devices, body(): other_outer = lax.ppermute(outer, 'grid', chips)  4.44 us
    pallas_call x1, Pallas kernels, body(): call(tables_b_kernel, (shape(fields, rows_b, rows_b), shape(fields, 2 * n...  4.06 us
  transfers between devices with their start and end apart: 7, of which 4 were waited for; matrix products, arithmetic and copies ran while one was open for 1% of the time, Pallas kernels for 8%

profile of v8, /device:TPU:2, one launch (start us, length us, event | category | flops | bytes accessed | tf_op | source)
XLA Modules:
  0.0 143.5 jit_solution(14785441747063770270)
XLA Ops:
  0.6 1.9 %collective-permute-start = (f32[2,5,2,64,128]{4,3,2,1,0:T(8,128)}, f32[2,5,2,64,128]{4,3,2,1,0:T(8,128)S(1)}, u32[]{:S(2)}, u32[]{:S(2)}) collective-permute-start(f32[2,5,2,64,128]{4,3,2,1,0:T(8,128)} %adjoint.3), channel_id=1, source_target_pairs={{0,1},{1,0},{2,3},{3,2},{4,5},{5,4},{6,7},{7,6},{8,9},{9,8},{10,11... | collective-permute-start | bytes 1966088 | tf_op jit(solution)/shard_map/ppermute | solution.py:378
  4.0 1.5 %solve_tables.1 = (f32[2,5,128,128]{3,2,1,0:T(8,128)S(1)}, f32[2,5,64,64]{3,2,1,0:T(8,128)S(1)}) custom-call(f32[3,2,5]{2,1,0:T(2,128)S(1)} %bitcast.21, f32[128,128]{1,0:T(8,128)S(1)} %fusion.3.sine_z, f32[1,128]{1,0:T(1,128)S(1)} %multiply_add_fusion.2.spec_z, f32[64,64]{1,0:T(8,128)S(1)} %fusion.10.sine_y, f32[1,64]{1,0:T(1,128)S(1)} %multiply_add_fusion.1.spec_y), custom_call_target="tpu_custom_call" | custom-call | flops 100000000 | bytes 4000000 | tf_op jit(solution)/shard_map/solve_tables/pallas_call | solution.py:388
  5.6 1.1 copy-done
  6.7 1.1 copy-done.3
  7.8 0.8 copy-done.4
  10.0 3.9 %first_residual.1 = (f32[4,2,2,17,8,128]{5,4,3,2,1,0:T(8,128)}, f32[8,128]{1,0:T(8,128)S(1)}) custom-call(s32[4]{0:T(128)S(1)} %pad_add_fusion.info, f32[5,2,5]{2,1,0:T(2,128)S(1)} %bitcast.15, f32[5,2,5]{2,1,0:T(2,128)S(1)} %bitcast.17, f32[2,5,2,64,128]{4,3,2,1,0:T(8,128)S(1)} %copy-done, f32[2,5,2,64,128]{4,3,2,1,0:T(8,128)S(1)} %collective-permute-done.other, ...), custom_call_target="tpu_custom_call" | custom-call | flops 200000000 | bytes 4000000 | tf_op jit(solution)/shard_map/first_residual/pallas_call | solution.py:396
  14.0 10.4 %all-to-all-start = ((f32[16,17,8,128]{3,2,1,0:T(8,128)}), f32[16,17,8,128]{3,2,1,0:T(8,128)S(1)}, u32[]{:S(2)}, u32[]{:S(2)}) async-start(f32[16,17,8,128]{3,2,1,0:T(8,128)} %bitcast.8), calls=%async_computation | async-start | bytes 2228224 | tf_op jit(solution)/shard_map/all_to_all | solution.py:414
  25.7 4.1 %tables_b.1 = (f32[5,256,256]{2,1,0:T(8,128)S(1)}, f32[5,64,64]{2,1,0:T(8,128)S(1)}, f32[5,64,64]{2,1,0:T(8,128)S(1)}, f32[5,128,128]{2,1,0:T(8,128)S(1)}, f32[3,5,5]{2,1,0:T(8,128)S(1)}) custom-call(s32[4]{0:T(128)S(1)} %pad_add_fusion.info, f32[5,2,5]{2,1,0:T(2,128)S(1)} %bitcast.16, f32[5,2,5]{2,1,0:T(2,128)S(1)} %bitcast.18, f32[5,2,5]{2,1,0:T(2,128)S(1)} %bitcast.19, ...), custom_call_target="tpu_custom_call" | custom-call | flops 100000000 | bytes 4000000 | tf_op jit(solution)/shard_map/tables_b/pallas_call | solution.py:416
  29.8 20.8 %all-to-all-done.lines = f32[16,17,8,128]{3,2,1,0:T(8,128)S(1)} async-done(((f32[16,17,8,128]{3,2,1,0:T(8,128)}), f32[16,17,8,128]{3,2,1,0:T(8,128)S(1)}, u32[]{:S(2)}, u32[]{:S(2)}) %all-to-all-start) | async-done | bytes 1114144 | tf_op jit(solution)/shard_map/all_to_all | solution.py:414
  51.2 1.9 %collective-permute-start.2 = (f32[5,64,128]{2,1,0:T(8,128)S(1)}, f32[5,64,128]{2,1,0:T(8,128)S(1)}, u32[]{:S(2)}, u32[]{:S(2)}) collective-permute-start(f32[5,64,128]{2,1,0:T(8,128)S(1)} %bitcast.25), channel_id=1, source_target_pairs={{1,0},{4,1},{5,4},{8,5},{9,8},{12,9},{13,12},{3,2},{6,3},{7,6},{10... | collective-permute-start | bytes 491528 | tf_op jit(solution)/shard_map/ppermute | solution.py:447
  53.1 2.4 %collective-permute-start.1 = (f32[5,64,128]{2,1,0:T(8,128)S(1)}, f32[5,64,128]{2,1,0:T(8,128)S(1)}, u32[]{:S(2)}, u32[]{:S(2)}) collective-permute-start(f32[5,64,128]{2,1,0:T(8,128)S(1)} %bitcast.24), channel_id=1, source_target_pairs={{0,1},{1,4},{4,5},{5,8},{8,9},{9,12},{12,13},{2,3},{3,6},{6,7},{7,... | collective-permute-start | bytes 491528 | tf_op jit(solution)/shard_map/ppermute | solution.py:446
  55.5 3.7 %second_residual.1.local = f32[5,32,8,128]{3,2,1,0:T(8,128)S(1)} custom-call(s32[4]{0:T(128)S(1)} %pad_add_fusion.info, f32[3,5,5]{2,1,0:T(8,128)S(1)} %get-tuple-element.21.mixes, f32[16,17,8,128]{3,2,1,0:T(8,128)S(1)} %all-to-all-done.lines, f32[5,256,256]{2,1,0:T(8,128)S(1)} %get-tuple-element.23.solve_x, f32[5,128,128]{2,1,0:T(8,128)S(1)} %get-tuple-element.24.solve_z), custom_call_target="tpu_custom_call" | custom-call | flops 300000000 | bytes 4000000 | tf_op jit(solution)/shard_map/second_residual/pallas_call | solution.py:449
  59.8 2.0 %halo_rows.1 = (f32[16,10,8,128]{3,2,1,0:T(8,128)}, f32[8,128]{1,0:T(8,128)S(1)}) custom-call(f32[3,5,5]{2,1,0:T(8,128)S(1)} %get-tuple-element.21.mixes, f32[5,32,8,128]{3,2,1,0:T(8,128)S(1)} %second_residual.1.local, f32[5,64,128]{2,1,0:T(8,128)S(1)} %collective-permute-done.1.from_prev, f32[5,64,128]{2,1,0:T(8,128)S(1)} %collective-permute-done.2.from_next, ...), custom_call_target="tpu_custom_call" | custom-call | flops 50000000 | bytes 4000000 | tf_op jit(solution)/shard_map/halo_rows/pallas_call | solution.py:458
  61.8 3.9 %all-to-all-start.1 = ((f32[16,10,8,128]{3,2,1,0:T(8,128)}), f32[16,10,8,128]{3,2,1,0:T(8,128)S(1)}, u32[]{:S(2)}, u32[]{:S(2)}) async-start(f32[16,10,8,128]{3,2,1,0:T(8,128)} %get-tuple-element.29), calls=%async_computation.1 | async-start | bytes 1310720 | tf_op jit(solution)/shard_map/all_to_all | solution.py:468
  65.7 1.0 tables_y.1.solve_y
  66.7 12.7 %all-to-all-done.1.solved = f32[16,10,8,128]{3,2,1,0:T(8,128)S(1)} async-done(((f32[16,10,8,128]{3,2,1,0:T(8,128)}), f32[16,10,8,128]{3,2,1,0:T(8,128)S(1)}, u32[]{:S(2)}, u32[]{:S(2)}) %all-to-all-start.1) | async-done | bytes 655392 | tf_op jit(solution)/shard_map/all_to_all | solution.py:468
  79.4 2.0 %update.1 = (f32[2,5,2,64,128]{4,3,2,1,0:T(8,128)}, f32[2,5,64,128]{3,2,1,0:T(8,128)S(1)}, f32[2,5,64,128]{3,2,1,0:T(8,128)S(1)}) custom-call(s32[4]{0:T(128)S(1)} %pad_add_fusion.info, f32[5,2,5]{2,1,0:T(2,128)S(1)} %bitcast.20, f32[2,5,2,64,128]{4,3,2,1,0:T(8,128)S(1)} %copy-done.1, f32[16,10,8,128]{3,2,1,0:T(8,128)S(1)} %all-to-all-done.1.solved, ...), custom_call_target="tpu_custom_call" | custom-call | flops 60000000 | bytes 4000000 | tf_op jit(solution)/shard_map/update/pallas_call | solution.py:479
  81.3 4.4 %collective-permute-start.3 = (f32[2,5,64,128]{3,2,1,0:T(8,128)S(1)}, f32[2,5,64,128]{3,2,1,0:T(8,128)S(1)}, u32[]{:S(2)}, u32[]{:S(2)}) collective-permute-start(f32[2,5,64,128]{3,2,1,0:T(8,128)S(1)} %get-tuple-element.32.outer), channel_id=1, source_target_pairs={{1,2},{3,4},{5,6},{7,8},{9,10},{11,12},{13,14},{2,1},{4,3},{6,5},{... | collective-permute-start | bytes 983048 | tf_op jit(solution)/shard_map/ppermute | solution.py:489
  85.8 1.9 %collective-permute-start.4 = (f32[2,5,64,128]{3,2,1,0:T(8,128)S(1)}, f32[2,5,64,128]{3,2,1,0:T(8,128)S(1)}, u32[]{:S(2)}, u32[]{:S(2)}) collective-permute-start(f32[2,5,64,128]{3,2,1,0:T(8,128)S(1)} %get-tuple-element.33.inner), channel_id=1, source_target_pairs={{0,1},{1,0},{2,3},{3,2},{4,5},{5,4},{6,7},{7,6},{8,9},{9,8},{10,11... | collective-permute-start | bytes 983048 | tf_op jit(solution)/shard_map/ppermute | solution.py:488
  87.7 1.1 copy-done.2
  88.8 1.0 inside_terms.1.inside
  89.8 7.5 %collective-permute-done.3.other_outer = f32[2,5,64,128]{3,2,1,0:T(8,128)S(1)} collective-permute-done((f32[2,5,64,128]{3,2,1,0:T(8,128)S(1)}, f32[2,5,64,128]{3,2,1,0:T(8,128)S(1)}, u32[]{:S(2)}, u32[]{:S(2)}) %collective-permute-start.3) | collective-permute-done | bytes 327712 | tf_op jit(solution)/shard_map/ppermute | solution.py:489
  98.0 29.8 %all_to_all.20.pieces = f32[32,3,4,128]{3,2,1,0:T(4,128)S(1)} all-to-all(f32[32,3,4,128]{3,2,1,0:T(4,128)S(1)} %terms.1), channel_id=1, replica_groups=mesh['cond'=32,'grid'=16] {'cond'}, dimensions={0} | all-to-all | bytes 393216 | tf_op jit(solution)/shard_map/all_to_all | solution.py:508
  127.9 15.0 %all_to_all.21 = f32[32,3,4,128]{3,2,1,0:T(4,128)S(1)} all-to-all(f32[32,3,4,128]{3,2,1,0:T(4,128)S(1)} %sum_conditions.1), channel_id=1, replica_groups=mesh['cond'=32,'grid'=16] {'cond'}, dimensions={0} | all-to-all | bytes 393216 | tf_op jit(solution)/shard_map/all_to_all | solution.py:517
  (49 shorter events, 6.7 us)
Async XLA Ops:
  0.6 5.0 %collective-permute-start = (f32[2,5,2,64,128]{4,3,2,1,0:T(8,128)}, f32[2,5,2,64,128]{4,3,2,1,0:T(8,128)S(1)}, u32[]{:S(2)}, u32[]{:S(2)}) collective-permute-start(f32[2,5,2,64,128]{4,3,2,1,0:T(8,128)} %adjoint.3), channel_id=1, source_target_pairs={{0,1},{1,0},{2,3},{3,2},{4,5},{5,4},{6,7},{7,6},{8,9},{9,8},{10,11... | collective-permute-start | bytes 1966088 | tf_op jit(solution)/shard_map/ppermute | solution.py:378
  3.3 0.7 copy-start.11
  5.6 1.1 copy-start
  6.7 1.1 copy-start.3
  7.8 0.8 copy-start.4
  8.7 0.7 copy-start.6
  9.3 0.7 copy-start.8
  13.9 11.7 %copy-start.7 = (f32[2,5,5]{2,0,1:T(2,128)S(1)}, f32[2,5,5]{2,0,1:T(2,128)}, u32[]{:S(2)}) copy-start(f32[2,5,5]{2,0,1:T(2,128)} %param.12) | copy-start | bytes 604
  13.9 11.7 %copy-start.9 = (f32[2,5,5]{2,0,1:T(2,128)S(1)}, f32[2,5,5]{2,0,1:T(2,128)}, u32[]{:S(2)}) copy-start(f32[2,5,5]{2,0,1:T(2,128)} %param.13) | copy-start | bytes 604
  14.0 11.7 %copy-start.10 = (f32[2,5,5]{2,0,1:T(2,128)S(1)}, f32[2,5,5]{2,0,1:T(2,128)}, u32[]{:S(2)}) copy-start(f32[2,5,5]{2,0,1:T(2,128)} %param.14) | copy-start | bytes 604
  14.0 11.7 %copy-start.12 = (f32[2,5,3]{1,0,2:T(2,128)S(1)}, f32[2,5,3]{1,0,2:T(2,128)}, u32[]{:S(2)}) copy-start(f32[2,5,3]{1,0,2:T(2,128)} %param.15) | copy-start | bytes 364
  14.0 36.5 %all-to-all-start = ((f32[16,17,8,128]{3,2,1,0:T(8,128)}), f32[16,17,8,128]{3,2,1,0:T(8,128)S(1)}, u32[]{:S(2)}, u32[]{:S(2)}) async-start(f32[16,17,8,128]{3,2,1,0:T(8,128)} %bitcast.8), calls=%async_computation | async-start | bytes 2228224 | tf_op jit(solution)/shard_map/all_to_all | solution.py:414
  51.2 8.0 %collective-permute-start.2 = (f32[5,64,128]{2,1,0:T(8,128)S(1)}, f32[5,64,128]{2,1,0:T(8,128)S(1)}, u32[]{:S(2)}, u32[]{:S(2)}) collective-permute-start(f32[5,64,128]{2,1,0:T(8,128)S(1)} %bitcast.25), channel_id=1, source_target_pairs={{1,0},{4,1},{5,4},{8,5},{9,8},{12,9},{13,12},{3,2},{6,3},{7,6},{10... | collective-permute-start | bytes 491528 | tf_op jit(solution)/shard_map/ppermute | solution.py:447
  53.1 6.6 %collective-permute-start.1 = (f32[5,64,128]{2,1,0:T(8,128)S(1)}, f32[5,64,128]{2,1,0:T(8,128)S(1)}, u32[]{:S(2)}, u32[]{:S(2)}) collective-permute-start(f32[5,64,128]{2,1,0:T(8,128)S(1)} %bitcast.24), channel_id=1, source_target_pairs={{0,1},{1,4},{4,5},{5,8},{8,9},{9,12},{12,13},{2,3},{3,6},{6,7},{7,... | collective-permute-start | bytes 491528 | tf_op jit(solution)/shard_map/ppermute | solution.py:446
  61.8 17.6 %copy-start.1 = (f32[2,5,2,64,128]{4,3,2,1,0:T(8,128)S(1)}, f32[2,5,2,64,128]{4,3,2,1,0:T(8,128)}, u32[]{:S(2)}) copy-start(f32[2,5,2,64,128]{4,3,2,1,0:T(8,128)} %adjoint.3) | copy-start | bytes 1966084
  61.8 17.6 %all-to-all-start.1 = ((f32[16,10,8,128]{3,2,1,0:T(8,128)}), f32[16,10,8,128]{3,2,1,0:T(8,128)S(1)}, u32[]{:S(2)}, u32[]{:S(2)}) async-start(f32[16,10,8,128]{3,2,1,0:T(8,128)} %get-tuple-element.29), calls=%async_computation.1 | async-start | bytes 1310720 | tf_op jit(solution)/shard_map/all_to_all | solution.py:468
  65.7 22.0 %copy-start.5 = (f32[2,3,5]{2,0,1:T(2,128)S(1)}, f32[2,3,5]{2,0,1:T(2,128)}, u32[]{:S(2)}) copy-start(f32[2,3,5]{2,0,1:T(2,128)} %param.16) | copy-start | bytes 364
  65.7 22.0 %copy-start.13 = (s32[2]{0:T(128)S(1)}, s32[2]{0:T(128)}, u32[]{:S(2)}) copy-start(s32[2]{0:T(128)} %weights.3) | copy-start | bytes 28
  81.3 16.0 %collective-permute-start.3 = (f32[2,5,64,128]{3,2,1,0:T(8,128)S(1)}, f32[2,5,64,128]{3,2,1,0:T(8,128)S(1)}, u32[]{:S(2)}, u32[]{:S(2)}) collective-permute-start(f32[2,5,64,128]{3,2,1,0:T(8,128)S(1)} %get-tuple-element.32.outer), channel_id=1, source_target_pairs={{1,2},{3,4},{5,6},{7,8},{9,10},{11,12},{13,14},{2,1},{4,3},{6,5},{... | collective-permute-start | bytes 983048 | tf_op jit(solution)/shard_map/ppermute | solution.py:489
  85.8 11.6 %collective-permute-start.4 = (f32[2,5,64,128]{3,2,1,0:T(8,128)S(1)}, f32[2,5,64,128]{3,2,1,0:T(8,128)S(1)}, u32[]{:S(2)}, u32[]{:S(2)}) collective-permute-start(f32[2,5,64,128]{3,2,1,0:T(8,128)S(1)} %get-tuple-element.33.inner), channel_id=1, source_target_pairs={{0,1},{1,0},{2,3},{3,2},{4,5},{5,4},{6,7},{7,6},{8,9},{9,8},{10,11... | collective-permute-start | bytes 983048 | tf_op jit(solution)/shard_map/ppermute | solution.py:488
  87.7 1.1 copy-start.2

commit v9 on v8

--- a/solution.py
+++ b/solution.py
@@ -143,6 +143,12 @@
         solve_z[f] = exact(sine_z[...] / denom, sine_z[...])
 
 
+def plane_kernel(info, adjoint, inner, sem):
+    copy = pltpu.make_async_copy(adjoint.at[:, :, 1 - info[0]], inner, sem)
+    copy.start()
+    copy.wait()
+
+
 def first_kernel(info, coup, left, adjoint, other, source_in, radius, solve_z, solve_y, out, token,
                  source, made, lapped, stage, sems, out_sems):
     copies = fetch([source_in.at[c] for c in range(2)], [source.at[c] for c in range(2)], sems)
@@ -158,7 +164,7 @@
             for f in range(FIELDS):
                 v = adjoint[c, f, x]
                 beside = adjoint[c, f, 1 - x]
-                beside = beside + (other[c, f, 1] * before if x == 0 else other[c, f, 0] * after)
+                beside = beside + other[c, f] * (before if x == 0 else after)
                 beside = beside + shifted(v, 0, 1) + shifted(v, 0, -1)
                 beside = beside + shifted(v, 1, 1) + shifted(v, 1, -1)
                 lapped[x, f] = 6.0 * v - beside
@@ -375,7 +381,16 @@
     cores = [(i, i ^ 1) for i in range(peers)]
     chips = [(i, i + 1) for i in range(1, peers - 1, 2)]
     chips = chips + [(j, i) for i, j in chips]
-    other = lax.ppermute(adjoint_start, "grid", cores)
+    other = call(
+        plane_kernel,
+        shape(2, fields, ny, nz),
+        [SMEM, ANY],
+        1000,
+        "inner_plane",
+        [pltpu.SemaphoreType.DMA(())],
+        ANY,
+    )(info, adjoint_start)
+    other = lax.ppermute(other, "grid", cores)
 
     sine_z, spec_z = sine_table(nz), spectrum(nz)
     sine_y, spec_y = sine_table(ny), spectrum(ny)

time: 144 us -> 141 us (0.979)
  waiting for transfers between devices: 41.5 us -> 38.8 us
    all_to_all x1, waiting for transfers between devices: 20.8 us -> 18.1 us  [body(): lines = lax.all_to_all(lines, 'grid', 0, 0, tiled=True)]
    unnamed x29 -> x39, local copies, waits for them, and re-layouts: 6.87 us -> 6.16 us
where the time goes in v9:
time: 141 us
  blocking collectives  44.7 us (32%)
  waiting for transfers between devices  38.8 us (28%)
  starting transfers between devices  26.7 us (19%)
  Pallas kernels  21.1 us (15%)
  local copies, waits for them, and re-layouts  6.25 us (4%)
  other arithmetic  1.89 us (1%)
    all_to_all x2, blocking collectives, body(): pieces = lax.all_to_all(pieces, 'cond', 0, 0, tiled=True)  44.7 us
    all_to_all x1, waiting for transfers between devices, body(): lines = lax.all_to_all(lines, 'grid', 0, 0, tiled=True)  18.1 us
    all_to_all x1, waiting for transfers between devices, body(): step = lax.all_to_all(step, 'grid', 0, 0, tiled=True)  12.7 us
    all_to_all x1, starting transfers between devices, body(): lines = lax.all_to_all(lines, 'grid', 0, 0, tiled=True)  10.3 us
    ppermute x1, waiting for transfers between devices, body(): other_outer = lax.ppermute(outer, 'grid', chips)  7.5 us
    unnamed x39, local copies, waits for them, and re-layouts  6.16 us
    ppermute x1, starting transfers between devices, body(): other_outer = lax.ppermute(outer, 'grid', chips)  4.44 us
    pallas_call x1, Pallas kernels, body(): call(tables_b_kernel, (shape(fields, rows_b, rows_b), shape(fields, 2 * n...  4.05 us
  transfers between devices with their start and end apart: 7, of which 4 were waited for; matrix products, arithmetic and copies ran while one was open for 1% of the time, Pallas kernels for 8%

profile of v9, /device:TPU:2, one launch (start us, length us, event | category | flops | bytes accessed | tf_op | source)
XLA Modules:
  0.0 140.6 jit_solution(5102915612674834305)
XLA Ops:
  0.8 1.1 copy-done
  2.5 1.9 %collective-permute-start = (f32[2,5,64,128]{3,2,1,0:T(8,128)S(1)}, f32[2,5,64,128]{3,2,1,0:T(8,128)S(1)}, u32[]{:S(2)}, u32[]{:S(2)}) collective-permute-start(f32[2,5,64,128]{3,2,1,0:T(8,128)S(1)} %inner_plane.1), channel_id=1, source_target_pairs={{0,1},{1,0},{2,3},{3,2},{4,5},{5,4},{6,7},{7,6},{8,9},{9,8},{10,11... | collective-permute-start | bytes 983048 | tf_op jit(solution)/shard_map/ppermute | solution.py:393
  5.1 1.6 %solve_tables.1 = (f32[2,5,128,128]{3,2,1,0:T(8,128)S(1)}, f32[2,5,64,64]{3,2,1,0:T(8,128)S(1)}) custom-call(f32[3,2,5]{2,1,0:T(2,128)S(1)} %bitcast.21, f32[128,128]{1,0:T(8,128)S(1)} %fusion.3.sine_z, f32[1,128]{1,0:T(1,128)S(1)} %multiply_add_fusion.2.spec_z, f32[64,64]{1,0:T(8,128)S(1)} %fusion.10.sine_y, f32[1,64]{1,0:T(1,128)S(1)} %multiply_add_fusion.1.spec_y), custom_call_target="tpu_custom_call" | custom-call | flops 100000000 | bytes 4000000 | tf_op jit(solution)/shard_map/solve_tables/pallas_call | solution.py:403
  6.7 3.8 %first_residual.1 = (f32[4,2,2,17,8,128]{5,4,3,2,1,0:T(8,128)}, f32[8,128]{1,0:T(8,128)S(1)}) custom-call(s32[4]{0:T(128)S(1)} %pad_add_fusion.info, f32[5,2,5]{2,1,0:T(2,128)S(1)} %bitcast.15, f32[5,2,5]{2,1,0:T(2,128)S(1)} %bitcast.17, f32[2,5,2,64,128]{4,3,2,1,0:T(8,128)S(1)} %copy-done.1, f32[2,5,64,128]{3,2,1,0:T(8,128)S(1)} %collective-permute-done.other, ...), custom_call_target="tpu_custom_call" | custom-call | flops 200000000 | bytes 4000000 | tf_op jit(solution)/shard_map/first_residual/pallas_call | solution.py:411
  11.2 10.3 %all-to-all-start = ((f32[16,17,8,128]{3,2,1,0:T(8,128)}), f32[16,17,8,128]{3,2,1,0:T(8,128)S(1)}, u32[]{:S(2)}, u32[]{:S(2)}) async-start(f32[16,17,8,128]{3,2,1,0:T(8,128)} %bitcast.8), calls=%async_computation | async-start | bytes 2228224 | tf_op jit(solution)/shard_map/all_to_all | solution.py:429
  22.8 0.7 copy-done.16
  24.2 4.0 %tables_b.1 = (f32[5,256,256]{2,1,0:T(8,128)S(1)}, f32[5,64,64]{2,1,0:T(8,128)S(1)}, f32[5,64,64]{2,1,0:T(8,128)S(1)}, f32[5,128,128]{2,1,0:T(8,128)S(1)}, f32[3,5,5]{2,1,0:T(8,128)S(1)}) custom-call(s32[4]{0:T(128)S(1)} %pad_add_fusion.info, f32[5,2,5]{2,1,0:T(2,128)S(1)} %bitcast.16, f32[5,2,5]{2,1,0:T(2,128)S(1)} %bitcast.18, f32[5,2,5]{2,1,0:T(2,128)S(1)} %bitcast.19, ...), custom_call_target="tpu_custom_call" | custom-call | flops 100000000 | bytes 4000000 | tf_op jit(solution)/shard_map/tables_b/pallas_call | solution.py:431
  29.6 18.1 %all-to-all-done.lines = f32[16,17,8,128]{3,2,1,0:T(8,128)S(1)} async-done(((f32[16,17,8,128]{3,2,1,0:T(8,128)}), f32[16,17,8,128]{3,2,1,0:T(8,128)S(1)}, u32[]{:S(2)}, u32[]{:S(2)}) %all-to-all-start) | async-done | bytes 1114144 | tf_op jit(solution)/shard_map/all_to_all | solution.py:429
  48.4 1.9 %collective-permute-start.2 = (f32[5,64,128]{2,1,0:T(8,128)S(1)}, f32[5,64,128]{2,1,0:T(8,128)S(1)}, u32[]{:S(2)}, u32[]{:S(2)}) collective-permute-start(f32[5,64,128]{2,1,0:T(8,128)S(1)} %bitcast.25), channel_id=1, source_target_pairs={{1,0},{4,1},{5,4},{8,5},{9,8},{12,9},{13,12},{3,2},{6,3},{7,6},{10... | collective-permute-start | bytes 491528 | tf_op jit(solution)/shard_map/ppermute | solution.py:462
  50.3 2.4 %collective-permute-start.1 = (f32[5,64,128]{2,1,0:T(8,128)S(1)}, f32[5,64,128]{2,1,0:T(8,128)S(1)}, u32[]{:S(2)}, u32[]{:S(2)}) collective-permute-start(f32[5,64,128]{2,1,0:T(8,128)S(1)} %bitcast.24), channel_id=1, source_target_pairs={{0,1},{1,4},{4,5},{5,8},{8,9},{9,12},{12,13},{2,3},{3,6},{6,7},{7,... | collective-permute-start | bytes 491528 | tf_op jit(solution)/shard_map/ppermute | solution.py:461
  52.7 3.7 %second_residual.1.local = f32[5,32,8,128]{3,2,1,0:T(8,128)S(1)} custom-call(s32[4]{0:T(128)S(1)} %pad_add_fusion.info, f32[3,5,5]{2,1,0:T(8,128)S(1)} %get-tuple-element.21.mixes, f32[16,17,8,128]{3,2,1,0:T(8,128)S(1)} %all-to-all-done.lines, f32[5,256,256]{2,1,0:T(8,128)S(1)} %get-tuple-element.23.solve_x, f32[5,128,128]{2,1,0:T(8,128)S(1)} %get-tuple-element.24.solve_z), custom_call_target="tpu_custom_call" | custom-call | flops 300000000 | bytes 4000000 | tf_op jit(solution)/shard_map/second_residual/pallas_call | solution.py:464
  57.0 2.0 %halo_rows.1 = (f32[16,10,8,128]{3,2,1,0:T(8,128)}, f32[8,128]{1,0:T(8,128)S(1)}) custom-call(f32[3,5,5]{2,1,0:T(8,128)S(1)} %get-tuple-element.21.mixes, f32[5,32,8,128]{3,2,1,0:T(8,128)S(1)} %second_residual.1.local, f32[5,64,128]{2,1,0:T(8,128)S(1)} %collective-permute-done.1.from_prev, f32[5,64,128]{2,1,0:T(8,128)S(1)} %collective-permute-done.2.from_next, ...), custom_call_target="tpu_custom_call" | custom-call | flops 50000000 | bytes 4000000 | tf_op jit(solution)/shard_map/halo_rows/pallas_call | solution.py:473
  59.0 3.8 %all-to-all-start.1 = ((f32[16,10,8,128]{3,2,1,0:T(8,128)}), f32[16,10,8,128]{3,2,1,0:T(8,128)S(1)}, u32[]{:S(2)}, u32[]{:S(2)}) async-start(f32[16,10,8,128]{3,2,1,0:T(8,128)} %get-tuple-element.29), calls=%async_computation.1 | async-start | bytes 1310720 | tf_op jit(solution)/shard_map/all_to_all | solution.py:483
  62.8 1.0 tables_y.1.solve_y
  63.8 12.7 %all-to-all-done.1.solved = f32[16,10,8,128]{3,2,1,0:T(8,128)S(1)} async-done(((f32[16,10,8,128]{3,2,1,0:T(8,128)}), f32[16,10,8,128]{3,2,1,0:T(8,128)S(1)}, u32[]{:S(2)}, u32[]{:S(2)}) %all-to-all-start.1) | async-done | bytes 655392 | tf_op jit(solution)/shard_map/all_to_all | solution.py:483
  76.4 1.9 %update.1 = (f32[2,5,2,64,128]{4,3,2,1,0:T(8,128)}, f32[2,5,64,128]{3,2,1,0:T(8,128)S(1)}, f32[2,5,64,128]{3,2,1,0:T(8,128)S(1)}) custom-call(s32[4]{0:T(128)S(1)} %pad_add_fusion.info, f32[5,2,5]{2,1,0:T(2,128)S(1)} %bitcast.20, f32[2,5,2,64,128]{4,3,2,1,0:T(8,128)S(1)} %copy-done.1, f32[16,10,8,128]{3,2,1,0:T(8,128)S(1)} %all-to-all-done.1.solved, ...), custom_call_target="tpu_custom_call" | custom-call | flops 60000000 | bytes 4000000 | tf_op jit(solution)/shard_map/update/pallas_call | solution.py:494
  78.4 4.4 %collective-permute-start.3 = (f32[2,5,64,128]{3,2,1,0:T(8,128)S(1)}, f32[2,5,64,128]{3,2,1,0:T(8,128)S(1)}, u32[]{:S(2)}, u32[]{:S(2)}) collective-permute-start(f32[2,5,64,128]{3,2,1,0:T(8,128)S(1)} %get-tuple-element.32.outer), channel_id=1, source_target_pairs={{1,2},{3,4},{5,6},{7,8},{9,10},{11,12},{13,14},{2,1},{4,3},{6,5},{... | collective-permute-start | bytes 983048 | tf_op jit(solution)/shard_map/ppermute | solution.py:504
  82.8 1.9 %collective-permute-start.4 = (f32[2,5,64,128]{3,2,1,0:T(8,128)S(1)}, f32[2,5,64,128]{3,2,1,0:T(8,128)S(1)}, u32[]{:S(2)}, u32[]{:S(2)}) collective-permute-start(f32[2,5,64,128]{3,2,1,0:T(8,128)S(1)} %get-tuple-element.33.inner), channel_id=1, source_target_pairs={{0,1},{1,0},{2,3},{3,2},{4,5},{5,4},{6,7},{7,6},{8,9},{9,8},{10,11... | collective-permute-start | bytes 983048 | tf_op jit(solution)/shard_map/ppermute | solution.py:503
  84.8 1.1 copy-done.3
  85.9 1.0 inside_terms.1.inside
  86.9 7.5 %collective-permute-done.3.other_outer = f32[2,5,64,128]{3,2,1,0:T(8,128)S(1)} collective-permute-done((f32[2,5,64,128]{3,2,1,0:T(8,128)S(1)}, f32[2,5,64,128]{3,2,1,0:T(8,128)S(1)}, u32[]{:S(2)}, u32[]{:S(2)}) %collective-permute-start.3) | collective-permute-done | bytes 327712 | tf_op jit(solution)/shard_map/ppermute | solution.py:504
  94.4 0.7 terms.1
  95.1 29.8 %all_to_all.20.pieces = f32[32,3,4,128]{3,2,1,0:T(4,128)S(1)} all-to-all(f32[32,3,4,128]{3,2,1,0:T(4,128)S(1)} %terms.1), channel_id=1, replica_groups=mesh['cond'=32,'grid'=16] {'cond'}, dimensions={0} | all-to-all | bytes 393216 | tf_op jit(solution)/shard_map/all_to_all | solution.py:523
  124.9 15.0 %all_to_all.21 = f32[32,3,4,128]{3,2,1,0:T(4,128)S(1)} all-to-all(f32[32,3,4,128]{3,2,1,0:T(4,128)S(1)} %sum_conditions.1), channel_id=1, replica_groups=mesh['cond'=32,'grid'=16] {'cond'}, dimensions={0} | all-to-all | bytes 393216 | tf_op jit(solution)/shard_map/all_to_all | solution.py:532
  (60 shorter events, 7.1 us)
Async XLA Ops:
  0.6 4.5 %copy-start.13 = (f32[2,5,3]{1,0,2:T(2,128)S(1)}, f32[2,5,3]{1,0,2:T(2,128)}, u32[]{:S(2)}) copy-start(f32[2,5,3]{1,0,2:T(2,128)} %param.15) | copy-start | bytes 364
  0.6 6.0 %copy-start.11 = (f32[2,5,5]{2,0,1:T(2,128)S(1)}, f32[2,5,5]{2,0,1:T(2,128)}, u32[]{:S(2)}) copy-start(f32[2,5,5]{2,0,1:T(2,128)} %param.13) | copy-start | bytes 604
  0.7 6.0 %copy-start.10 = (f32[2,5,5]{2,0,1:T(2,128)S(1)}, f32[2,5,5]{2,0,1:T(2,128)}, u32[]{:S(2)}) copy-start(f32[2,5,5]{2,0,1:T(2,128)} %param.12) | copy-start | bytes 604
  0.7 6.0 %copy-start.8 = (f32[2,64,128]{2,1,0:T(8,128)S(1)}, f32[2,64,128]{2,1,0:T(8,128)}, u32[]{:S(2)}) copy-start(f32[2,64,128]{2,1,0:T(8,128)} %radius.1) | copy-start | bytes 196612
  0.8 1.1 copy-start
  1.9 4.8 %copy-start.1 = (f32[2,5,2,64,128]{4,3,2,1,0:T(8,128)S(1)}, f32[2,5,2,64,128]{4,3,2,1,0:T(8,128)}, u32[]{:S(2)}) copy-start(f32[2,5,2,64,128]{4,3,2,1,0:T(8,128)} %adjoint.5) | copy-start | bytes 1966084
  1.9 4.8 %copy-start.2 = (f32[2,5,2,64,128]{4,3,2,1,0:T(8,128)S(1)}, f32[2,5,2,64,128]{4,3,2,1,0:T(8,128)}, u32[]{:S(2)}) copy-start(f32[2,5,2,64,128]{4,3,2,1,0:T(8,128)} %source_in.1) | copy-start | bytes 1966084
  2.5 4.2 %collective-permute-start = (f32[2,5,64,128]{3,2,1,0:T(8,128)S(1)}, f32[2,5,64,128]{3,2,1,0:T(8,128)S(1)}, u32[]{:S(2)}, u32[]{:S(2)}) collective-permute-start(f32[2,5,64,128]{3,2,1,0:T(8,128)S(1)} %inner_plane.1), channel_id=1, source_target_pairs={{0,1},{1,0},{2,3},{3,2},{4,5},{5,4},{6,7},{7,6},{8,9},{9,8},{10,11... | collective-permute-start | bytes 983048 | tf_op jit(solution)/shard_map/ppermute | solution.py:393
  4.5 6.1 %copy-start.17 = (f32[1,128]{1,0:T(1,128)}, f32[1,128]{1,0:T(1,128)S(1)}, u32[]{:S(2)}) copy-start(f32[1,128]{1,0:T(1,128)S(1)} %multiply_add_fusion.2.spec_z) | copy-start | bytes 1540
  11.2 11.7 %copy-start.12 = (f32[2,5,5]{2,0,1:T(2,128)S(1)}, f32[2,5,5]{2,0,1:T(2,128)}, u32[]{:S(2)}) copy-start(f32[2,5,5]{2,0,1:T(2,128)} %param.14) | copy-start | bytes 604
  11.2 36.5 %all-to-all-start = ((f32[16,17,8,128]{3,2,1,0:T(8,128)}), f32[16,17,8,128]{3,2,1,0:T(8,128)S(1)}, u32[]{:S(2)}, u32[]{:S(2)}) async-start(f32[16,17,8,128]{3,2,1,0:T(8,128)} %bitcast.8), calls=%async_computation | async-start | bytes 2228224 | tf_op jit(solution)/shard_map/all_to_all | solution.py:429
  22.8 0.7 copy-start.16
  28.2 0.7 copy-start.4
  28.9 0.7 copy-start.6
  48.4 8.1 %collective-permute-start.2 = (f32[5,64,128]{2,1,0:T(8,128)S(1)}, f32[5,64,128]{2,1,0:T(8,128)S(1)}, u32[]{:S(2)}, u32[]{:S(2)}) collective-permute-start(f32[5,64,128]{2,1,0:T(8,128)S(1)} %bitcast.25), channel_id=1, source_target_pairs={{1,0},{4,1},{5,4},{8,5},{9,8},{12,9},{13,12},{3,2},{6,3},{7,6},{10... | collective-permute-start | bytes 491528 | tf_op jit(solution)/shard_map/ppermute | solution.py:462
  50.3 6.6 %collective-permute-start.1 = (f32[5,64,128]{2,1,0:T(8,128)S(1)}, f32[5,64,128]{2,1,0:T(8,128)S(1)}, u32[]{:S(2)}, u32[]{:S(2)}) collective-permute-start(f32[5,64,128]{2,1,0:T(8,128)S(1)} %bitcast.24), channel_id=1, source_target_pairs={{0,1},{1,4},{4,5},{5,8},{8,9},{9,12},{12,13},{2,3},{3,6},{6,7},{7,... | collective-permute-start | bytes 491528 | tf_op jit(solution)/shard_map/ppermute | solution.py:461
  52.7 4.2 %copy-start.5 = (f32[5,64,64]{2,1,0:T(8,128)S(1)}, f32[5,64,64]{2,1,0:T(8,128)}, u32[]{:S(2)}) copy-start(f32[5,64,64]{2,1,0:T(8,128)} %copy-done.4) | copy-start | bytes 245764
  52.7 4.2 %copy-start.7 = (f32[5,64,64]{2,1,0:T(8,128)S(1)}, f32[5,64,64]{2,1,0:T(8,128)}, u32[]{:S(2)}) copy-start(f32[5,64,64]{2,1,0:T(8,128)} %copy-done.6) | copy-start | bytes 245764
  59.0 17.5 %all-to-all-start.1 = ((f32[16,10,8,128]{3,2,1,0:T(8,128)}), f32[16,10,8,128]{3,2,1,0:T(8,128)S(1)}, u32[]{:S(2)}, u32[]{:S(2)}) async-start(f32[16,10,8,128]{3,2,1,0:T(8,128)} %get-tuple-element.29), calls=%async_computation.1 | async-start | bytes 1310720 | tf_op jit(solution)/shard_map/all_to_all | solution.py:483
  62.7 22.0 %copy-start.9 = (f32[2,3,5]{2,0,1:T(2,128)S(1)}, f32[2,3,5]{2,0,1:T(2,128)}, u32[]{:S(2)}) copy-start(f32[2,3,5]{2,0,1:T(2,128)} %param.16) | copy-start | bytes 364
  62.7 22.0 %copy-start.14 = (s32[2]{0:T(128)S(1)}, s32[2]{0:T(128)}, u32[]{:S(2)}) copy-start(s32[2]{0:T(128)} %weights.3) | copy-start | bytes 28
  78.4 16.0 %collective-permute-start.3 = (f32[2,5,64,128]{3,2,1,0:T(8,128)S(1)}, f32[2,5,64,128]{3,2,1,0:T(8,128)S(1)}, u32[]{:S(2)}, u32[]{:S(2)}) collective-permute-start(f32[2,5,64,128]{3,2,1,0:T(8,128)S(1)} %get-tuple-element.32.outer), channel_id=1, source_target_pairs={{1,2},{3,4},{5,6},{7,8},{9,10},{11,12},{13,14},{2,1},{4,3},{6,5},{... | collective-permute-start | bytes 983048 | tf_op jit(solution)/shard_map/ppermute | solution.py:504
  82.8 11.5 %collective-permute-start.4 = (f32[2,5,64,128]{3,2,1,0:T(8,128)S(1)}, f32[2,5,64,128]{3,2,1,0:T(8,128)S(1)}, u32[]{:S(2)}, u32[]{:S(2)}) collective-permute-start(f32[2,5,64,128]{3,2,1,0:T(8,128)S(1)} %get-tuple-element.33.inner), channel_id=1, source_target_pairs={{0,1},{1,0},{2,3},{3,2},{4,5},{5,4},{6,7},{7,6},{8,9},{9,8},{10,11... | collective-permute-start | bytes 983048 | tf_op jit(solution)/shard_map/ppermute | solution.py:503
  84.8 1.1 copy-start.3
  (2 other events, 1.3 us)

commit v10 on v9

--- a/solution.py
+++ b/solution.py
@@ -24,8 +24,16 @@
 
 def dot(a, b):
     one = functools.partial(jnp.dot, preferred_element_type=F32)
-    (a_high, a_low), (b_high, b_low) = split(a), split(b)
+    (a_high, a_low), (b_high, b_low) = (v if isinstance(v, tuple) else split(v) for v in (a, b))
     return one(a_high, b_high) + (one(a_high, b_low) + one(a_low, b_high))
+
+
+def keep(ref, at, v):
+    ref[(0, *at)], ref[(1, *at)] = split(v)
+
+
+def kept_at(ref, *at):
+    return ref[(0, *at)], ref[(1, *at)]
 
 
 def exact(a, b):
@@ -65,6 +73,10 @@
     return jax.ShapeDtypeStruct(dims, F32)
 
 
+def parts(*dims):
+    return jax.ShapeDtypeStruct((2, *dims), jnp.bfloat16)
+
+
 def vmem(*dims):
     return pltpu.VMEM(dims, F32)
 
@@ -98,16 +110,16 @@
     for c in range(2):
         for f in range(FIELDS):
             denom = 1.0 + rates[2, c, f] * spec_z[...]
-            solve_z[c, f] = exact(sine_z[...] / denom, sine_z[...])
+            keep(solve_z, (c, f), exact(sine_z[...] / denom, sine_z[...]))
             denom = 1.0 + rates[1, c, f] * spec_y[...]
-            solve_y[c, f] = exact(sine_y[...] / denom, sine_y[...])
+            keep(solve_y, (c, f), exact(sine_y[...] / denom, sine_y[...]))
 
 
 def tables_y_kernel(rates, token, sine_y, spec_y, solve_y):
     for c in range(2):
         for f in range(FIELDS):
             denom = 1.0 + rates[1, c, f] * spec_y[...]
-            solve_y[c, f] = exact(sine_y[...] / denom, sine_y[...])
+            keep(solve_y, (c, f), exact(sine_y[...] / denom, sine_y[...]))
 
 
 def tables_b_kernel(info, coup, left_map, right_map, rates, token, sine_z, spec_z, left, right, left_2, right_2, spec_x,
@@ -134,13 +146,13 @@
     for f in range(FIELDS):
         denom = 1.0 + rates[0, mine, f] * spec_x[...]
         scaled = left[...] / denom
-        solve_x[f] = jnp.where(same, exact(scaled, right[...]), 0.0)
+        keep(solve_x, (f,), jnp.where(same, exact(scaled, right[...]), 0.0))
         scaled_2 = left_2[...] / denom
         both = exact(scaled_2, right_2[...])
-        halo_prev[f] = jnp.where(from_last, both, 0.0)
-        halo_next[f] = jnp.where(from_first, both, 0.0)
+        keep(halo_prev, (f,), jnp.where(from_last, both, 0.0))
+        keep(halo_next, (f,), jnp.where(from_first, both, 0.0))
         denom = 1.0 + rates[2, mine, f] * spec_z[...]
-        solve_z[f] = exact(sine_z[...] / denom, sine_z[...])
+        keep(solve_z, (f,), exact(sine_z[...] / denom, sine_z[...]))
 
 
 def plane_kernel(info, adjoint, inner, sem):
@@ -184,9 +196,9 @@
         for f in range(FIELDS):
             stage[f, 2 * ny : 3 * ny] = mixed(lambda g: left[f, c, g], outer)
         for f in range(FIELDS):
-            r = dot(stage[f], solve_z[c, f])
+            r = dot(stage[f], kept_at(solve_z, c, f))
             r = jnp.concatenate([r[p * ny : p * ny + ny] for p in range(3)], axis=1)
-            r = dot(solve_y[c, f], r)
+            r = dot(kept_at(solve_y, c, f), r)
             for p in range(3):
                 for b in range(blocks):
                     made[b // 2, c, b % 2, 3 * f + p] = r[8 * b : 8 * b + 8, 128 * p : 128 * p + 128]
@@ -208,9 +220,9 @@
 
 
 def ends_kernel(lines, solve_x, to_prev, to_next):
-    n = solve_x.shape[1]
+    n = solve_x.shape[2]
     for f in range(FIELDS):
-        u = dot(solve_x[f], assembled(lines, f).reshape(n, 128))
+        u = dot(kept_at(solve_x, f), assembled(lines, f).reshape(n, 128))
         quad = u.reshape(n // 32, 4, 8, 128)
         for j in range(4):
             to_prev[f, :, 2 * j : 2 * j + 2, :] = quad[:, j, 0:2, :]
@@ -224,7 +236,7 @@
     has_prev, has_next = info[2].astype(F32), info[3].astype(F32)
     zero = jnp.zeros((1, 8, 128), F32)
     for f in range(FIELDS):
-        u = dot(solve_x[f], assembled(lines, f).reshape(nx * 8, 128)).reshape(full)
+        u = dot(kept_at(solve_x, f), assembled(lines, f).reshape(nx * 8, 128)).reshape(full)
         solved[f] = u
         up = jnp.where(row == 7, 0.0, pltpu.roll(u, 7, 1))
         down = jnp.where(row == 0, 0.0, pltpu.roll(u, 1, 1))
@@ -242,7 +254,7 @@
         near = mixed(lambda g: mixes[0, f, g], solved)
         far = mixed(lambda g: mixes[1, f, g], lapped)
         v = (sr * near + far).reshape(nx * 8, 128)
-        v = dot(solve_x[f], dot(v, solve_z[f]))
+        v = dot(kept_at(solve_x, f), dot(v, kept_at(solve_z, f)))
         out[f] = kept[f] - v.reshape(full)
 
 
@@ -258,13 +270,13 @@
         far = jnp.concatenate(
             [mixed(lambda g: mixes[1, f, g], from_prev), mixed(lambda g: mixes[1, f, g], from_next)], axis=0
         )
-        far = dot(far, solve_z[f])
+        far = dot(far, kept_at(solve_z, f))
         far_prev, far_next = far[: 2 * nx], far[2 * nx :]
         scale = 2.0 * mixes[2, f, 0]
         add_prev = jnp.where(odd, first, first - 5.0 * pltpu.roll(first, 2 * nx - 1, 0))
         add_next = jnp.where(odd, last - 5.0 * pltpu.roll(last, 1, 0), last)
-        add_prev = scale * add_prev + dot(halo_prev[f], far_prev)
-        add_next = scale * add_next + dot(halo_next[f], far_next)
+        add_prev = scale * add_prev + dot(kept_at(halo_prev, f), far_prev)
+        add_next = scale * add_next + dot(kept_at(halo_next, f), far_next)
         spread = lambda v, at: jnp.stack(
             [pltpu.roll(v.reshape(nx // 4, 8, 128), (at - 2 * j) % 8, 1) for j in range(4)], axis=1
         ).reshape(full)
@@ -289,7 +301,7 @@
     for c in range(2):
         for f in range(FIELDS):
             q = jnp.concatenate([gathered(solved, c, 2 * f + x, ny // 8) for x in range(2)], axis=1)
-            step[f] = dot(solve_y[c, f], q)
+            step[f] = dot(kept_at(solve_y, c, f), q)
         steps = [[step[g, :, 128 * x : 128 * x + 128] for g in range(FIELDS)] for x in range(2)]
         for f in range(FIELDS):
             planes = [adjoint[c, f, x] + mixed(lambda g: right[f, c, g], steps[x]) for x in range(2)]
@@ -402,7 +414,7 @@
 
     solve_z, solve_y = call(
         tables_kernel,
-        (shape(2, fields, nz, nz), shape(2, fields, ny, ny)),
+        (parts(2, fields, nz, nz), parts(2, fields, ny, ny)),
         [SMEM] + [VMEM] * 4,
         100_000_000,
         "solve_tables",
@@ -431,10 +443,10 @@
     solve_x, halo_prev, halo_next, solve_zb, mixes = call(
         tables_b_kernel,
         (
-            shape(fields, rows_b, rows_b),
-            shape(fields, 2 * nx, 2 * nx),
-            shape(fields, 2 * nx, 2 * nx),
-            shape(fields, nz, nz),
+            parts(fields, rows_b, rows_b),
+            parts(fields, 2 * nx, 2 * nx),
+            parts(fields, 2 * nx, 2 * nx),
+            parts(fields, nz, nz),
             shape(3, fields, fields),
         ),
         [SMEM] * 5 + [VMEM] * 8,
@@ -484,7 +496,7 @@
 
     solve_y = call(
         tables_y_kernel,
-        shape(2, fields, ny, ny),
+        parts(2, fields, ny, ny),
         [SMEM, VMEM, VMEM, VMEM],
         50_000_000,
         "tables_y",

time: 141 us -> 141 us (level)
  no operation moved by 1% of the time
where the time goes in v10:
time: 141 us
  blocking collectives  44.7 us (32%)
  waiting for transfers between devices  38.8 us (28%)
  starting transfers between devices  26.7 us (19%)
  Pallas kernels  21.1 us (15%)
  local copies, waits for them, and re-layouts  6.25 us (4%)
  other arithmetic  1.89 us (1%)
    all_to_all x2, blocking collectives, body(): pieces = lax.all_to_all(pieces, 'cond', 0, 0, tiled=True)  44.7 us
    all_to_all x1, waiting for transfers between devices, body(): lines = lax.all_to_all(lines, 'grid', 0, 0, tiled=True)  18.1 us
    all_to_all x1, waiting for transfers between devices, body(): step = lax.all_to_all(step, 'grid', 0, 0, tiled=True)  12.7 us
    all_to_all x1, starting transfers between devices, body(): lines = lax.all_to_all(lines, 'grid', 0, 0, tiled=True)  10.3 us
    ppermute x1, waiting for transfers between devices, body(): other_outer = lax.ppermute(outer, 'grid', chips)  7.49 us
    unnamed x39, local copies, waits for them, and re-layouts  6.16 us
    ppermute x1, starting transfers between devices, body(): other_outer = lax.ppermute(outer, 'grid', chips)  4.44 us
    pallas_call x1, Pallas kernels, body(): call(tables_b_kernel, (parts(fields, rows_b, rows_b), parts(fields, 2 * n...  4.09 us
  transfers between devices with their start and end apart: 7, of which 4 were waited for; matrix products, arithmetic and copies ran while one was open for 1% of the time, Pallas kernels for 8%

profile of v10, /device:TPU:2, one launch (start us, length us, event | category | flops | bytes accessed | tf_op | source)
XLA Modules:
  0.0 140.6 jit_solution(5283529108281503341)
XLA Ops:
  0.8 1.1 copy-done
  2.5 1.9 %collective-permute-start = (f32[2,5,64,128]{3,2,1,0:T(8,128)S(1)}, f32[2,5,64,128]{3,2,1,0:T(8,128)S(1)}, u32[]{:S(2)}, u32[]{:S(2)}) collective-permute-start(f32[2,5,64,128]{3,2,1,0:T(8,128)S(1)} %inner_plane.1), channel_id=1, source_target_pairs={{0,1},{1,0},{2,3},{3,2},{4,5},{5,4},{6,7},{7,6},{8,9},{9,8},{10,11... | collective-permute-start | bytes 983048 | tf_op jit(solution)/shard_map/ppermute | solution.py:405
  5.1 1.6 %solve_tables.1 = (bf16[2,2,5,128,128]{4,3,2,1,0:T(8,128)(2,1)S(1)}, bf16[2,2,5,64,64]{4,3,2,1,0:T(8,128)(2,1)S(1)}) custom-call(f32[3,2,5]{2,1,0:T(2,128)S(1)} %bitcast.21, f32[128,128]{1,0:T(8,128)S(1)} %fusion.3.sine_z, f32[1,128]{1,0:T(1,128)S(1)} %multiply_add_fusion.2.spec_z, f32[64,64]{1,0:T(8,128)S(1)} %fusion.10.sine_y, ...), custom_call_target="tpu_custom_call" | custom-call | flops 100000000 | bytes 4000000 | tf_op jit(solution)/shard_map/solve_tables/pallas_call | solution.py:415
  6.7 3.8 %first_residual.1 = (f32[4,2,2,17,8,128]{5,4,3,2,1,0:T(8,128)}, f32[8,128]{1,0:T(8,128)S(1)}) custom-call(s32[4]{0:T(128)S(1)} %pad_add_fusion.info, f32[5,2,5]{2,1,0:T(2,128)S(1)} %bitcast.15, f32[5,2,5]{2,1,0:T(2,128)S(1)} %bitcast.17, f32[2,5,2,64,128]{4,3,2,1,0:T(8,128)S(1)} %copy-done.1, f32[2,5,64,128]{3,2,1,0:T(8,128)S(1)} %collective-permute-done.other, ...), custom_call_target="tpu_custom_call" | custom-call | flops 200000000 | bytes 4000000 | tf_op jit(solution)/shard_map/first_residual/pallas_call | solution.py:423
  11.2 10.3 %all-to-all-start = ((f32[16,17,8,128]{3,2,1,0:T(8,128)}), f32[16,17,8,128]{3,2,1,0:T(8,128)S(1)}, u32[]{:S(2)}, u32[]{:S(2)}) async-start(f32[16,17,8,128]{3,2,1,0:T(8,128)} %bitcast.8), calls=%async_computation | async-start | bytes 2228224 | tf_op jit(solution)/shard_map/all_to_all | solution.py:441
  22.9 0.7 copy-done.16
  24.2 4.1 %tables_b.1 = (bf16[2,5,256,256]{3,2,1,0:T(8,128)(2,1)S(1)}, bf16[2,5,64,64]{3,2,1,0:T(8,128)(2,1)S(1)}, bf16[2,5,64,64]{3,2,1,0:T(8,128)(2,1)S(1)}, bf16[2,5,128,128]{3,2,1,0:T(8,128)(2,1)S(1)}, f32[3,5,5]{2,1,0:T(8,128)S(1)}) custom-call(s32[4]{0:T(128)S(1)} %pad_add_fusion.info, f32[5,2,5]{2,1,0:T(2,128)S(1)} %bitcast.16, f32[5,2,5]{2,1,0:T(2,128)S(1)} %bitcast.18, ...), custom_call_target="tpu_custom_call" | custom-call | flops 100000000 | bytes 4000000 | tf_op jit(solution)/shard_map/tables_b/pallas_call | solution.py:443
  29.6 18.1 %all-to-all-done.lines = f32[16,17,8,128]{3,2,1,0:T(8,128)S(1)} async-done(((f32[16,17,8,128]{3,2,1,0:T(8,128)}), f32[16,17,8,128]{3,2,1,0:T(8,128)S(1)}, u32[]{:S(2)}, u32[]{:S(2)}) %all-to-all-start) | async-done | bytes 1114144 | tf_op jit(solution)/shard_map/all_to_all | solution.py:441
  48.4 1.9 %collective-permute-start.2 = (f32[5,64,128]{2,1,0:T(8,128)S(1)}, f32[5,64,128]{2,1,0:T(8,128)S(1)}, u32[]{:S(2)}, u32[]{:S(2)}) collective-permute-start(f32[5,64,128]{2,1,0:T(8,128)S(1)} %bitcast.25), channel_id=1, source_target_pairs={{1,0},{4,1},{5,4},{8,5},{9,8},{12,9},{13,12},{3,2},{6,3},{7,6},{10... | collective-permute-start | bytes 491528 | tf_op jit(solution)/shard_map/ppermute | solution.py:474
  50.3 2.4 %collective-permute-start.1 = (f32[5,64,128]{2,1,0:T(8,128)S(1)}, f32[5,64,128]{2,1,0:T(8,128)S(1)}, u32[]{:S(2)}, u32[]{:S(2)}) collective-permute-start(f32[5,64,128]{2,1,0:T(8,128)S(1)} %bitcast.24), channel_id=1, source_target_pairs={{0,1},{1,4},{4,5},{5,8},{8,9},{9,12},{12,13},{2,3},{3,6},{6,7},{7,... | collective-permute-start | bytes 491528 | tf_op jit(solution)/shard_map/ppermute | solution.py:473
  52.8 3.6 %second_residual.1.local = f32[5,32,8,128]{3,2,1,0:T(8,128)S(1)} custom-call(s32[4]{0:T(128)S(1)} %pad_add_fusion.info, f32[3,5,5]{2,1,0:T(8,128)S(1)} %get-tuple-element.21.mixes, f32[16,17,8,128]{3,2,1,0:T(8,128)S(1)} %all-to-all-done.lines, bf16[2,5,256,256]{3,2,1,0:T(8,128)(2,1)S(1)} %get-tuple-element.23.solve_x, ...), custom_call_target="tpu_custom_call" | custom-call | flops 300000000 | bytes 4000000 | tf_op jit(solution)/shard_map/second_residual/pallas_call | solution.py:476
  57.0 2.0 %halo_rows.1 = (f32[16,10,8,128]{3,2,1,0:T(8,128)}, f32[8,128]{1,0:T(8,128)S(1)}) custom-call(f32[3,5,5]{2,1,0:T(8,128)S(1)} %get-tuple-element.21.mixes, f32[5,32,8,128]{3,2,1,0:T(8,128)S(1)} %second_residual.1.local, f32[5,64,128]{2,1,0:T(8,128)S(1)} %collective-permute-done.1.from_prev, f32[5,64,128]{2,1,0:T(8,128)S(1)} %collective-permute-done.2.from_next, ...), custom_call_target="tpu_custom_call" | custom-call | flops 50000000 | bytes 4000000 | tf_op jit(solution)/shard_map/halo_rows/pallas_call | solution.py:485
  59.0 3.8 %all-to-all-start.1 = ((f32[16,10,8,128]{3,2,1,0:T(8,128)}), f32[16,10,8,128]{3,2,1,0:T(8,128)S(1)}, u32[]{:S(2)}, u32[]{:S(2)}) async-start(f32[16,10,8,128]{3,2,1,0:T(8,128)} %get-tuple-element.29), calls=%async_computation.1 | async-start | bytes 1310720 | tf_op jit(solution)/shard_map/all_to_all | solution.py:495
  62.8 1.0 tables_y.1.solve_y
  63.8 12.7 %all-to-all-done.1.solved = f32[16,10,8,128]{3,2,1,0:T(8,128)S(1)} async-done(((f32[16,10,8,128]{3,2,1,0:T(8,128)}), f32[16,10,8,128]{3,2,1,0:T(8,128)S(1)}, u32[]{:S(2)}, u32[]{:S(2)}) %all-to-all-start.1) | async-done | bytes 655392 | tf_op jit(solution)/shard_map/all_to_all | solution.py:495
  76.4 1.9 %update.1 = (f32[2,5,2,64,128]{4,3,2,1,0:T(8,128)}, f32[2,5,64,128]{3,2,1,0:T(8,128)S(1)}, f32[2,5,64,128]{3,2,1,0:T(8,128)S(1)}) custom-call(s32[4]{0:T(128)S(1)} %pad_add_fusion.info, f32[5,2,5]{2,1,0:T(2,128)S(1)} %bitcast.20, f32[2,5,2,64,128]{4,3,2,1,0:T(8,128)S(1)} %copy-done.1, f32[16,10,8,128]{3,2,1,0:T(8,128)S(1)} %all-to-all-done.1.solved, ...), custom_call_target="tpu_custom_call" | custom-call | flops 60000000 | bytes 4000000 | tf_op jit(solution)/shard_map/update/pallas_call | solution.py:506
  78.4 4.4 %collective-permute-start.3 = (f32[2,5,64,128]{3,2,1,0:T(8,128)S(1)}, f32[2,5,64,128]{3,2,1,0:T(8,128)S(1)}, u32[]{:S(2)}, u32[]{:S(2)}) collective-permute-start(f32[2,5,64,128]{3,2,1,0:T(8,128)S(1)} %get-tuple-element.32.outer), channel_id=1, source_target_pairs={{1,2},{3,4},{5,6},{7,8},{9,10},{11,12},{13,14},{2,1},{4,3},{6,5},{... | collective-permute-start | bytes 983048 | tf_op jit(solution)/shard_map/ppermute | solution.py:516
  82.8 1.9 %collective-permute-start.4 = (f32[2,5,64,128]{3,2,1,0:T(8,128)S(1)}, f32[2,5,64,128]{3,2,1,0:T(8,128)S(1)}, u32[]{:S(2)}, u32[]{:S(2)}) collective-permute-start(f32[2,5,64,128]{3,2,1,0:T(8,128)S(1)} %get-tuple-element.33.inner), channel_id=1, source_target_pairs={{0,1},{1,0},{2,3},{3,2},{4,5},{5,4},{6,7},{7,6},{8,9},{9,8},{10,11... | collective-permute-start | bytes 983048 | tf_op jit(solution)/shard_map/ppermute | solution.py:515
  84.8 1.1 copy-done.3
  85.9 1.0 inside_terms.1.inside
  86.9 7.5 %collective-permute-done.3.other_outer = f32[2,5,64,128]{3,2,1,0:T(8,128)S(1)} collective-permute-done((f32[2,5,64,128]{3,2,1,0:T(8,128)S(1)}, f32[2,5,64,128]{3,2,1,0:T(8,128)S(1)}, u32[]{:S(2)}, u32[]{:S(2)}) %collective-permute-start.3) | collective-permute-done | bytes 327712 | tf_op jit(solution)/shard_map/ppermute | solution.py:516
  94.4 0.7 terms.1
  95.1 29.8 %all_to_all.20.pieces = f32[32,3,4,128]{3,2,1,0:T(4,128)S(1)} all-to-all(f32[32,3,4,128]{3,2,1,0:T(4,128)S(1)} %terms.1), channel_id=1, replica_groups=mesh['cond'=32,'grid'=16] {'cond'}, dimensions={0} | all-to-all | bytes 393216 | tf_op jit(solution)/shard_map/all_to_all | solution.py:535
  124.9 15.0 %all_to_all.21 = f32[32,3,4,128]{3,2,1,0:T(4,128)S(1)} all-to-all(f32[32,3,4,128]{3,2,1,0:T(4,128)S(1)} %sum_conditions.1), channel_id=1, replica_groups=mesh['cond'=32,'grid'=16] {'cond'}, dimensions={0} | all-to-all | bytes 393216 | tf_op jit(solution)/shard_map/all_to_all | solution.py:544
  (60 shorter events, 7.2 us)
Async XLA Ops:
  0.6 4.5 %copy-start.13 = (f32[2,5,3]{1,0,2:T(2,128)S(1)}, f32[2,5,3]{1,0,2:T(2,128)}, u32[]{:S(2)}) copy-start(f32[2,5,3]{1,0,2:T(2,128)} %param.15) | copy-start | bytes 364
  0.6 6.1 %copy-start.11 = (f32[2,5,5]{2,0,1:T(2,128)S(1)}, f32[2,5,5]{2,0,1:T(2,128)}, u32[]{:S(2)}) copy-start(f32[2,5,5]{2,0,1:T(2,128)} %param.13) | copy-start | bytes 604
  0.7 6.1 %copy-start.10 = (f32[2,5,5]{2,0,1:T(2,128)S(1)}, f32[2,5,5]{2,0,1:T(2,128)}, u32[]{:S(2)}) copy-start(f32[2,5,5]{2,0,1:T(2,128)} %param.12) | copy-start | bytes 604
  0.7 6.1 %copy-start.8 = (f32[2,64,128]{2,1,0:T(8,128)S(1)}, f32[2,64,128]{2,1,0:T(8,128)}, u32[]{:S(2)}) copy-start(f32[2,64,128]{2,1,0:T(8,128)} %radius.1) | copy-start | bytes 196612
  0.8 1.1 copy-start
  1.9 4.8 %copy-start.1 = (f32[2,5,2,64,128]{4,3,2,1,0:T(8,128)S(1)}, f32[2,5,2,64,128]{4,3,2,1,0:T(8,128)}, u32[]{:S(2)}) copy-start(f32[2,5,2,64,128]{4,3,2,1,0:T(8,128)} %adjoint.5) | copy-start | bytes 1966084
  1.9 4.8 %copy-start.2 = (f32[2,5,2,64,128]{4,3,2,1,0:T(8,128)S(1)}, f32[2,5,2,64,128]{4,3,2,1,0:T(8,128)}, u32[]{:S(2)}) copy-start(f32[2,5,2,64,128]{4,3,2,1,0:T(8,128)} %source_in.1) | copy-start | bytes 1966084
  2.5 4.2 %collective-permute-start = (f32[2,5,64,128]{3,2,1,0:T(8,128)S(1)}, f32[2,5,64,128]{3,2,1,0:T(8,128)S(1)}, u32[]{:S(2)}, u32[]{:S(2)}) collective-permute-start(f32[2,5,64,128]{3,2,1,0:T(8,128)S(1)} %inner_plane.1), channel_id=1, source_target_pairs={{0,1},{1,0},{2,3},{3,2},{4,5},{5,4},{6,7},{7,6},{8,9},{9,8},{10,11... | collective-permute-start | bytes 983048 | tf_op jit(solution)/shard_map/ppermute | solution.py:405
  4.5 6.1 %copy-start.17 = (f32[1,128]{1,0:T(1,128)}, f32[1,128]{1,0:T(1,128)S(1)}, u32[]{:S(2)}) copy-start(f32[1,128]{1,0:T(1,128)S(1)} %multiply_add_fusion.2.spec_z) | copy-start | bytes 1540
  11.2 11.7 %copy-start.12 = (f32[2,5,5]{2,0,1:T(2,128)S(1)}, f32[2,5,5]{2,0,1:T(2,128)}, u32[]{:S(2)}) copy-start(f32[2,5,5]{2,0,1:T(2,128)} %param.14) | copy-start | bytes 604
  11.2 36.5 %all-to-all-start = ((f32[16,17,8,128]{3,2,1,0:T(8,128)}), f32[16,17,8,128]{3,2,1,0:T(8,128)S(1)}, u32[]{:S(2)}, u32[]{:S(2)}) async-start(f32[16,17,8,128]{3,2,1,0:T(8,128)} %bitcast.8), calls=%async_computation | async-start | bytes 2228224 | tf_op jit(solution)/shard_map/all_to_all | solution.py:441
  22.8 0.7 copy-start.16
  28.3 0.7 copy-start.4
  29.0 0.7 copy-start.6
  48.4 8.0 %collective-permute-start.2 = (f32[5,64,128]{2,1,0:T(8,128)S(1)}, f32[5,64,128]{2,1,0:T(8,128)S(1)}, u32[]{:S(2)}, u32[]{:S(2)}) collective-permute-start(f32[5,64,128]{2,1,0:T(8,128)S(1)} %bitcast.25), channel_id=1, source_target_pairs={{1,0},{4,1},{5,4},{8,5},{9,8},{12,9},{13,12},{3,2},{6,3},{7,6},{10... | collective-permute-start | bytes 491528 | tf_op jit(solution)/shard_map/ppermute | solution.py:474
  50.3 6.6 %collective-permute-start.1 = (f32[5,64,128]{2,1,0:T(8,128)S(1)}, f32[5,64,128]{2,1,0:T(8,128)S(1)}, u32[]{:S(2)}, u32[]{:S(2)}) collective-permute-start(f32[5,64,128]{2,1,0:T(8,128)S(1)} %bitcast.24), channel_id=1, source_target_pairs={{0,1},{1,4},{4,5},{5,8},{8,9},{9,12},{12,13},{2,3},{3,6},{6,7},{7,... | collective-permute-start | bytes 491528 | tf_op jit(solution)/shard_map/ppermute | solution.py:473
  52.7 4.2 %copy-start.5 = (bf16[2,5,64,64]{3,2,1,0:T(8,128)(2,1)S(1)}, bf16[2,5,64,64]{3,2,1,0:T(8,128)(2,1)}, u32[]{:S(2)}) copy-start(bf16[2,5,64,64]{3,2,1,0:T(8,128)(2,1)} %copy-done.4) | copy-start | bytes 245764
  52.7 4.2 %copy-start.7 = (bf16[2,5,64,64]{3,2,1,0:T(8,128)(2,1)S(1)}, bf16[2,5,64,64]{3,2,1,0:T(8,128)(2,1)}, u32[]{:S(2)}) copy-start(bf16[2,5,64,64]{3,2,1,0:T(8,128)(2,1)} %copy-done.6) | copy-start | bytes 245764
  59.0 17.5 %all-to-all-start.1 = ((f32[16,10,8,128]{3,2,1,0:T(8,128)}), f32[16,10,8,128]{3,2,1,0:T(8,128)S(1)}, u32[]{:S(2)}, u32[]{:S(2)}) async-start(f32[16,10,8,128]{3,2,1,0:T(8,128)} %get-tuple-element.29), calls=%async_computation.1 | async-start | bytes 1310720 | tf_op jit(solution)/shard_map/all_to_all | solution.py:495
  62.7 22.0 %copy-start.9 = (f32[2,3,5]{2,0,1:T(2,128)S(1)}, f32[2,3,5]{2,0,1:T(2,128)}, u32[]{:S(2)}) copy-start(f32[2,3,5]{2,0,1:T(2,128)} %param.16) | copy-start | bytes 364
  62.8 22.0 %copy-start.14 = (s32[2]{0:T(128)S(1)}, s32[2]{0:T(128)}, u32[]{:S(2)}) copy-start(s32[2]{0:T(128)} %weights.3) | copy-start | bytes 28
  78.4 16.0 %collective-permute-start.3 = (f32[2,5,64,128]{3,2,1,0:T(8,128)S(1)}, f32[2,5,64,128]{3,2,1,0:T(8,128)S(1)}, u32[]{:S(2)}, u32[]{:S(2)}) collective-permute-start(f32[2,5,64,128]{3,2,1,0:T(8,128)S(1)} %get-tuple-element.32.outer), channel_id=1, source_target_pairs={{1,2},{3,4},{5,6},{7,8},{9,10},{11,12},{13,14},{2,1},{4,3},{6,5},{... | collective-permute-start | bytes 983048 | tf_op jit(solution)/shard_map/ppermute | solution.py:516
  82.8 11.5 %collective-permute-start.4 = (f32[2,5,64,128]{3,2,1,0:T(8,128)S(1)}, f32[2,5,64,128]{3,2,1,0:T(8,128)S(1)}, u32[]{:S(2)}, u32[]{:S(2)}) collective-permute-start(f32[2,5,64,128]{3,2,1,0:T(8,128)S(1)} %get-tuple-element.33.inner), channel_id=1, source_target_pairs={{0,1},{1,0},{2,3},{3,2},{4,5},{5,4},{6,7},{7,6},{8,9},{9,8},{10,11... | collective-permute-start | bytes 983048 | tf_op jit(solution)/shard_map/ppermute | solution.py:515
  84.8 1.1 copy-start.3
  (2 other events, 1.3 us)
